TPU v7x, 256 devices: a whole 4x4x8 slice. The times are simulated.
256 devices in a mesh: tile: 64 (over z_lo, y, x), slab: 4 (over z_hi, core).
Axes of the slice: x: 4, y: 4, z: 8 (z_hi: 2, z_lo: 4; z = z_hi * 4 + z_lo), core: 2. Of those that a mesh axis runs over, the one named last changes fastest.
Arguments:
- old_conc: float32 [32, 512, 32, 128], P(None, 'tile', 'slab'), may hold values from -6 to 6
- upwind: bfloat16 [512, 32, 3, 128, 128], P('tile', 'slab'), may hold values from -0.09375 to 0.09375
- diag_inverse: bfloat16 [512, 32, 128, 128], P('tile', 'slab')
- neighbours: int32 [512, 32, 3], P('tile', 'slab'), may hold values from 0 to 99, as said below
- streams: float32 [64, 32, 128], P('tile'), may hold values from -6 to 6
- injector_row: int32 [64], replicated, may hold values from 0 to 63, each once
- perf_well: int32 [64, 4, 4], P('tile', 'slab'), may hold values from 0 to 63
- perf_block: int32 [64, 4, 4], P('tile', 'slab'), may hold values from 0 to 63
- perf_rate: float32 [64, 4, 4], P('tile', 'slab'), may hold values from 0.5 to 2
Outputs:
- new_conc: float32 [32, 512, 32, 128], P(None, 'tile', 'slab')
Inputs may be any that keep to these rules, and one draw needn't show every extreme that they name: `neighbours`: indices into a grid of (10) x (10) blocks, row-major, each within one block of its own block in both directions, never the block itself. `injector_row`: each row of streams is named by exactly one well.
All inputs are finite; a program needn't handle non-finite values.
Results may differ from a plain program's by a relative error of at most 0.0045.
Values may be sent and summed in bfloat16 or wider, within the bound.
No kernel may reach another device: no remote copies, remote signals or barrier semaphores. Data moves between devices by JAX's collectives and lax.ppermute only.
A program may use at most 64 MiB of HBM per device.

v0:
```python
import jax
import jax.numpy as jnp
from jax import lax
from jax.sharding import PartitionSpec as P

SWEEPS = 3


def padded_2(cells, sides, width):
    for axis, dim in sides:
        count = lax.axis_size(axis)
        ends = count - 1
        head = lax.slice_in_dim(cells, 0, width, axis=dim)
        tail = lax.slice_in_dim(cells, cells.shape[dim] - width, cells.shape[dim], axis=dim)
        cells = jnp.concatenate(
            [
                lax.ppermute(tail, axis, [(i, (i + 1) % count) for i in range(ends)]),
                cells,
                lax.ppermute(head, axis, [((i + 1) % count, i) for i in range(ends)]),
            ],
            axis=dim,
        )
    return cells


def body(
    old_conc,
    upwind,
    diag_inverse,
    neighbours,
    streams,
    injector_row,
    perf_well,
    perf_block,
    perf_rate,
):
    tracers, tile_blocks, slab_blocks, cell_count = old_conc.shape
    slot_count = neighbours.shape[2]
    stream_slots = injector_row[perf_well.reshape(-1)]
    weights = perf_rate.reshape(-1)
    allrows = lax.all_gather(streams, "tile", axis=0, tiled=True)
    picked = jnp.take(allrows, stream_slots, axis=0)
    block_total = tile_blocks * slab_blocks
    placing = (
        perf_block.reshape(-1)[:, None] == jnp.arange(block_total, dtype=jnp.int32)[None, :]
    ).astype(jnp.float32) * weights[:, None]
    sources = jnp.einsum("pb,ptc->tbc", placing, picked, precision=lax.Precision.HIGHEST)
    rhs = old_conc + sources.reshape(tracers, tile_blocks, slab_blocks, cell_count)
    neighbour_flat = neighbours.reshape(-1)
    concentration = old_conc
    for sweep_index in range(SWEEPS):
        rounded = concentration.astype(jnp.bfloat16)
        padded = padded_2(rounded, (("tile", 1), ("slab", 2)), 1)
        flat_grid = padded.reshape(tracers, -1, cell_count)
        upstream = jnp.take(flat_grid, neighbour_flat, axis=1).reshape(
            tracers, tile_blocks, slab_blocks, slot_count, cell_count
        )
        coupled = jnp.einsum(
            "tabkj,abkij->tabi", upstream, upwind, preferred_element_type=jnp.float32
        )
        remainder = (rhs - coupled).astype(jnp.bfloat16)
        concentration = jnp.einsum(
            "tabj,abij->tabi", remainder, diag_inverse, preferred_element_type=jnp.float32
        )
    return concentration


def solution(mesh):
    in_specs = (
        P(None, "tile", "slab", None),
        P("tile", "slab", None, None, None),
        P("tile", "slab", None, None),
        P("tile", "slab", None),
        P("tile", None, None),
        P(),
        P("tile", "slab", None),
        P("tile", "slab", None),
        P("tile", "slab", None),
    )
    out_specs = P(None, "tile", "slab", None)
    return jax.shard_map(body, mesh=mesh, in_specs=in_specs, out_specs=out_specs, check_vma=False)
```

profile of v0, /device:TPU:1, one launch (start us, length us, event | category | flops | bytes accessed | tf_op | source)
XLA Modules:
  0.0 460.4 jit_solution(4040292959848366074)
XLA Ops:
  6.5 0.0 copy-start
  6.5 0.0 copy-start.3
  6.5 0.0 copy-start.6
  6.5 0.0 copy-start.1
  6.5 0.0 all-gather.2.cloned.1.call-start
  6.6 0.7 all-gather.2.cloned.1.call-update
  7.3 1.8 copy.54
  9.1 3.9 collective-permute-start
  13.1 1.3 collective-permute-start.1
  14.4 0.0 copy-done.3
  14.4 0.1 copy.25
  14.5 0.1 reshape.83
  14.7 0.0 copy-done.6
  14.7 0.0 copy-done.1
  14.7 0.6 gather_fusion
  15.4 0.0 collective-permute-done
  15.4 2.7 collective-permute-done.1
  18.1 0.0 copy-start.2
  18.1 10.8 %collective-permute-start.2 = (bf16[32,10,1,128]{3,0,2,1:T(8,128)(2,1)S(1)}, bf16[32,10,1,128]{3,0,2,1:T(8,128)(2,1)S(1)}, u32[]{:S(2)}, u32[]{:S(2)}) collective-permute-start(bf16[32,10,1,128]{3,0,2,1:T(8,128)(2,1)S(1)} %get-tuple-element.10), channel_id=1, source_target_pairs={{0,1},{1,2},{2,3},{4,5},{5,6},{6,7},{8,9},{9,10},{10,11},{12,13},{... | collective-permute-start | bytes 245768 | tf_op jit(solution)/shard_map/ppermute | solution.py:17
  28.9 1.9 collective-permute-start.3
  30.9 0.0 collective-permute-done.2
  30.9 0.0 copy-done.2
  30.9 7.8 %collective-permute-done.3 = bf16[32,10,1,128]{3,0,2,1:T(8,128)(2,1)S(1)} collective-permute-done((bf16[32,10,1,128]{3,0,2,1:T(8,128)(2,1)S(1)}, bf16[32,10,1,128]{3,0,2,1:T(8,128)(2,1)S(1)}, u32[]{:S(2)}, u32[]{:S(2)}) %collective-permute-start.3) | collective-permute-done | bytes 81952 | tf_op jit(solution)/shard_map/ppermute | solution.py:19
  38.7 1.0 pad_maximum_fusion
  39.7 2.0 gather_fusion.2
  41.7 0.0 copy-start.4
  41.7 2.9 broadcast_select_fusion
  44.6 270.3 %all-gather.2.cloned.1.call-done = f32[64,32,128]{2,1,0:T(8,128)} async-done(((f32[1,32,128]{2,1,0:T(8,128)}), f32[64,32,128]{2,1,0:T(8,128)}) %all-gather.2.cloned.1.call-update) | async-done | bytes 1048592 | tf_op jit(solution)/shard_map/all_gather | solution.py:41
  314.9 1.8 gather_fusion.1
  316.7 0.1 broadcast_select_fusion.3
  316.8 0.0 copy-done.4
  316.8 0.0 copy-done.5
  316.8 1.1 convolution_bitcast_fusion.4
  317.9 0.0 copy-done
  317.9 7.8 %fusion.6 = bf16[32,8,8,128]{3,0,2,1:T(8,128)(2,1)} fusion(bf16[8,8,128,128]{3,2,1,0:T(8,128)(2,1)S(1)} %copy-done, bf16[32,8,8,3,128]{4,0,3,2,1:T(8,128)(2,1)} %bitcast.80, bf16[8,8,3,128,128]{4,3,2,1,0:T(8,128)(2,1)} %param.12, f32[32,8,8,128]{3,2,1,0:T(8,128)S(1)} %convolution_bitcast_fusion.4, f32[32,8,8,128]{3,2,1,0:T(8,128)} %param.11), kind=kOutput, calls=%fused_computation.21 | convolution fusion | flops 269484032 | bytes 12582912 | tf_op jit(solution)/shard_map/tabj,abij->tabi/dot_general | solution.py:62
  325.7 0.9 fusion.18
  326.6 2.5 collective-permute-start.4
  329.0 1.3 collective-permute-start.5
  330.3 0.0 collective-permute-done.4
  330.4 3.7 collective-permute-done.5
  334.1 0.9 pad_maximum_fusion.8
  335.0 51.3 %collective-permute-start.6 = (bf16[32,10,1,128]{3,0,2,1:T(8,128)(2,1)S(1)}, bf16[32,10,1,128]{3,0,2,1:T(8,128)(2,1)S(1)}, u32[]{:S(2)}, u32[]{:S(2)}) collective-permute-start(bf16[32,10,1,128]{3,0,2,1:T(8,128)(2,1)S(1)} %get-tuple-element.8), channel_id=1, source_target_pairs={{0,1},{1,2},{2,3},{4,5},{5,6},{6,7},{8,9},{9,10},{10,11},{12,13},{... | collective-permute-start | bytes 245768 | tf_op jit(solution)/shard_map/ppermute | solution.py:17
  386.3 1.9 collective-permute-start.7
  388.2 0.0 collective-permute-done.6
  388.2 7.7 %collective-permute-done.7 = bf16[32,10,1,128]{3,0,2,1:T(8,128)(2,1)S(1)} collective-permute-done((bf16[32,10,1,128]{3,0,2,1:T(8,128)(2,1)S(1)}, bf16[32,10,1,128]{3,0,2,1:T(8,128)(2,1)S(1)}, u32[]{:S(2)}, u32[]{:S(2)}) %collective-permute-start.7) | collective-permute-done | bytes 81952 | tf_op jit(solution)/shard_map/ppermute | solution.py:19
  396.0 2.1 pad_maximum_fusion.1
  398.0 3.2 gather_fusion.3
  401.2 2.9 broadcast_select_fusion.1
  404.1 7.8 %fusion.7 = bf16[32,8,8,128]{3,0,2,1:T(8,128)(2,1)} fusion(bf16[8,8,128,128]{3,2,1,0:T(8,128)(2,1)S(1)} %copy-done, bf16[32,8,8,3,128]{4,0,3,2,1:T(8,128)(2,1)} %bitcast.82, bf16[8,8,3,128,128]{4,3,2,1,0:T(8,128)(2,1)} %param.12, f32[32,8,8,128]{3,2,1,0:T(8,128)S(1)} %convolution_bitcast_fusion.4, f32[32,8,8,128]{3,2,1,0:T(8,128)} %param.11), kind=kOutput, calls=%fused_computation.22 | convolution fusion | flops 269484032 | bytes 12582912 | tf_op jit(solution)/shard_map/tabj,abij->tabi/dot_general | solution.py:62
  411.9 0.9 fusion.17
  412.8 3.0 collective-permute-start.8
  415.7 1.3 collective-permute-start.9
  417.0 0.0 collective-permute-done.8
  417.0 3.7 collective-permute-done.9
  420.7 0.9 pad_maximum_fusion.5
  421.6 3.3 collective-permute-start.10
  424.9 2.1 collective-permute-start.11
  427.0 0.0 collective-permute-done.10
  427.1 7.5 %collective-permute-done.11 = bf16[32,10,1,128]{3,0,2,1:T(8,128)(2,1)S(1)} collective-permute-done((bf16[32,10,1,128]{3,0,2,1:T(8,128)(2,1)S(1)}, bf16[32,10,1,128]{3,0,2,1:T(8,128)(2,1)S(1)}, u32[]{:S(2)}, u32[]{:S(2)}) %collective-permute-start.11) | collective-permute-done | bytes 81952 | tf_op jit(solution)/shard_map/ppermute | solution.py:19
  434.6 2.1 pad_maximum_fusion.2
  436.7 3.2 gather_fusion.4
  439.8 2.9 broadcast_select_fusion.2
  442.7 8.0 %convolution_bitcast_fusion = f32[32,8,8,128]{3,0,2,1:T(8,128)} fusion(bf16[8,8,128,128]{3,2,1,0:T(8,128)(2,1)S(1)} %copy-done, bf16[32,8,8,3,128]{4,0,3,2,1:T(8,128)(2,1)} %bitcast.81, bf16[8,8,3,128,128]{4,3,2,1,0:T(8,128)(2,1)} %param.12, f32[32,8,8,128]{3,2,1,0:T(8,128)S(1)} %convolution_bitcast_fusion.4, f32[32,8,8,128]{3,2,1,0:T(8,128)} %param.11), kind=kOutput, calls=%fused_computation.8 | convolution fusion | flops 269221888 | bytes 13107200 | tf_op jit(solution)/shard_map/tabj,abij->tabi/dot_general | solution.py:62
  450.7 2.8 copy.27
  (11 shorter events, 0.1 us)
Async XLA Ops:
  6.5 311.3 %copy-start = (bf16[8,8,128,128]{3,2,1,0:T(8,128)(2,1)S(1)}, bf16[8,8,128,128]{3,2,1,0:T(8,128)(2,1)}, u32[]{:S(2)}) copy-start(bf16[8,8,128,128]{3,2,1,0:T(8,128)(2,1)} %param.13) | copy-start | bytes 6291460
  6.5 7.9 %copy-start.3 = (s32[8,8,3]{1,0,2:T(8,128)S(1)}, s32[8,8,3]{1,0,2:T(8,128)}, u32[]{:S(2)}) copy-start(s32[8,8,3]{1,0,2:T(8,128)} %param.14) | copy-start | bytes 2308
  6.5 8.1 %copy-start.6 = (s32[1,1,4]{2,1,0:T(1,128)S(1)}, s32[1,1,4]{2,1,0:T(1,128)}, u32[]{:S(2)}) copy-start(s32[1,1,4]{2,1,0:T(1,128)} %param.17) | copy-start | bytes 52
  6.5 8.2 %copy-start.1 = (s32[64]{0:T(128)S(1)}, s32[64]{0:T(128)}, u32[]{:S(2)}) copy-start(s32[64]{0:T(128)} %param.16) | copy-start | bytes 772
  6.5 308.4 %all-gather.2.cloned.1.call-start = ((), (), s32[]{:S(2)}) async-start(), calls=%async_computation | async-start | bytes 1064960 | tf_op jit(solution)/shard_map/all_gather | solution.py:41
  9.1 6.3 %collective-permute-start = (bf16[32,1,8,128]{3,0,2,1:T(8,128)(2,1)S(1)}, bf16[32,1,8,128]{3,0,2,1:T(8,128)(2,1)S(1)}, u32[]{:S(2)}, u32[]{:S(2)}) collective-permute-start(bf16[32,1,8,128]{3,0,2,1:T(8,128)(2,1)S(1)} %get-tuple-element.16), channel_id=1, source_target_pairs={{0,4},{4,8},{8,12},{12,16},{16,20},{20,24},{24,28},{28,32},{32,36}... | collective-permute-start | bytes 196616 | tf_op jit(solution)/shard_map/ppermute | solution.py:17
  13.1 5.0 %collective-permute-start.1 = (bf16[32,1,8,128]{3,0,2,1:T(8,128)(2,1)S(1)}, bf16[32,1,8,128]{3,0,2,1:T(8,128)(2,1)S(1)}, u32[]{:S(2)}, u32[]{:S(2)}) collective-permute-start(bf16[32,1,8,128]{3,0,2,1:T(8,128)(2,1)S(1)} %get-tuple-element.17), channel_id=1, source_target_pairs={{4,0},{8,4},{12,8},{16,12},{20,16},{24,20},{28,24},{32,28},{36,32}... | collective-permute-start | bytes 196616 | tf_op jit(solution)/shard_map/ppermute | solution.py:19
  18.1 12.8 %copy-start.2 = (bf16[32,1,8,128]{3,0,2,1:T(8,128)(2,1)}, bf16[32,1,8,128]{3,0,2,1:T(8,128)(2,1)S(1)}, u32[]{:S(2)}) copy-start(bf16[32,1,8,128]{3,0,2,1:T(8,128)(2,1)S(1)} %collective-permute-done.1) | copy-start | bytes 196612
  18.1 12.8 %collective-permute-start.2 = (bf16[32,10,1,128]{3,0,2,1:T(8,128)(2,1)S(1)}, bf16[32,10,1,128]{3,0,2,1:T(8,128)(2,1)S(1)}, u32[]{:S(2)}, u32[]{:S(2)}) collective-permute-start(bf16[32,10,1,128]{3,0,2,1:T(8,128)(2,1)S(1)} %get-tuple-element.10), channel_id=1, source_target_pairs={{0,1},{1,2},{2,3},{4,5},{5,6},{6,7},{8,9},{9,10},{10,11},{12,13},{... | collective-permute-start | bytes 245768 | tf_op jit(solution)/shard_map/ppermute | solution.py:17
  28.9 9.7 %collective-permute-start.3 = (bf16[32,10,1,128]{3,0,2,1:T(8,128)(2,1)S(1)}, bf16[32,10,1,128]{3,0,2,1:T(8,128)(2,1)S(1)}, u32[]{:S(2)}, u32[]{:S(2)}) collective-permute-start(bf16[32,10,1,128]{3,0,2,1:T(8,128)(2,1)S(1)} %get-tuple-element.11), channel_id=1, source_target_pairs={{1,0},{2,1},{3,2},{5,4},{6,5},{7,6},{9,8},{10,9},{11,10},{13,12},{... | collective-permute-start | bytes 245768 | tf_op jit(solution)/shard_map/ppermute | solution.py:19
  41.7 275.1 %copy-start.4 = (f32[1,1,4]{2,1,0:T(1,128)S(1)}, f32[1,1,4]{2,1,0:T(1,128)}, u32[]{:S(2)}) copy-start(f32[1,1,4]{2,1,0:T(1,128)} %param.19) | copy-start | bytes 52
  41.7 275.1 %copy-start.5 = (s32[1,1,4]{2,1,0:T(1,128)S(1)}, s32[1,1,4]{2,1,0:T(1,128)}, u32[]{:S(2)}) copy-start(s32[1,1,4]{2,1,0:T(1,128)} %param.18) | copy-start | bytes 52
  326.6 3.8 collective-permute-start.4
  329.0 5.0 %collective-permute-start.5 = (bf16[32,1,8,128]{3,0,2,1:T(8,128)(2,1)S(1)}, bf16[32,1,8,128]{3,0,2,1:T(8,128)(2,1)S(1)}, u32[]{:S(2)}, u32[]{:S(2)}) collective-permute-start(bf16[32,1,8,128]{3,0,2,1:T(8,128)(2,1)S(1)} %get-tuple-element.15), channel_id=1, source_target_pairs={{4,0},{8,4},{12,8},{16,12},{20,16},{24,20},{28,24},{32,28},{36,32}... | collective-permute-start | bytes 196616 | tf_op jit(solution)/shard_map/ppermute | solution.py:19
  335.0 53.3 %collective-permute-start.6 = (bf16[32,10,1,128]{3,0,2,1:T(8,128)(2,1)S(1)}, bf16[32,10,1,128]{3,0,2,1:T(8,128)(2,1)S(1)}, u32[]{:S(2)}, u32[]{:S(2)}) collective-permute-start(bf16[32,10,1,128]{3,0,2,1:T(8,128)(2,1)S(1)} %get-tuple-element.8), channel_id=1, source_target_pairs={{0,1},{1,2},{2,3},{4,5},{5,6},{6,7},{8,9},{9,10},{10,11},{12,13},{... | collective-permute-start | bytes 245768 | tf_op jit(solution)/shard_map/ppermute | solution.py:17
  386.3 9.7 %collective-permute-start.7 = (bf16[32,10,1,128]{3,0,2,1:T(8,128)(2,1)S(1)}, bf16[32,10,1,128]{3,0,2,1:T(8,128)(2,1)S(1)}, u32[]{:S(2)}, u32[]{:S(2)}) collective-permute-start(bf16[32,10,1,128]{3,0,2,1:T(8,128)(2,1)S(1)} %get-tuple-element.9), channel_id=1, source_target_pairs={{1,0},{2,1},{3,2},{5,4},{6,5},{7,6},{9,8},{10,9},{11,10},{13,12},{... | collective-permute-start | bytes 245768 | tf_op jit(solution)/shard_map/ppermute | solution.py:19
  412.8 4.3 collective-permute-start.8
  415.7 5.0 %collective-permute-start.9 = (bf16[32,1,8,128]{3,0,2,1:T(8,128)(2,1)S(1)}, bf16[32,1,8,128]{3,0,2,1:T(8,128)(2,1)S(1)}, u32[]{:S(2)}, u32[]{:S(2)}) collective-permute-start(bf16[32,1,8,128]{3,0,2,1:T(8,128)(2,1)S(1)} %get-tuple-element.13), channel_id=1, source_target_pairs={{4,0},{8,4},{12,8},{16,12},{20,16},{24,20},{28,24},{32,28},{36,32}... | collective-permute-start | bytes 196616 | tf_op jit(solution)/shard_map/ppermute | solution.py:19
  421.6 5.4 %collective-permute-start.10 = (bf16[32,10,1,128]{3,0,2,1:T(8,128)(2,1)S(1)}, bf16[32,10,1,128]{3,0,2,1:T(8,128)(2,1)S(1)}, u32[]{:S(2)}, u32[]{:S(2)}) collective-permute-start(bf16[32,10,1,128]{3,0,2,1:T(8,128)(2,1)S(1)} %get-tuple-element.6), channel_id=1, source_target_pairs={{0,1},{1,2},{2,3},{4,5},{5,6},{6,7},{8,9},{9,10},{10,11},{12,13},{... | collective-permute-start | bytes 245768 | tf_op jit(solution)/shard_map/ppermute | solution.py:17
  424.9 9.7 %collective-permute-start.11 = (bf16[32,10,1,128]{3,0,2,1:T(8,128)(2,1)S(1)}, bf16[32,10,1,128]{3,0,2,1:T(8,128)(2,1)S(1)}, u32[]{:S(2)}, u32[]{:S(2)}) collective-permute-start(bf16[32,10,1,128]{3,0,2,1:T(8,128)(2,1)S(1)} %get-tuple-element.7), channel_id=1, source_target_pairs={{1,0},{2,1},{3,2},{5,4},{6,5},{7,6},{9,8},{10,9},{11,10},{13,12},{... | collective-permute-start | bytes 245768 | tf_op jit(solution)/shard_map/ppermute | solution.py:19
Sparse Core Ops, SparseCore 0:
  9.2 305.7 all-gather.1
where the time goes:
time: 461 us; the launch traced here: 460 us
  waiting for transfers between devices  304 us (66%)
  starting transfers between devices  84.7 us (18%)
  matrix products  24.7 us (5%)
  local copies, waits for them, and re-layouts  17.5 us (4%)
  other arithmetic  15.7 us (3%)
  between operations  13.7 us (3%)
    all_gather x1, waiting for transfers between devices, body(): allrows = lax.all_gather(streams, 'tile', axis=0, tiled=True)  270 us
    ppermute x6, starting transfers between devices, padded_2(): lax.ppermute(tail, axis, [(i, (i + 1) % count) for i in range(ends)])  74.8 us
    ppermute x6, waiting for transfers between devices, padded_2(): lax.ppermute(head, axis, [((i + 1) % count, i) for i in range(ends)])  33.1 us
    dot_general x3, matrix products, body(): jnp.einsum('tabj,abij->tabi', remainder, diag_inverse, preferred_element_...  23.6 us
    ppermute x6, starting transfers between devices, padded_2(): lax.ppermute(head, axis, [((i + 1) % count, i) for i in range(ends)])  9.82 us
  transfers between devices with their start and end apart: 13, of which 7 were waited for; matrix products, arithmetic and copies ran while one was open for 2% of the time, Pallas kernels for 0%

commit v1 on v0

v1 whole, which is shorter than its diff:
```python
import functools

import jax
import jax.numpy as jnp
from jax import lax
from jax.experimental import pallas as pl
from jax.experimental.pallas import tpu as pltpu
from jax.sharding import PartitionSpec as P

BF16 = jnp.bfloat16
F32 = jnp.float32
BATCH = 16
WIDE = 10

dot_t = functools.partial(
    lax.dot_general,
    dimension_numbers=(((1,), (1,)), ((), ())),
    preferred_element_type=F32,
)


def place():
    slab = lax.axis_index("slab")
    return lax.axis_index("tile"), slab, lax.rem(slab, 2)


def edge_columns(parity):
    return 7 * (1 - parity), 7 * parity


def far_is_real(slab):
    return jnp.logical_or(slab == 1, slab == 2)


def only_if(real, value):
    return jnp.where(real, value, jnp.zeros_like(value))


def prepare(old, x, base, to_near, to_far):
    _, _, parity = place()
    near, far = edge_columns(parity)
    for b in range(64):
        block = old[pl.ds(b, 32, stride=64), :]
        base[b] = block
        x[b] = block.astype(BF16)
    for r in range(8):
        to_near[r] = x[r * 8 + near]
        to_far[r] = x[r * 8 + far]


def rows_to_send(x, from_near, from_far, to_below, to_above):
    _, slab, parity = place()
    near, far = 9 * (1 - parity), 9 * parity
    real = far_is_real(slab)
    for out, r in ((to_below, 7), (to_above, 0)):
        out[pl.ds(1, 8)] = x[pl.ds(8 * r, 8)]
        out[near] = from_near[r]
        out[far] = only_if(real, from_far[r])


def widen(grid, x, from_near, from_far, from_above, from_below):
    tile, slab, parity = place()
    near, far = 9 * (1 - parity), 9 * parity
    real = far_is_real(slab)
    grid[pl.ds(0, WIDE)] = only_if(tile > 0, from_above[...])
    grid[pl.ds(90, WIDE)] = only_if(tile < lax.axis_size("tile") - 1, from_below[...])
    for r in range(8):
        grid[pl.ds((r + 1) * WIDE + 1, 8)] = x[pl.ds(8 * r, 8)]
        grid[(r + 1) * WIDE + near] = from_near[r]
        grid[(r + 1) * WIDE + far] = only_if(real, from_far[r])


def sweep(neighbour, grid, rhs, upwind, diag, store):
    @pl.loop(0, 64 // BATCH)
    def _(step):
        first = step * BATCH
        remainders = []
        for q in range(BATCH):
            b = first + q
            upstream = jnp.concatenate([grid[neighbour[3 * b + k]] for k in range(3)], axis=1)
            weights = jnp.concatenate([upwind[b, k] for k in range(3)], axis=1)
            remainders.append((rhs[b] - dot_t(upstream, weights)).astype(BF16))
        for q in range(0, BATCH, 2):
            b = first + q
            both = jnp.concatenate(remainders[q : q + 2], axis=0)
            conc = dot_t(both, diag[pl.ds(b, 2)].reshape(256, 128))
            store(b, conc[:32, :128])
            store(b + 1, conc[32:, 128:])


def send_edges(x, to_near, to_far):
    _, _, parity = place()
    near, far = edge_columns(parity)
    for r in range(8):
        to_near[r] = x[r * 8 + near]
        to_far[r] = x[r * 8 + far]


def first_sweep(
    neighbour, slot_row, slot_block, slot_rate,
    x, from_near, from_far, from_above, from_below, base, rows, upwind, diag,
    x_next, to_near, to_far, rhs, grid,
):
    widen(grid, x, from_near, from_far, from_above, from_below)
    rhs[...] = base[...]
    for p in range(4):
        b = slot_block[p]
        rhs[b] = rhs[b] + slot_rate[p] * rows[slot_row[p]].astype(F32)

    def store(b, conc):
        x_next[b] = conc.astype(BF16)

    sweep(neighbour, grid, rhs, upwind, diag, store)
    send_edges(x_next, to_near, to_far)


def middle_sweep(
    neighbour, x, from_near, from_far, from_above, from_below, rhs, upwind, diag,
    x_next, to_near, to_far, grid,
):
    widen(grid, x, from_near, from_far, from_above, from_below)

    def store(b, conc):
        x_next[b] = conc.astype(BF16)

    sweep(neighbour, grid, rhs, upwind, diag, store)
    send_edges(x_next, to_near, to_far)


def last_sweep(
    neighbour, x, from_near, from_far, from_above, from_below, rhs, upwind, diag,
    out, grid,
):
    widen(grid, x, from_near, from_far, from_above, from_below)

    def store(b, conc):
        out[pl.ds(b, 32, stride=64), :] = conc

    sweep(neighbour, grid, rhs, upwind, diag, store)


def call(kernel, outs, scalars, arrays, scratch=(), flops=0):
    vmem = pl.BlockSpec(memory_space=pltpu.VMEM)
    smem = pl.BlockSpec(memory_space=pltpu.SMEM)
    return pl.pallas_call(
        kernel,
        out_shape=outs,
        in_specs=[smem] * len(scalars) + [vmem] * len(arrays),
        out_specs=[vmem] * len(outs),
        scratch_shapes=list(scratch),
        compiler_params=pltpu.CompilerParams(vmem_limit_bytes=32 * 2**20),
    )(*scalars, *arrays)


def blocks(count, dtype=BF16):
    return jax.ShapeDtypeStruct((count, 32, 128), dtype)


def body(
    old_conc, upwind, diag_inverse, neighbours, streams, injector_row, perf_well, perf_block, perf_rate
):
    tiles, slabs = lax.axis_size("tile"), lax.axis_size("slab")
    on_chip = [(s, s ^ 1) for s in range(slabs)]
    far_pairs = []
    for t in range(tiles):
        for s in range(slabs):
            to = (t, 3 - s) if s in (1, 2) else (t ^ 1, s)
            far_pairs.append((t * slabs + s, to[0] * slabs + to[1]))
    down = [(t, (t + 1) % tiles) for t in range(tiles)]
    up = [((t + 1) % tiles, t) for t in range(tiles)]

    def exchange(x, to_near, to_far):
        from_far = lax.ppermute(to_far, ("tile", "slab"), far_pairs)
        from_near = lax.ppermute(to_near, "slab", on_chip)
        to_below, to_above = call(rows_to_send, [blocks(10)] * 2, [], [x, from_near, from_far])
        from_above = lax.ppermute(to_below, "tile", down)
        from_below = lax.ppermute(to_above, "tile", up)
        return x, from_near, from_far, from_above, from_below

    old = old_conc.reshape(32 * 64, 128)
    upwind = pltpu.with_memory_space_constraint(upwind.reshape(64, 3, 128, 128), pltpu.VMEM)
    diag = pltpu.with_memory_space_constraint(diag_inverse.reshape(64, 128, 128), pltpu.VMEM)
    neighbour = neighbours.reshape(-1)
    slot_row = injector_row[perf_well.reshape(-1)]
    grid = pltpu.VMEM((100, 32, 128), BF16)

    x, base, to_near, to_far = call(prepare, [blocks(64), blocks(64, F32), blocks(8), blocks(8)], [], [old])
    everyone = jnp.broadcast_to(streams.astype(BF16), (tiles, 32, 128))
    rows = lax.all_to_all(everyone, "tile", 0, 0)
    x, to_near, to_far, rhs = call(
        first_sweep,
        [blocks(64), blocks(8), blocks(8), blocks(64, F32)],
        [neighbour, slot_row, perf_block.reshape(-1), perf_rate.reshape(-1)],
        [*exchange(x, to_near, to_far), base, rows, upwind, diag],
        [grid],
    )
    x, to_near, to_far = call(
        middle_sweep,
        [blocks(64), blocks(8), blocks(8)],
        [neighbour],
        [*exchange(x, to_near, to_far), rhs, upwind, diag],
        [grid],
    )
    (out,) = call(
        last_sweep,
        [jax.ShapeDtypeStruct((2048, 128), F32)],
        [neighbour],
        [*exchange(x, to_near, to_far), rhs, upwind, diag],
        [grid],
    )
    return out.reshape(old_conc.shape)


def solution(mesh):
    in_specs = (
        P(None, "tile", "slab", None),
        P("tile", "slab", None, None, None),
        P("tile", "slab", None, None),
        P("tile", "slab", None),
        P("tile", None, None),
        P(),
        P("tile", "slab", None),
        P("tile", "slab", None),
        P("tile", "slab", None),
    )
    out_specs = P(None, "tile", "slab", None)
    return jax.shard_map(body, mesh=mesh, in_specs=in_specs, out_specs=out_specs, check_vma=False)
```

time: 461 us -> 99.2 us (0.22)
  waiting for transfers between devices: 304 us -> 21.1 us
  starting transfers between devices: 84.7 us -> 46.9 us
  matrix products: 24.7 us -> 0 us
  Pallas kernels: 0 us -> 14.8 us
  other arithmetic: 15.7 us -> 1.4 us
  between operations: 13.7 us -> 0.12 us
    all_gather x1 -> x0, waiting for transfers between devices: 270 us -> none  [body(): allrows = lax.all_gather(streams, 'tile', axis=0, tiled=True)]
    ppermute x12, starting transfers between devices: 84.6 us -> 34.4 us  [the longest x3 23.4 us: exchange(): from_below = lax.ppermute(to_above, 'tile', up)]
    dot_general x4 -> x0, matrix products: 24.7 us -> none  [the longest x3 23.6 us: body(): jnp.einsum('tabj,abij->tabi', remainder, diag_inverse, preferred_element_...]
    pallas_call x0 -> x7, Pallas kernels: none -> 14.8 us  [call(): pl.pallas_call(kernel, out_shape=outs, in_specs=[smem] * len(scalars) + [...]
    all_to_all x0 -> x1, starting transfers between devices: none -> 12.6 us  [body(): rows = lax.all_to_all(everyone, 'tile', 0, 0)]
    ppermute x12, waiting for transfers between devices: 33.2 us -> 21.1 us  [the longest x3 16.2 us: exchange(): from_far = lax.ppermute(to_far, ('tile', 'slab'), far_pairs)]
    unnamed x16 -> x23, local copies, waits for them, and re-layouts: 1.99 us -> 12.7 us
    gather x5 -> x1, local copies, waits for them, and re-layouts: 10.8 us -> 0.64 us  [body(): slot_row = injector_row[perf_well.reshape(-1)]]
  transfers between devices with their start and end apart: 13 -> 13, of which waited for: 7 -> 6; matrix products, arithmetic and copies ran while one was open for 2% -> 2% of each run, Pallas kernels for 0% -> 1%
where the time goes in v1:
time: 99.2 us; the launch traced here: 98.7 us
  starting transfers between devices  46.9 us (47%)
  waiting for transfers between devices  21.1 us (21%)
  Pallas kernels  14.8 us (15%)
  local copies, waits for them, and re-layouts  14.4 us (15%)
  other arithmetic  1.4 us (1%)
    ppermute x3, starting transfers between devices, exchange(): from_below = lax.ppermute(to_above, 'tile', up)  23.4 us
    ppermute x3, waiting for transfers between devices, exchange(): from_far = lax.ppermute(to_far, ('tile', 'slab'), far_pairs)  16.2 us
    pallas_call x7, Pallas kernels, call(): pl.pallas_call(kernel, out_shape=outs, in_specs=[smem] * len(scalars) + [...  14.8 us
    unnamed x23, local copies, waits for them, and re-layouts  12.7 us
    all_to_all x1, starting transfers between devices, body(): rows = lax.all_to_all(everyone, 'tile', 0, 0)  12.6 us
    ppermute x3, starting transfers between devices, exchange(): from_far = lax.ppermute(to_far, ('tile', 'slab'), far_pairs)  8.49 us
    ppermute x3, waiting for transfers between devices, exchange(): from_above = lax.ppermute(to_below, 'tile', down)  4.87 us
  transfers between devices with their start and end apart: 13, of which 6 were waited for; matrix products, arithmetic and copies ran while one was open for 2% of the time, Pallas kernels for 1%

profile of v1, /device:TPU:1, one launch (start us, length us, event | category | flops | bytes accessed | tf_op | source)
XLA Modules:
  0.0 98.7 jit_solution(9401968928142619813)
XLA Ops:
  0.0 0.0 copy-start
  0.0 0.7 convert_bitcast_fusion
  0.7 0.9 broadcast_in_dim.9
  1.6 12.6 %all-to-all-start = ((bf16[64,32,128]{2,1,0:T(8,128)(2,1)}), bf16[64,32,128]{2,1,0:T(8,128)(2,1)S(1)}, u32[]{:S(2)}, u32[]{:S(2)}) async-start(bf16[64,32,128]{2,1,0:T(8,128)(2,1)} %broadcast_in_dim.9), calls=%async_computation | async-start | bytes 1048576 | tf_op jit(solution)/shard_map/all_to_all | solution.py:189
  14.2 0.0 copy-start.8
  14.2 1.2 %copy-done.8 = f32[32,8,8,128]{3,2,1,0:T(8,128)S(1)} copy-done((f32[32,8,8,128]{3,2,1,0:T(8,128)S(1)}, f32[32,8,8,128]{3,2,1,0:T(8,128)}, u32[]{:S(2)}) %copy-start.8) | copy-done | bytes 1048600
  15.4 0.0 copy-start.5
  15.4 0.7 shard_map.91
  16.1 0.0 copy-start.6
  16.1 1.0 copy-done.6
  17.1 1.0 collective-permute-start
  18.0 4.1 %collective-permute-start.1 = (bf16[8,32,128]{2,1,0:T(8,128)(2,1)S(1)}, bf16[8,32,128]{2,1,0:T(8,128)(2,1)S(1)}, u32[]{:S(2)}, u32[]{:S(2)}) collective-permute-start(bf16[8,32,128]{2,1,0:T(8,128)(2,1)S(1)} %get-tuple-element.24), channel_id=1, source_target_pairs={{0,4},{1,2},{2,1},{3,7},{4,0},{5,6},{6,5},{7,3},{8,12},{9,10},{10,... | collective-permute-start | bytes 196616 | tf_op jit(solution)/shard_map/ppermute | solution.py:173
  22.1 0.7 fusion
  22.8 0.8 copy.10
  23.6 0.1 reshape.52.neighbour
  23.7 0.0 collective-permute-done.from_near
  23.7 4.8 %collective-permute-done.1.from_far = bf16[8,32,128]{2,1,0:T(8,128)(2,1)S(1)} collective-permute-done((bf16[8,32,128]{2,1,0:T(8,128)(2,1)S(1)}, bf16[8,32,128]{2,1,0:T(8,128)(2,1)S(1)}, u32[]{:S(2)}, u32[]{:S(2)}) %collective-permute-start.1) | collective-permute-done | bytes 65568 | tf_op jit(solution)/shard_map/ppermute | solution.py:173
  28.5 0.6 shard_map.92
  29.1 1.1 %collective-permute-start.2 = (bf16[10,32,128]{2,1,0:T(8,128)(2,1)}, bf16[10,32,128]{2,1,0:T(8,128)(2,1)S(1)}, u32[]{:S(2)}, u32[]{:S(2)}) collective-permute-start(bf16[10,32,128]{2,1,0:T(8,128)(2,1)} %get-tuple-element.25), channel_id=1, source_target_pairs={{0,4},{4,8},{8,12},{12,16},{16,20},{20,24},{24,28},{28,32},{32,36}... | collective-permute-start | bytes 245768 | tf_op jit(solution)/shard_map/ppermute | solution.py:176
  30.3 7.6 %collective-permute-start.3 = (bf16[10,32,128]{2,1,0:T(8,128)(2,1)S(1)}, bf16[10,32,128]{2,1,0:T(8,128)(2,1)S(1)}, u32[]{:S(2)}, u32[]{:S(2)}) collective-permute-start(bf16[10,32,128]{2,1,0:T(8,128)(2,1)S(1)} %get-tuple-element.26), channel_id=1, source_target_pairs={{4,0},{8,4},{12,8},{16,12},{20,16},{24,20},{28,24},{32,28},{36,32}... | collective-permute-start | bytes 245768 | tf_op jit(solution)/shard_map/ppermute | solution.py:177
  37.8 0.0 copy-done
  37.8 0.6 gather_fusion
  38.5 1.4 %collective-permute-done.2.from_above = bf16[10,32,128]{2,1,0:T(8,128)(2,1)S(1)} collective-permute-done((bf16[10,32,128]{2,1,0:T(8,128)(2,1)}, bf16[10,32,128]{2,1,0:T(8,128)(2,1)S(1)}, u32[]{:S(2)}, u32[]{:S(2)}) %collective-permute-start.2) | collective-permute-done | bytes 81952 | tf_op jit(solution)/shard_map/ppermute | solution.py:176
  39.9 0.0 collective-permute-done.3.from_below
  39.9 0.0 all-to-all-done.rows
  39.9 0.0 copy-start.1
  39.9 2.8 %copy-done.1 = bf16[8,8,3,128,128]{4,3,2,1,0:T(8,128)(2,1)S(1)} copy-done((bf16[8,8,3,128,128]{4,3,2,1,0:T(8,128)(2,1)S(1)}, bf16[8,8,3,128,128]{4,3,2,1,0:T(8,128)(2,1)}, u32[]{:S(2)}) %copy-start.1) | copy-done | bytes 6291480
  42.7 0.0 copy-start.4
  42.7 1.6 %copy-done.4 = bf16[8,8,128,128]{3,2,1,0:T(8,128)(2,1)S(1)} copy-done((bf16[8,8,128,128]{3,2,1,0:T(8,128)(2,1)S(1)}, bf16[8,8,128,128]{3,2,1,0:T(8,128)(2,1)}, u32[]{:S(2)}) %copy-start.4) | copy-done | bytes 2097176
  44.3 0.0 copy-start.7
  44.3 1.2 %copy-done.7 = f32[64,32,128]{2,1,0:T(8,128)S(1)} copy-done((f32[64,32,128]{2,1,0:T(8,128)S(1)}, f32[64,32,128]{2,1,0:T(8,128)}, u32[]{:S(2)}) %copy-start.7) | copy-done | bytes 1048600
  45.5 0.0 copy-start.9
  45.5 0.7 copy-done.9
  46.1 0.0 copy-start.10
  46.1 0.7 copy-done.10
  46.8 0.0 copy-start.3
  46.8 4.1 %shard_map.93 = (bf16[64,32,128]{2,1,0:T(8,128)(2,1)S(1)}, bf16[8,32,128]{2,1,0:T(8,128)(2,1)S(1)}, bf16[8,32,128]{2,1,0:T(8,128)(2,1)S(1)}, f32[64,32,128]{2,1,0:T(8,128)S(1)}) custom-call(s32[192]{0:T(256)S(1)} %reshape.52.neighbour, s32[4]{0:T(128)S(1)} %gather_fusion, s32[4]{0:T(128)S(1)} %bitcast.19, f32[4]{0:T(128)S(1)} %bitcast.20, ...), custom_call_target="tpu_custom_call" | custom-call | tf_op jit(solution)/shard_map/pallas_call | solution.py:145
  50.9 0.1 collective-permute-start.4
  51.0 1.9 %collective-permute-start.5 = (bf16[8,32,128]{2,1,0:T(8,128)(2,1)S(1)}, bf16[8,32,128]{2,1,0:T(8,128)(2,1)S(1)}, u32[]{:S(2)}, u32[]{:S(2)}) collective-permute-start(bf16[8,32,128]{2,1,0:T(8,128)(2,1)S(1)} %get-tuple-element.30), channel_id=1, source_target_pairs={{0,4},{1,2},{2,1},{3,7},{4,0},{5,6},{6,5},{7,3},{8,12},{9,10},{10,... | collective-permute-start | bytes 196616 | tf_op jit(solution)/shard_map/ppermute | solution.py:173
  52.9 0.0 collective-permute-done.4.from_near
  52.9 6.3 %collective-permute-done.5.from_far = bf16[8,32,128]{2,1,0:T(8,128)(2,1)S(1)} collective-permute-done((bf16[8,32,128]{2,1,0:T(8,128)(2,1)S(1)}, bf16[8,32,128]{2,1,0:T(8,128)(2,1)S(1)}, u32[]{:S(2)}, u32[]{:S(2)}) %collective-permute-start.5) | collective-permute-done | bytes 65568 | tf_op jit(solution)/shard_map/ppermute | solution.py:173
  59.2 0.1 collective-permute-start.6
  59.3 7.6 %collective-permute-start.7 = (bf16[10,32,128]{2,1,0:T(8,128)(2,1)S(1)}, bf16[10,32,128]{2,1,0:T(8,128)(2,1)S(1)}, u32[]{:S(2)}, u32[]{:S(2)}) collective-permute-start(bf16[10,32,128]{2,1,0:T(8,128)(2,1)S(1)} %get-tuple-element.32), channel_id=1, source_target_pairs={{4,0},{8,4},{12,8},{16,12},{20,16},{24,20},{28,24},{32,28},{36,32}... | collective-permute-start | bytes 245768 | tf_op jit(solution)/shard_map/ppermute | solution.py:177
  66.9 1.7 %collective-permute-done.6.from_above = bf16[10,32,128]{2,1,0:T(8,128)(2,1)S(1)} collective-permute-done((bf16[10,32,128]{2,1,0:T(8,128)(2,1)S(1)}, bf16[10,32,128]{2,1,0:T(8,128)(2,1)S(1)}, u32[]{:S(2)}, u32[]{:S(2)}) %collective-permute-start.6) | collective-permute-done | bytes 81952 | tf_op jit(solution)/shard_map/ppermute | solution.py:176
  68.6 0.0 collective-permute-done.7.from_below
  68.6 0.0 copy-done.5
  68.6 0.0 copy-start.2
  68.6 2.8 %copy-done.2 = bf16[8,8,3,128,128]{4,3,2,1,0:T(8,128)(2,1)S(1)} copy-done((bf16[8,8,3,128,128]{4,3,2,1,0:T(8,128)(2,1)S(1)}, bf16[8,8,3,128,128]{4,3,2,1,0:T(8,128)(2,1)}, u32[]{:S(2)}) %copy-start.2) | copy-done | bytes 6291480
  71.4 4.0 %shard_map.95 = (bf16[64,32,128]{2,1,0:T(8,128)(2,1)S(1)}, bf16[8,32,128]{2,1,0:T(8,128)(2,1)S(1)}, bf16[8,32,128]{2,1,0:T(8,128)(2,1)S(1)}) custom-call(s32[192]{0:T(256)S(1)} %reshape.52.neighbour, bf16[64,32,128]{2,1,0:T(8,128)(2,1)S(1)} %get-tuple-element.28.x, bf16[8,32,128]{2,1,0:T(8,128)(2,1)S(1)} %collective-permute-done.4.from_near, ...), custom_call_target="tpu_custom_call" | custom-call | tf_op jit(solution)/shard_map/pallas_call | solution.py:145
  75.5 0.1 collective-permute-start.8
  75.6 2.5 %collective-permute-start.9 = (bf16[8,32,128]{2,1,0:T(8,128)(2,1)S(1)}, bf16[8,32,128]{2,1,0:T(8,128)(2,1)S(1)}, u32[]{:S(2)}, u32[]{:S(2)}) collective-permute-start(bf16[8,32,128]{2,1,0:T(8,128)(2,1)S(1)} %get-tuple-element.36), channel_id=1, source_target_pairs={{0,4},{1,2},{2,1},{3,7},{4,0},{5,6},{6,5},{7,3},{8,12},{9,10},{10,... | collective-permute-start | bytes 196616 | tf_op jit(solution)/shard_map/ppermute | solution.py:173
  78.1 0.0 collective-permute-done.8.from_near
  78.1 5.2 %collective-permute-done.9.from_far = bf16[8,32,128]{2,1,0:T(8,128)(2,1)S(1)} collective-permute-done((bf16[8,32,128]{2,1,0:T(8,128)(2,1)S(1)}, bf16[8,32,128]{2,1,0:T(8,128)(2,1)S(1)}, u32[]{:S(2)}, u32[]{:S(2)}) %collective-permute-start.9) | collective-permute-done | bytes 65568 | tf_op jit(solution)/shard_map/ppermute | solution.py:173
  83.3 0.1 collective-permute-start.10
  83.4 8.3 %collective-permute-start.11 = (bf16[10,32,128]{2,1,0:T(8,128)(2,1)S(1)}, bf16[10,32,128]{2,1,0:T(8,128)(2,1)S(1)}, u32[]{:S(2)}, u32[]{:S(2)}) collective-permute-start(bf16[10,32,128]{2,1,0:T(8,128)(2,1)S(1)} %get-tuple-element.38), channel_id=1, source_target_pairs={{4,0},{8,4},{12,8},{16,12},{20,16},{24,20},{28,24},{32,28},{36,32}... | collective-permute-start | bytes 245768 | tf_op jit(solution)/shard_map/ppermute | solution.py:177
  91.7 1.7 %collective-permute-done.10.from_above = bf16[10,32,128]{2,1,0:T(8,128)(2,1)S(1)} collective-permute-done((bf16[10,32,128]{2,1,0:T(8,128)(2,1)S(1)}, bf16[10,32,128]{2,1,0:T(8,128)(2,1)S(1)}, u32[]{:S(2)}, u32[]{:S(2)}) %collective-permute-start.10) | collective-permute-done | bytes 81952 | tf_op jit(solution)/shard_map/ppermute | solution.py:176
  93.4 0.0 collective-permute-done.11.from_below
  93.4 0.0 copy-done.3
  93.4 5.3 %shard_map.97 = f32[2048,128]{1,0:T(8,128)} custom-call(s32[192]{0:T(256)S(1)} %reshape.52.neighbour, bf16[64,32,128]{2,1,0:T(8,128)(2,1)S(1)} %get-tuple-element.34.x, bf16[8,32,128]{2,1,0:T(8,128)(2,1)S(1)} %collective-permute-done.8.from_near, bf16[8,32,128]{2,1,0:T(8,128)(2,1)S(1)} %collective-permute-done.9.from_far, ...), custom_call_target="tpu_custom_call" | custom-call | tf_op jit(solution)/shard_map/pallas_call | solution.py:145
  (3 shorter events, 0.0 us)
Async XLA Ops:
  0.0 37.8 %copy-start = (s32[64]{0:T(128)S(1)}, s32[64]{0:T(128)}, u32[]{:S(2)}) copy-start(s32[64]{0:T(128)} %param.14) | copy-start | bytes 772
  1.6 38.2 %all-to-all-start = ((bf16[64,32,128]{2,1,0:T(8,128)(2,1)}), bf16[64,32,128]{2,1,0:T(8,128)(2,1)S(1)}, u32[]{:S(2)}, u32[]{:S(2)}) async-start(bf16[64,32,128]{2,1,0:T(8,128)(2,1)} %broadcast_in_dim.9), calls=%async_computation | async-start | bytes 1048576 | tf_op jit(solution)/shard_map/all_to_all | solution.py:189
  14.2 1.2 %copy-start.8 = (f32[32,8,8,128]{3,2,1,0:T(8,128)S(1)}, f32[32,8,8,128]{3,2,1,0:T(8,128)}, u32[]{:S(2)}) copy-start(f32[32,8,8,128]{3,2,1,0:T(8,128)} %param.9) | copy-start | bytes 3145732
  15.4 53.2 %copy-start.5 = (bf16[8,8,128,128]{3,2,1,0:T(8,128)(2,1)S(1)}, bf16[8,8,128,128]{3,2,1,0:T(8,128)(2,1)}, u32[]{:S(2)}) copy-start(bf16[8,8,128,128]{3,2,1,0:T(8,128)(2,1)} %param.11) | copy-start | bytes 6291460
  16.1 1.0 copy-start.6
  17.1 6.7 %collective-permute-start = (bf16[8,32,128]{2,1,0:T(8,128)(2,1)S(1)}, bf16[8,32,128]{2,1,0:T(8,128)(2,1)S(1)}, u32[]{:S(2)}, u32[]{:S(2)}) collective-permute-start(bf16[8,32,128]{2,1,0:T(8,128)(2,1)S(1)} %get-tuple-element.23), channel_id=1, source_target_pairs={{0,1},{1,0},{2,3},{3,2},{4,5},{5,4},{6,7},{7,6},{8,9},{9,8},{10,11... | collective-permute-start | bytes 196616 | tf_op jit(solution)/shard_map/ppermute | solution.py:174
  18.0 10.5 %collective-permute-start.1 = (bf16[8,32,128]{2,1,0:T(8,128)(2,1)S(1)}, bf16[8,32,128]{2,1,0:T(8,128)(2,1)S(1)}, u32[]{:S(2)}, u32[]{:S(2)}) collective-permute-start(bf16[8,32,128]{2,1,0:T(8,128)(2,1)S(1)} %get-tuple-element.24), channel_id=1, source_target_pairs={{0,4},{1,2},{2,1},{3,7},{4,0},{5,6},{6,5},{7,3},{8,12},{9,10},{10,... | collective-permute-start | bytes 196616 | tf_op jit(solution)/shard_map/ppermute | solution.py:173
  29.1 10.7 %collective-permute-start.2 = (bf16[10,32,128]{2,1,0:T(8,128)(2,1)}, bf16[10,32,128]{2,1,0:T(8,128)(2,1)S(1)}, u32[]{:S(2)}, u32[]{:S(2)}) collective-permute-start(bf16[10,32,128]{2,1,0:T(8,128)(2,1)} %get-tuple-element.25), channel_id=1, source_target_pairs={{0,4},{4,8},{8,12},{12,16},{16,20},{20,24},{24,28},{28,32},{32,36}... | collective-permute-start | bytes 245768 | tf_op jit(solution)/shard_map/ppermute | solution.py:176
  30.3 9.6 %collective-permute-start.3 = (bf16[10,32,128]{2,1,0:T(8,128)(2,1)S(1)}, bf16[10,32,128]{2,1,0:T(8,128)(2,1)S(1)}, u32[]{:S(2)}, u32[]{:S(2)}) collective-permute-start(bf16[10,32,128]{2,1,0:T(8,128)(2,1)S(1)} %get-tuple-element.26), channel_id=1, source_target_pairs={{4,0},{8,4},{12,8},{16,12},{20,16},{24,20},{28,24},{32,28},{36,32}... | collective-permute-start | bytes 245768 | tf_op jit(solution)/shard_map/ppermute | solution.py:177
  39.9 2.8 %copy-start.1 = (bf16[8,8,3,128,128]{4,3,2,1,0:T(8,128)(2,1)S(1)}, bf16[8,8,3,128,128]{4,3,2,1,0:T(8,128)(2,1)}, u32[]{:S(2)}) copy-start(bf16[8,8,3,128,128]{4,3,2,1,0:T(8,128)(2,1)} %param.10) | copy-start | bytes 18874372
  42.7 1.6 %copy-start.4 = (bf16[8,8,128,128]{3,2,1,0:T(8,128)(2,1)S(1)}, bf16[8,8,128,128]{3,2,1,0:T(8,128)(2,1)}, u32[]{:S(2)}) copy-start(bf16[8,8,128,128]{3,2,1,0:T(8,128)(2,1)} %param.11) | copy-start | bytes 6291460
  44.3 1.2 %copy-start.7 = (f32[64,32,128]{2,1,0:T(8,128)S(1)}, f32[64,32,128]{2,1,0:T(8,128)}, u32[]{:S(2)}) copy-start(f32[64,32,128]{2,1,0:T(8,128)} %copy-done.6) | copy-start | bytes 3145732
  45.5 0.7 copy-start.9
  46.1 0.7 copy-start.10
  46.8 46.6 %copy-start.3 = (bf16[8,8,3,128,128]{4,3,2,1,0:T(8,128)(2,1)S(1)}, bf16[8,8,3,128,128]{4,3,2,1,0:T(8,128)(2,1)}, u32[]{:S(2)}) copy-start(bf16[8,8,3,128,128]{4,3,2,1,0:T(8,128)(2,1)} %param.10) | copy-start | bytes 18874372
  50.9 2.0 %collective-permute-start.4 = (bf16[8,32,128]{2,1,0:T(8,128)(2,1)S(1)}, bf16[8,32,128]{2,1,0:T(8,128)(2,1)S(1)}, u32[]{:S(2)}, u32[]{:S(2)}) collective-permute-start(bf16[8,32,128]{2,1,0:T(8,128)(2,1)S(1)} %get-tuple-element.29), channel_id=1, source_target_pairs={{0,1},{1,0},{2,3},{3,2},{4,5},{5,4},{6,7},{7,6},{8,9},{9,8},{10,11... | collective-permute-start | bytes 196616 | tf_op jit(solution)/shard_map/ppermute | solution.py:174
  51.0 8.2 %collective-permute-start.5 = (bf16[8,32,128]{2,1,0:T(8,128)(2,1)S(1)}, bf16[8,32,128]{2,1,0:T(8,128)(2,1)S(1)}, u32[]{:S(2)}, u32[]{:S(2)}) collective-permute-start(bf16[8,32,128]{2,1,0:T(8,128)(2,1)S(1)} %get-tuple-element.30), channel_id=1, source_target_pairs={{0,4},{1,2},{2,1},{3,7},{4,0},{5,6},{6,5},{7,3},{8,12},{9,10},{10,... | collective-permute-start | bytes 196616 | tf_op jit(solution)/shard_map/ppermute | solution.py:173
  59.2 9.4 %collective-permute-start.6 = (bf16[10,32,128]{2,1,0:T(8,128)(2,1)S(1)}, bf16[10,32,128]{2,1,0:T(8,128)(2,1)S(1)}, u32[]{:S(2)}, u32[]{:S(2)}) collective-permute-start(bf16[10,32,128]{2,1,0:T(8,128)(2,1)S(1)} %get-tuple-element.31), channel_id=1, source_target_pairs={{0,4},{4,8},{8,12},{12,16},{16,20},{20,24},{24,28},{28,32},{32,36}... | collective-permute-start | bytes 245768 | tf_op jit(solution)/shard_map/ppermute | solution.py:176
  59.3 9.3 %collective-permute-start.7 = (bf16[10,32,128]{2,1,0:T(8,128)(2,1)S(1)}, bf16[10,32,128]{2,1,0:T(8,128)(2,1)S(1)}, u32[]{:S(2)}, u32[]{:S(2)}) collective-permute-start(bf16[10,32,128]{2,1,0:T(8,128)(2,1)S(1)} %get-tuple-element.32), channel_id=1, source_target_pairs={{4,0},{8,4},{12,8},{16,12},{20,16},{24,20},{28,24},{32,28},{36,32}... | collective-permute-start | bytes 245768 | tf_op jit(solution)/shard_map/ppermute | solution.py:177
  68.6 2.8 %copy-start.2 = (bf16[8,8,3,128,128]{4,3,2,1,0:T(8,128)(2,1)S(1)}, bf16[8,8,3,128,128]{4,3,2,1,0:T(8,128)(2,1)}, u32[]{:S(2)}) copy-start(bf16[8,8,3,128,128]{4,3,2,1,0:T(8,128)(2,1)} %param.10) | copy-start | bytes 18874372
  75.5 2.6 %collective-permute-start.8 = (bf16[8,32,128]{2,1,0:T(8,128)(2,1)S(1)}, bf16[8,32,128]{2,1,0:T(8,128)(2,1)S(1)}, u32[]{:S(2)}, u32[]{:S(2)}) collective-permute-start(bf16[8,32,128]{2,1,0:T(8,128)(2,1)S(1)} %get-tuple-element.35), channel_id=1, source_target_pairs={{0,1},{1,0},{2,3},{3,2},{4,5},{5,4},{6,7},{7,6},{8,9},{9,8},{10,11... | collective-permute-start | bytes 196616 | tf_op jit(solution)/shard_map/ppermute | solution.py:174
  75.6 7.7 %collective-permute-start.9 = (bf16[8,32,128]{2,1,0:T(8,128)(2,1)S(1)}, bf16[8,32,128]{2,1,0:T(8,128)(2,1)S(1)}, u32[]{:S(2)}, u32[]{:S(2)}) collective-permute-start(bf16[8,32,128]{2,1,0:T(8,128)(2,1)S(1)} %get-tuple-element.36), channel_id=1, source_target_pairs={{0,4},{1,2},{2,1},{3,7},{4,0},{5,6},{6,5},{7,3},{8,12},{9,10},{10,... | collective-permute-start | bytes 196616 | tf_op jit(solution)/shard_map/ppermute | solution.py:173
  83.3 10.2 %collective-permute-start.10 = (bf16[10,32,128]{2,1,0:T(8,128)(2,1)S(1)}, bf16[10,32,128]{2,1,0:T(8,128)(2,1)S(1)}, u32[]{:S(2)}, u32[]{:S(2)}) collective-permute-start(bf16[10,32,128]{2,1,0:T(8,128)(2,1)S(1)} %get-tuple-element.37), channel_id=1, source_target_pairs={{0,4},{4,8},{8,12},{12,16},{16,20},{20,24},{24,28},{28,32},{32,36}... | collective-permute-start | bytes 245768 | tf_op jit(solution)/shard_map/ppermute | solution.py:176
  83.4 10.1 %collective-permute-start.11 = (bf16[10,32,128]{2,1,0:T(8,128)(2,1)S(1)}, bf16[10,32,128]{2,1,0:T(8,128)(2,1)S(1)}, u32[]{:S(2)}, u32[]{:S(2)}) collective-permute-start(bf16[10,32,128]{2,1,0:T(8,128)(2,1)S(1)} %get-tuple-element.38), channel_id=1, source_target_pairs={{4,0},{8,4},{12,8},{16,12},{20,16},{24,20},{28,24},{32,28},{36,32}... | collective-permute-start | bytes 245768 | tf_op jit(solution)/shard_map/ppermute | solution.py:177

commit v2 on v0

v2 whole, which is shorter than its diff:
```python
import functools

import jax
import jax.numpy as jnp
from jax import lax
from jax.experimental import pallas as pl
from jax.experimental.pallas import tpu as pltpu
from jax.sharding import PartitionSpec as P

BF16 = jnp.bfloat16
F32 = jnp.float32
WIDE = 10
CORNERS = (0, 7, 56, 63)
CORNER_HALOS = (0, 9, 90, 99)
INNER = tuple(b for b in range(64) if b not in CORNERS)

dot_t = functools.partial(
    lax.dot_general,
    dimension_numbers=(((1,), (1,)), ((), ())),
    preferred_element_type=F32,
)


def parity():
    return lax.rem(lax.axis_index("slab"), 2)


def even_tile():
    return lax.rem(lax.axis_index("tile"), 2) == 0


def far_is_real():
    slab = lax.axis_index("slab")
    return jnp.logical_or(slab == 1, slab == 2)


def above_is_real():
    return lax.axis_index("tile") > 0


def below_is_real():
    return lax.axis_index("tile") < lax.axis_size("tile") - 1


def only_if(real, value):
    return jnp.where(real, value, jnp.zeros_like(value))


def send_edges(x, to_near, to_far, to_mate, to_other):
    right, even = parity() == 0, even_tile()
    for r in range(8):
        first, last = x(r * 8), x(r * 8 + 7)
        to_near[r] = jnp.where(right, last, first)
        to_far[r] = jnp.where(right, first, last)
        top, bottom = x(r), x(56 + r)
        to_mate[r] = jnp.where(even, bottom, top)
        to_other[r] = jnp.where(even, top, bottom)


def bring_old(old, held, sems):
    copies = []
    for r in range(8):
        part = pl.ds(8 * r, 8)
        copies.append(pltpu.make_async_copy(old.at[:, part], held.at[:, part], sems.at[r]))
        copies[-1].start()
    return copies


def prepare(old, stream, x, everyone, to_near, to_far, to_mate, to_other, held, sems):
    copies = bring_old(old, held, sems)
    row = stream[0].astype(BF16)
    for t in range(everyone.shape[0]):
        everyone[t] = row
    rows = held.reshape(32 * 64, 128)
    for r in range(8):
        copies[r].wait()
        for b in range(8 * r, 8 * r + 8):
            x[b] = rows[pl.ds(b, 32, stride=64), :].astype(BF16)
    send_edges(lambda b: x[b], to_near, to_far, to_mate, to_other)


def pass_corners(from_near, from_far, to_mate, to_other):
    right, even = parity() == 0, even_tile()
    real = far_is_real()
    ends = []
    for r in (0, 7):
        near, far = from_near[r], only_if(real, from_far[r])
        ends.append((jnp.where(right, far, near), jnp.where(right, near, far)))
    for i in range(2):
        top, bottom = ends[0][i], ends[1][i]
        to_mate[i] = jnp.where(even, bottom, top)
        to_other[i] = jnp.where(even, top, bottom)


def widen(grid, x, corners, from_near, from_far, from_mate, from_other):
    right, even = parity() == 0, even_tile()
    real, above, below = far_is_real(), above_is_real(), below_is_real()
    for r in range(8):
        near, far = from_near[r], only_if(real, from_far[r])
        grid[(r + 1) * WIDE] = jnp.where(right, far, near)
        grid[(r + 1) * WIDE + 9] = jnp.where(right, near, far)
        mate, other = from_mate[r], from_other[r]
        grid[1 + r] = only_if(above, jnp.where(even, other, mate))
        grid[91 + r] = only_if(below, jnp.where(even, mate, other))
        grid[pl.ds((r + 1) * WIDE + 1, 8)] = x[pl.ds(8 * r, 8)]
    if corners is not None:
        for i, b in enumerate(CORNERS):
            grid[(b // 8 + 1) * WIDE + b % 8 + 1] = corners[i]


def sweep(ids, upstream, rhs, upwind, diag, store):
    remainders = []
    for b in ids:
        weights = jnp.concatenate([upwind[b, k] for k in range(3)], axis=1)
        remainders.append((rhs[b] - dot_t(upstream(b), weights)).astype(BF16))
    for i in range(0, len(ids), 2):
        both = jnp.concatenate(remainders[i : i + 2], axis=0)
        weights = jnp.concatenate([diag[ids[i]], diag[ids[i + 1]]], axis=0)
        conc = dot_t(both, weights)
        store(ids[i], conc[:32, :128])
        store(ids[i + 1], conc[32:, 128:])


def sweep_inner(neighbour, grid, rhs, upwind, diag, store, before=None, after=None):
    def upstream(b):
        return jnp.concatenate([grid[neighbour[3 * b + k]] for k in range(3)], axis=1)

    for r in range(0, 8, 2):
        if before is not None:
            before(r)
        sweep([b for b in range(8 * r, 8 * r + 16) if b in INNER], upstream, rhs, upwind, diag, store)
        if after is not None:
            after(r)


def inner_first(
    neighbour, well, row, where, rate, x, near, far, mate, other, rows, old, upwind_far, diag_far,
    x_next, grid, rhs, upwind, diag, held, old_sems, sems,
):
    old_copies = bring_old(old, held, old_sems)
    copies = []
    for r in range(0, 8, 2):
        part = pl.ds(8 * r, 16)
        copies.append(pltpu.make_async_copy(upwind_far.at[part], upwind.at[part], sems.at[r]))
        copies.append(pltpu.make_async_copy(diag_far.at[part], diag.at[part], sems.at[r + 1]))
    for copy in copies:
        copy.start()
    widen(grid, x, None, near, far, mate, other)
    for copy in old_copies:
        copy.wait()
    old_rows = held.reshape(32 * 64, 128)
    for b in range(64):
        rhs[b] = old_rows[pl.ds(b, 32, stride=64), :]
    for p in range(4):
        b = where[0, 0, p]
        rhs[b] = rhs[b] + rate[0, 0, p] * rows[row[well[0, 0, p]]].astype(F32)

    def store(b, conc):
        x_next[b] = conc.astype(BF16)

    def before(r):
        copies[r].wait()
        copies[r + 1].wait()

    sweep_inner(neighbour, grid, rhs, upwind, diag, store, before)


def inner(neighbour, x, corners, near, far, mate, other, rhs, upwind, diag, x_next, grid):
    widen(grid, x, corners, near, far, mate, other)

    def store(b, conc):
        x_next[b] = conc.astype(BF16)

    sweep_inner(neighbour, grid, rhs, upwind, diag, store)


def sweep_corners(neighbour, grid, mate, other, rhs, upwind, diag, store):
    even, above, below = even_tile(), above_is_real(), below_is_real()
    halos = [only_if(above, jnp.where(even, other[i], mate[i])) for i in range(2)]
    halos += [only_if(below, jnp.where(even, mate[i], other[i])) for i in range(2)]

    def upstream(b):
        i = CORNERS.index(b)
        slots = [neighbour[3 * b + k] for k in range(3)]
        return jnp.concatenate([jnp.where(n == CORNER_HALOS[i], halos[i], grid[n]) for n in slots], axis=1)

    sweep(CORNERS, upstream, rhs, upwind, diag, store)


def outer(neighbour, x, grid, mate, other, rhs, upwind, diag, corners, to_near, to_far, to_mate, to_other):
    def store(b, conc):
        corners[CORNERS.index(b)] = conc.astype(BF16)

    sweep_corners(neighbour, grid, mate, other, rhs, upwind, diag, store)
    block = lambda b: corners[CORNERS.index(b)] if b in CORNERS else x[b]
    send_edges(block, to_near, to_far, to_mate, to_other)


def inner_last(
    neighbour, x, corners, near, far, mate, other, rhs, upwind, diag, out, ends, grid, held, sems
):
    widen(grid, x, corners, near, far, mate, other)
    rows = held.reshape(32 * 64, 128)
    copies = []

    def store(b, conc):
        rows[pl.ds(b, 32, stride=64), :] = conc

    def after(r):
        for s in (r, r + 1):
            part = pl.ds(8 * s, 8)
            if s in (0, 7):
                ends[:, pl.ds(0 if s == 0 else 8, 8)] = held[:, part]
            else:
                copies.append(pltpu.make_async_copy(held.at[:, part], out.at[:, part], sems.at[s]))
                copies[-1].start()

    sweep_inner(neighbour, grid, rhs, upwind, diag, store, after=after)
    for copy in copies:
        copy.wait()


def outer_last(neighbour, partial, grid, mate, other, rhs, upwind, diag, ends, out, held, sems):
    del partial
    held[...] = ends[...]
    rows = held.reshape(32 * 16, 128)

    def store(b, conc):
        rows[pl.ds(b if b < 8 else b - 48, 32, stride=16), :] = conc

    sweep_corners(neighbour, grid, mate, other, rhs, upwind, diag, store)
    copies = []
    for i, r in enumerate((0, 7)):
        copies.append(pltpu.make_async_copy(held.at[:, pl.ds(8 * i, 8)], out.at[:, pl.ds(8 * r, 8)], sems.at[i]))
        copies[-1].start()
    for copy in copies:
        copy.wait()


VMEM, SMEM, ANY, HBM = (pl.BlockSpec(memory_space=m) for m in (pltpu.VMEM, pltpu.SMEM, pl.ANY, pltpu.HBM))


def call(kernel, outs, args, scratch=(), aliases=None, flops=0, moved=0):
    values = []
    for where, value in args:
        if where is VMEM:
            value = pltpu.with_memory_space_constraint(value, pltpu.VMEM)
        if where is HBM:
            value = pltpu.with_memory_space_constraint(value, pltpu.HBM)
        values.append(value)
    shapes = [pltpu.VMEM(s.shape, s.dtype) if where is VMEM else s for where, s in outs]
    return pl.pallas_call(
        kernel,
        out_shape=shapes,
        in_specs=[where for where, _ in args],
        out_specs=[where for where, _ in outs],
        scratch_shapes=list(scratch),
        input_output_aliases=aliases or {},
        cost_estimate=pl.CostEstimate(flops=flops, bytes_accessed=moved, transcendentals=0),
        compiler_params=pltpu.CompilerParams(vmem_limit_bytes=6 * 2**20),
    )(*values)


def blocks(count, dtype=BF16):
    return VMEM, jax.ShapeDtypeStruct((count, 32, 128), dtype)


def body(
    old_conc, upwind, diag_inverse, neighbours, streams, injector_row, perf_well, perf_block, perf_rate
):
    tiles, slabs = lax.axis_size("tile"), lax.axis_size("slab")
    both = ("tile", "slab")
    on_chip = [(s, s ^ 1) for s in range(slabs)]
    far_pairs, mates, others = [], [], []
    for t in range(tiles):
        for s in range(slabs):
            here = t * slabs + s
            far_pairs.append((here, t * slabs + 3 - s if s in (1, 2) else (t ^ 1) * slabs + s))
            mates.append((here, (t ^ 1) * slabs + s))
            other = t - 1 if t % 2 == 0 else t + 1
            others.append((here, other * slabs + s if 0 <= other < tiles else t * slabs + (s ^ 1)))

    def vmem(*values):
        return [(VMEM, v) for v in values]

    def exchange(to_near, to_far, to_mate, to_other):
        from_far = lax.ppermute(to_far, both, far_pairs)
        from_near = lax.ppermute(to_near, "slab", on_chip)
        from_mate = lax.ppermute(to_mate, both, mates)
        from_other = lax.ppermute(to_other, both, others)
        return from_near, from_far, from_mate, from_other

    def exchange_corners(from_near, from_far):
        to_mate, to_other = call(pass_corners, [blocks(2)] * 2, vmem(from_near, from_far))
        return lax.ppermute(to_mate, both, mates), lax.ppermute(to_other, both, others)

    dma = pltpu.SemaphoreType.DMA
    held = pltpu.VMEM((32, 64, 128), F32)
    edges = [blocks(8)] * 4
    neighbour = (SMEM, neighbours.reshape(-1))
    old = (HBM, old_conc.reshape(32, 64, 128))
    work = dict(flops=2 * 64 * 4 * 32 * 128 * 128, moved=9 * 2**20)

    x, everyone, *sent = call(
        prepare, [blocks(64), blocks(tiles), *edges], [old, (VMEM, streams)], [held, dma((8,))], moved=4 * 2**20
    )
    rows = lax.all_to_all(everyone, "tile", 0, 0)
    got = exchange(*sent)
    ends = exchange_corners(*got[:2])
    upwind_shape = jax.ShapeDtypeStruct((64, 3, 128, 128), BF16)
    diag_shape = jax.ShapeDtypeStruct((64, 128, 128), BF16)
    wells = [(SMEM, perf_well), (SMEM, injector_row), (SMEM, perf_block), (SMEM, perf_rate)]
    x, grid, rhs, *weights = call(
        inner_first,
        [blocks(64), blocks(100), blocks(64, F32), (VMEM, upwind_shape), (VMEM, diag_shape)],
        [neighbour, *wells, *vmem(x, *got, rows), old]
        + [(HBM, upwind.reshape(upwind_shape.shape)), (HBM, diag_inverse.reshape(diag_shape.shape))],
        [held, dma((8,)), dma((8,))],
        **work,
    )
    for last in (False, True):
        corners, *sent = call(outer, [blocks(4), *edges], [neighbour, *vmem(x, grid, *ends, rhs, *weights)])
        got = exchange(*sent)
        ends = exchange_corners(*got[:2])
        args = [neighbour, *vmem(x, corners, *got, rhs, *weights)]
        if not last:
            x, grid = call(inner, [blocks(64), blocks(100)], args, **work)
    whole = (ANY, jax.ShapeDtypeStruct((32, 64, 128), F32))
    partial, border, grid = call(
        inner_last,
        [whole, (VMEM, jax.ShapeDtypeStruct((32, 16, 128), F32)), blocks(100)],
        args,
        [held, pltpu.SemaphoreType.DMA((8,))],
        **work,
    )
    (out,) = call(
        outer_last,
        [whole],
        [neighbour, (ANY, partial), *vmem(grid, *ends, rhs, *weights, border)],
        [pltpu.VMEM((32, 16, 128), F32), pltpu.SemaphoreType.DMA((2,))],
        {1: 0},
    )
    return out.reshape(old_conc.shape)


def solution(mesh):
    in_specs = (
        P(None, "tile", "slab", None),
        P("tile", "slab", None, None, None),
        P("tile", "slab", None, None),
        P("tile", "slab", None),
        P("tile", None, None),
        P(),
        P("tile", "slab", None),
        P("tile", "slab", None),
        P("tile", "slab", None),
    )
    out_specs = P(None, "tile", "slab", None)
    return jax.shard_map(body, mesh=mesh, in_specs=in_specs, out_specs=out_specs, check_vma=False)
```

time: 461 us -> 82.2 us (0.18)
  the two profiles are of different devices: /device:TPU:1 before, /device:TPU:65 now
where the time goes in v2:
time: 82.2 us; the launch traced here: 81.8 us
  starting transfers between devices  44.7 us (54%)
  Pallas kernels  22 us (27%)
  waiting for transfers between devices  10.4 us (13%)
  local copies, waits for them, and re-layouts  4.29 us (5%)
    pallas_call x10, Pallas kernels, call(): pl.pallas_call(kernel, out_shape=shapes, in_specs=[where for where, _ in...  22 us
    ppermute x3, starting transfers between devices, exchange(): from_far = lax.ppermute(to_far, both, far_pairs)  14.3 us
    all_to_all x1, starting transfers between devices, body(): rows = lax.all_to_all(everyone, 'tile', 0, 0)  10.8 us
    ppermute x3, starting transfers between devices, exchange_corners(): lax.ppermute(to_other, both, others)  8.43 us
    ppermute x3, starting transfers between devices, exchange(): from_other = lax.ppermute(to_other, both, others)  6.58 us
    ppermute x3, waiting for transfers between devices, exchange(): from_other = lax.ppermute(to_other, both, others)  5.9 us
    ppermute x3, waiting for transfers between devices, exchange(): from_far = lax.ppermute(to_far, both, far_pairs)  4.2 us
    unnamed x11, local copies, waits for them, and re-layouts  4.16 us
  transfers between devices with their start and end apart: 19, of which 7 were waited for; matrix products, arithmetic and copies ran while one was open for 1% of the time, Pallas kernels for 20%

profile of v2, /device:TPU:65, one launch (start us, length us, event | category | flops | bytes accessed | tf_op | source)
XLA Modules:
  0.0 81.8 jit_solution(6854174626176418865)
XLA Ops:
  0.0 0.0 copy-start
  0.0 0.7 copy-done
  0.7 2.4 %shard_map.91 = (bf16[64,32,128]{2,1,0:T(8,128)(2,1)S(1)}, bf16[64,32,128]{2,1,0:T(8,128)(2,1)}, bf16[8,32,128]{2,1,0:T(8,128)(2,1)S(1)}, bf16[8,32,128]{2,1,0:T...) custom-call(f32[32,64,128]{2,1,0:T(8,128)} %bitcast.5, f32[1,32,128]{2,1,0:T(8,128)S(1)} %copy-done), custom_call_target="tpu_custom_call" | custom-call | bytes 4194304 | tf_op jit(solution)/shard_map/pallas_call | solution.py:252
  3.1 10.8 %all-to-all-start = ((bf16[64,32,128]{2,1,0:T(8,128)(2,1)}), bf16[64,32,128]{2,1,0:T(8,128)(2,1)S(1)}, u32[]{:S(2)}, u32[]{:S(2)}) async-start(bf16[64,32,128]{2,1,0:T(8,128)(2,1)} %get-tuple-element.42), calls=%async_computation | async-start | bytes 1048576 | tf_op jit(solution)/shard_map/all_to_all | solution.py:307
  13.9 1.3 %collective-permute-start = (bf16[8,32,128]{2,1,0:T(8,128)(2,1)S(1)}, bf16[8,32,128]{2,1,0:T(8,128)(2,1)S(1)}, u32[]{:S(2)}, u32[]{:S(2)}) collective-permute-start(bf16[8,32,128]{2,1,0:T(8,128)(2,1)S(1)} %get-tuple-element.38), channel_id=1, source_target_pairs={{0,1},{1,0},{2,3},{3,2},{4,5},{5,4},{6,7},{7,6},{8,9},{9,8},{10,11... | collective-permute-start | bytes 196616 | tf_op jit(solution)/shard_map/ppermute | solution.py:288
  15.2 4.2 %collective-permute-start.1 = (bf16[8,32,128]{2,1,0:T(8,128)(2,1)S(1)}, bf16[8,32,128]{2,1,0:T(8,128)(2,1)S(1)}, u32[]{:S(2)}, u32[]{:S(2)}) collective-permute-start(bf16[8,32,128]{2,1,0:T(8,128)(2,1)S(1)} %get-tuple-element.39), channel_id=1, source_target_pairs={{0,4},{1,2},{2,1},{3,7},{4,0},{5,6},{6,5},{7,3},{8,12},{9,10},{10,... | collective-permute-start | bytes 196616 | tf_op jit(solution)/shard_map/ppermute | solution.py:287
  19.4 1.2 %collective-permute-start.2 = (bf16[8,32,128]{2,1,0:T(8,128)(2,1)S(1)}, bf16[8,32,128]{2,1,0:T(8,128)(2,1)S(1)}, u32[]{:S(2)}, u32[]{:S(2)}) collective-permute-start(bf16[8,32,128]{2,1,0:T(8,128)(2,1)S(1)} %get-tuple-element.40), channel_id=1, source_target_pairs={{0,4},{1,5},{2,6},{3,7},{4,0},{5,1},{6,2},{7,3},{8,12},{9,13},{10,... | collective-permute-start | bytes 196616 | tf_op jit(solution)/shard_map/ppermute | solution.py:289
  20.6 3.9 %collective-permute-start.3 = (bf16[8,32,128]{2,1,0:T(8,128)(2,1)S(1)}, bf16[8,32,128]{2,1,0:T(8,128)(2,1)S(1)}, u32[]{:S(2)}, u32[]{:S(2)}) collective-permute-start(bf16[8,32,128]{2,1,0:T(8,128)(2,1)S(1)} %get-tuple-element.41), channel_id=1, source_target_pairs={{0,1},{1,0},{2,3},{3,2},{4,8},{5,9},{6,10},{7,11},{8,4},{9,5},{10,... | collective-permute-start | bytes 196616 | tf_op jit(solution)/shard_map/ppermute | solution.py:290
  24.5 0.8 %copy.11 = s32[8,8,3]{2,1,0:T(8,128)S(1)} copy(s32[8,8,3]{1,0,2:T(8,128)} %param.12) | data formatting | bytes 1536 | tf_op args[3]
  25.3 0.1 reshape.15.neighbour
  25.5 0.0 collective-permute-done.near.from_near
  25.5 1.0 %collective-permute-done.1.far.from_far = bf16[8,32,128]{2,1,0:T(8,128)(2,1)S(1)} collective-permute-done((bf16[8,32,128]{2,1,0:T(8,128)(2,1)S(1)}, bf16[8,32,128]{2,1,0:T(8,128)(2,1)S(1)}, u32[]{:S(2)}, u32[]{:S(2)}) %collective-permute-start.1) | collective-permute-done | bytes 65568 | tf_op jit(solution)/shard_map/ppermute | solution.py:287
  26.5 1.0 %collective-permute-start.4 = (bf16[2,32,128]{2,1,0:T(8,128)(2,1)S(1)}, bf16[2,32,128]{2,1,0:T(8,128)(2,1)S(1)}, u32[]{:S(2)}, u32[]{:S(2)}) collective-permute-start(bf16[2,32,128]{2,1,0:T(8,128)(2,1)S(1)} %get-tuple-element.45), channel_id=1, source_target_pairs={{0,4},{1,5},{2,6},{3,7},{4,0},{5,1},{6,2},{7,3},{8,12},{9,13},{10,... | collective-permute-start | bytes 49160 | tf_op jit(solution)/shard_map/ppermute | solution.py:295
  27.5 2.6 %collective-permute-start.5 = (bf16[2,32,128]{2,1,0:T(8,128)(2,1)S(1)}, bf16[2,32,128]{2,1,0:T(8,128)(2,1)S(1)}, u32[]{:S(2)}, u32[]{:S(2)}) collective-permute-start(bf16[2,32,128]{2,1,0:T(8,128)(2,1)S(1)} %get-tuple-element.46), channel_id=1, source_target_pairs={{0,1},{1,0},{2,3},{3,2},{4,8},{5,9},{6,10},{7,11},{8,4},{9,5},{10,... | collective-permute-start | bytes 49160 | tf_op jit(solution)/shard_map/ppermute | solution.py:295
  30.1 0.0 collective-permute-done.2.mate
  30.1 3.1 %collective-permute-done.3.other = bf16[8,32,128]{2,1,0:T(8,128)(2,1)S(1)} collective-permute-done((bf16[8,32,128]{2,1,0:T(8,128)(2,1)S(1)}, bf16[8,32,128]{2,1,0:T(8,128)(2,1)S(1)}, u32[]{:S(2)}, u32[]{:S(2)}) %collective-permute-start.3) | collective-permute-done | bytes 65568 | tf_op jit(solution)/shard_map/ppermute | solution.py:290
  33.1 0.0 all-to-all-done.rows
  33.1 0.0 copy-start.1
  33.1 0.7 copy-done.1
  33.8 0.0 copy-start.2
  33.8 0.7 copy-done.2
  34.4 0.0 copy-start.3
  34.4 0.7 copy-done.3
  35.1 0.0 copy-start.4
  35.1 0.7 copy-done.4
  35.7 8.1 %shard_map.92 = (bf16[64,32,128]{2,1,0:T(8,128)(2,1)S(1)}, bf16[100,32,128]{2,1,0:T(8,128)(2,1)S(1)}, f32[64,32,128]{2,1,0:T(8,128)S(1)}, bf16[64,3,128,128]{3,2,1,0:T(8,128)(2,1)S(1)}, bf16[64,128,128]{2,1,0:T(8,128)(2,1)S(1)}) custom-call(s32[192]{0:T(256)S(1)} %reshape.15.neighbour, s32[1,1,4]{2,1,0:T(1,128)S(1)} %copy-done.1, s32[64]{0:T(128)S(1)} %copy-done.2, ...), custom_call_target="tpu_custom_call" | custom-call | flops 268435456 | bytes 9437184 | tf_op jit(solution)/shard_map/pallas_call | solution.py:252
  43.9 0.0 collective-permute-done.4.mate
  43.9 0.0 collective-permute-done.5.other
  43.9 0.9 %shard_map.94 = (bf16[4,32,128]{2,1,0:T(8,128)(2,1)S(1)}, bf16[8,32,128]{2,1,0:T(8,128)(2,1)S(1)}, bf16[8,32,128]{2,1,0:T(8,128)(2,1)S(1)}, bf16[8,32,128]{2,1,0:T(8,128)(2,1)S(1)}, bf16[8,32,128]{2,1,0:T(8,128)(2,1)S(1)}) custom-call(s32[192]{0:T(256)S(1)} %reshape.15.neighbour, bf16[64,32,128]{2,1,0:T(8,128)(2,1)S(1)} %get-tuple-element.43.x, ...), custom_call_target="tpu_custom_call" | custom-call | tf_op jit(solution)/shard_map/pallas_call | solution.py:252
  44.9 0.9 %collective-permute-start.6 = (bf16[8,32,128]{2,1,0:T(8,128)(2,1)S(1)}, bf16[8,32,128]{2,1,0:T(8,128)(2,1)S(1)}, u32[]{:S(2)}, u32[]{:S(2)}) collective-permute-start(bf16[8,32,128]{2,1,0:T(8,128)(2,1)S(1)} %get-tuple-element.51), channel_id=1, source_target_pairs={{0,1},{1,0},{2,3},{3,2},{4,5},{5,4},{6,7},{7,6},{8,9},{9,8},{10,11... | collective-permute-start | bytes 196616 | tf_op jit(solution)/shard_map/ppermute | solution.py:288
  45.8 4.4 %collective-permute-start.7 = (bf16[8,32,128]{2,1,0:T(8,128)(2,1)S(1)}, bf16[8,32,128]{2,1,0:T(8,128)(2,1)S(1)}, u32[]{:S(2)}, u32[]{:S(2)}) collective-permute-start(bf16[8,32,128]{2,1,0:T(8,128)(2,1)S(1)} %get-tuple-element.52), channel_id=1, source_target_pairs={{0,4},{1,2},{2,1},{3,7},{4,0},{5,6},{6,5},{7,3},{8,12},{9,10},{10,... | collective-permute-start | bytes 196616 | tf_op jit(solution)/shard_map/ppermute | solution.py:287
  50.2 0.0 collective-permute-start.8
  50.2 1.2 %collective-permute-start.9 = (bf16[8,32,128]{2,1,0:T(8,128)(2,1)S(1)}, bf16[8,32,128]{2,1,0:T(8,128)(2,1)S(1)}, u32[]{:S(2)}, u32[]{:S(2)}) collective-permute-start(bf16[8,32,128]{2,1,0:T(8,128)(2,1)S(1)} %get-tuple-element.54), channel_id=1, source_target_pairs={{0,1},{1,0},{2,3},{3,2},{4,8},{5,9},{6,10},{7,11},{8,4},{9,5},{10,... | collective-permute-start | bytes 196616 | tf_op jit(solution)/shard_map/ppermute | solution.py:290
  51.4 0.0 collective-permute-done.6.near.from_near
  51.4 2.7 %collective-permute-done.7.far.from_far = bf16[8,32,128]{2,1,0:T(8,128)(2,1)S(1)} collective-permute-done((bf16[8,32,128]{2,1,0:T(8,128)(2,1)S(1)}, bf16[8,32,128]{2,1,0:T(8,128)(2,1)S(1)}, u32[]{:S(2)}, u32[]{:S(2)}) %collective-permute-start.7) | collective-permute-done | bytes 65568 | tf_op jit(solution)/shard_map/ppermute | solution.py:287
  54.1 0.1 collective-permute-start.10
  54.2 2.1 %collective-permute-start.11 = (bf16[2,32,128]{2,1,0:T(8,128)(2,1)S(1)}, bf16[2,32,128]{2,1,0:T(8,128)(2,1)S(1)}, u32[]{:S(2)}, u32[]{:S(2)}) collective-permute-start(bf16[2,32,128]{2,1,0:T(8,128)(2,1)S(1)} %get-tuple-element.58), channel_id=1, source_target_pairs={{0,1},{1,0},{2,3},{3,2},{4,8},{5,9},{6,10},{7,11},{8,4},{9,5},{10,... | collective-permute-start | bytes 49160 | tf_op jit(solution)/shard_map/ppermute | solution.py:295
  56.3 0.0 collective-permute-done.8.mate
  56.3 1.2 %collective-permute-done.9.other = bf16[8,32,128]{2,1,0:T(8,128)(2,1)S(1)} collective-permute-done((bf16[8,32,128]{2,1,0:T(8,128)(2,1)S(1)}, bf16[8,32,128]{2,1,0:T(8,128)(2,1)S(1)}, u32[]{:S(2)}, u32[]{:S(2)}) %collective-permute-start.9) | collective-permute-done | bytes 65568 | tf_op jit(solution)/shard_map/ppermute | solution.py:290
  57.6 3.5 %shard_map.95 = (bf16[64,32,128]{2,1,0:T(8,128)(2,1)S(1)}, bf16[100,32,128]{2,1,0:T(8,128)(2,1)S(1)}) custom-call(s32[192]{0:T(256)S(1)} %reshape.15.neighbour, bf16[64,32,128]{2,1,0:T(8,128)(2,1)S(1)} %get-tuple-element.43.x, bf16[4,32,128]{2,1,0:T(8,128)(2,1)S(1)} %get-tuple-element.50.corners, ...), custom_call_target="tpu_custom_call" | custom-call | flops 268435456 | bytes 9437184 | tf_op jit(solution)/shard_map/pallas_call | solution.py:252
  61.0 0.0 collective-permute-done.10.mate
  61.0 0.3 collective-permute-done.11.other
  61.3 0.9 %shard_map.97 = (bf16[4,32,128]{2,1,0:T(8,128)(2,1)S(1)}, bf16[8,32,128]{2,1,0:T(8,128)(2,1)S(1)}, bf16[8,32,128]{2,1,0:T(8,128)(2,1)S(1)}, bf16[8,32,128]{2,1,0:T(8,128)(2,1)S(1)}, bf16[8,32,128]{2,1,0:T(8,128)(2,1)S(1)}) custom-call(s32[192]{0:T(256)S(1)} %reshape.15.neighbour, bf16[64,32,128]{2,1,0:T(8,128)(2,1)S(1)} %get-tuple-element.55.x, ...), custom_call_target="tpu_custom_call" | custom-call | tf_op jit(solution)/shard_map/pallas_call | solution.py:252
  62.2 0.1 collective-permute-start.12
  62.3 5.7 %collective-permute-start.13 = (bf16[8,32,128]{2,1,0:T(8,128)(2,1)S(1)}, bf16[8,32,128]{2,1,0:T(8,128)(2,1)S(1)}, u32[]{:S(2)}, u32[]{:S(2)}) collective-permute-start(bf16[8,32,128]{2,1,0:T(8,128)(2,1)S(1)} %get-tuple-element.61), channel_id=1, source_target_pairs={{0,4},{1,2},{2,1},{3,7},{4,0},{5,6},{6,5},{7,3},{8,12},{9,10},{10,... | collective-permute-start | bytes 196616 | tf_op jit(solution)/shard_map/ppermute | solution.py:287
  68.0 0.0 collective-permute-start.14
  68.0 1.5 %collective-permute-start.15 = (bf16[8,32,128]{2,1,0:T(8,128)(2,1)S(1)}, bf16[8,32,128]{2,1,0:T(8,128)(2,1)S(1)}, u32[]{:S(2)}, u32[]{:S(2)}) collective-permute-start(bf16[8,32,128]{2,1,0:T(8,128)(2,1)S(1)} %get-tuple-element.63), channel_id=1, source_target_pairs={{0,1},{1,0},{2,3},{3,2},{4,8},{5,9},{6,10},{7,11},{8,4},{9,5},{10,... | collective-permute-start | bytes 196616 | tf_op jit(solution)/shard_map/ppermute | solution.py:290
  69.5 0.0 collective-permute-done.12.near.from_near
  69.5 0.5 collective-permute-done.13.far.from_far
  70.0 0.1 collective-permute-start.16
  70.1 3.8 %collective-permute-start.17 = (bf16[2,32,128]{2,1,0:T(8,128)(2,1)S(1)}, bf16[2,32,128]{2,1,0:T(8,128)(2,1)S(1)}, u32[]{:S(2)}, u32[]{:S(2)}) collective-permute-start(bf16[2,32,128]{2,1,0:T(8,128)(2,1)S(1)} %get-tuple-element.67), channel_id=1, source_target_pairs={{0,1},{1,0},{2,3},{3,2},{4,8},{5,9},{6,10},{7,11},{8,4},{9,5},{10,... | collective-permute-start | bytes 49160 | tf_op jit(solution)/shard_map/ppermute | solution.py:295
  73.9 0.0 collective-permute-done.14.mate
  73.9 1.6 %collective-permute-done.15.other = bf16[8,32,128]{2,1,0:T(8,128)(2,1)S(1)} collective-permute-done((bf16[8,32,128]{2,1,0:T(8,128)(2,1)S(1)}, bf16[8,32,128]{2,1,0:T(8,128)(2,1)S(1)}, u32[]{:S(2)}, u32[]{:S(2)}) %collective-permute-start.15) | collective-permute-done | bytes 65568 | tf_op jit(solution)/shard_map/ppermute | solution.py:290
  75.5 4.4 %shard_map.98 = (f32[32,64,128]{2,1,0:T(8,128)}, f32[32,16,128]{2,1,0:T(8,128)S(1)}, bf16[100,32,128]{2,1,0:T(8,128)(2,1)S(1)}) custom-call(s32[192]{0:T(256)S(1)} %reshape.15.neighbour, bf16[64,32,128]{2,1,0:T(8,128)(2,1)S(1)} %get-tuple-element.55.x, bf16[4,32,128]{2,1,0:T(8,128)(2,1)S(1)} %get-tuple-element.59.corners, ...), custom_call_target="tpu_custom_call" | custom-call | flops 268435456 | bytes 9437184 | tf_op jit(solution)/shard_map/pallas_call | solution.py:252
  79.9 0.0 collective-permute-done.16.mate
  80.0 0.0 collective-permute-done.17.other
  80.0 1.6 %shard_map.100 = f32[32,64,128]{2,1,0:T(8,128)} custom-call(s32[192]{0:T(256)S(1)} %reshape.15.neighbour, f32[32,64,128]{2,1,0:T(8,128)} %get-tuple-element.64.partial, bf16[100,32,128]{2,1,0:T(8,128)(2,1)S(1)} %get-tuple-element.65.grid, bf16[2,32,128]{2,1,0:T(8,128)(2,1)S(1)} %collective-permute-done.16.mate, ...), custom_call_target="tpu_custom_call", output_to_operand_aliasing={{}: (1, {})} | custom-call | tf_op jit(solution)/shard_map/pallas_call | solution.py:252
  (3 shorter events, 0.0 us)
Async XLA Ops:
  0.0 0.7 copy-start
  3.1 30.0 %all-to-all-start = ((bf16[64,32,128]{2,1,0:T(8,128)(2,1)}), bf16[64,32,128]{2,1,0:T(8,128)(2,1)S(1)}, u32[]{:S(2)}, u32[]{:S(2)}) async-start(bf16[64,32,128]{2,1,0:T(8,128)(2,1)} %get-tuple-element.42), calls=%async_computation | async-start | bytes 1048576 | tf_op jit(solution)/shard_map/all_to_all | solution.py:307
  13.9 11.5 %collective-permute-start = (bf16[8,32,128]{2,1,0:T(8,128)(2,1)S(1)}, bf16[8,32,128]{2,1,0:T(8,128)(2,1)S(1)}, u32[]{:S(2)}, u32[]{:S(2)}) collective-permute-start(bf16[8,32,128]{2,1,0:T(8,128)(2,1)S(1)} %get-tuple-element.38), channel_id=1, source_target_pairs={{0,1},{1,0},{2,3},{3,2},{4,5},{5,4},{6,7},{7,6},{8,9},{9,8},{10,11... | collective-permute-start | bytes 196616 | tf_op jit(solution)/shard_map/ppermute | solution.py:288
  15.2 11.2 %collective-permute-start.1 = (bf16[8,32,128]{2,1,0:T(8,128)(2,1)S(1)}, bf16[8,32,128]{2,1,0:T(8,128)(2,1)S(1)}, u32[]{:S(2)}, u32[]{:S(2)}) collective-permute-start(bf16[8,32,128]{2,1,0:T(8,128)(2,1)S(1)} %get-tuple-element.39), channel_id=1, source_target_pairs={{0,4},{1,2},{2,1},{3,7},{4,0},{5,6},{6,5},{7,3},{8,12},{9,10},{10,... | collective-permute-start | bytes 196616 | tf_op jit(solution)/shard_map/ppermute | solution.py:287
  19.4 10.6 %collective-permute-start.2 = (bf16[8,32,128]{2,1,0:T(8,128)(2,1)S(1)}, bf16[8,32,128]{2,1,0:T(8,128)(2,1)S(1)}, u32[]{:S(2)}, u32[]{:S(2)}) collective-permute-start(bf16[8,32,128]{2,1,0:T(8,128)(2,1)S(1)} %get-tuple-element.40), channel_id=1, source_target_pairs={{0,4},{1,5},{2,6},{3,7},{4,0},{5,1},{6,2},{7,3},{8,12},{9,13},{10,... | collective-permute-start | bytes 196616 | tf_op jit(solution)/shard_map/ppermute | solution.py:289
  20.6 12.5 %collective-permute-start.3 = (bf16[8,32,128]{2,1,0:T(8,128)(2,1)S(1)}, bf16[8,32,128]{2,1,0:T(8,128)(2,1)S(1)}, u32[]{:S(2)}, u32[]{:S(2)}) collective-permute-start(bf16[8,32,128]{2,1,0:T(8,128)(2,1)S(1)} %get-tuple-element.41), channel_id=1, source_target_pairs={{0,1},{1,0},{2,3},{3,2},{4,8},{5,9},{6,10},{7,11},{8,4},{9,5},{10,... | collective-permute-start | bytes 196616 | tf_op jit(solution)/shard_map/ppermute | solution.py:290
  26.5 17.4 %collective-permute-start.4 = (bf16[2,32,128]{2,1,0:T(8,128)(2,1)S(1)}, bf16[2,32,128]{2,1,0:T(8,128)(2,1)S(1)}, u32[]{:S(2)}, u32[]{:S(2)}) collective-permute-start(bf16[2,32,128]{2,1,0:T(8,128)(2,1)S(1)} %get-tuple-element.45), channel_id=1, source_target_pairs={{0,4},{1,5},{2,6},{3,7},{4,0},{5,1},{6,2},{7,3},{8,12},{9,13},{10,... | collective-permute-start | bytes 49160 | tf_op jit(solution)/shard_map/ppermute | solution.py:295
  27.5 16.4 %collective-permute-start.5 = (bf16[2,32,128]{2,1,0:T(8,128)(2,1)S(1)}, bf16[2,32,128]{2,1,0:T(8,128)(2,1)S(1)}, u32[]{:S(2)}, u32[]{:S(2)}) collective-permute-start(bf16[2,32,128]{2,1,0:T(8,128)(2,1)S(1)} %get-tuple-element.46), channel_id=1, source_target_pairs={{0,1},{1,0},{2,3},{3,2},{4,8},{5,9},{6,10},{7,11},{8,4},{9,5},{10,... | collective-permute-start | bytes 49160 | tf_op jit(solution)/shard_map/ppermute | solution.py:295
  33.1 0.7 copy-start.1
  33.8 0.7 copy-start.2
  34.4 0.7 copy-start.3
  35.1 0.7 copy-start.4
  44.9 6.6 %collective-permute-start.6 = (bf16[8,32,128]{2,1,0:T(8,128)(2,1)S(1)}, bf16[8,32,128]{2,1,0:T(8,128)(2,1)S(1)}, u32[]{:S(2)}, u32[]{:S(2)}) collective-permute-start(bf16[8,32,128]{2,1,0:T(8,128)(2,1)S(1)} %get-tuple-element.51), channel_id=1, source_target_pairs={{0,1},{1,0},{2,3},{3,2},{4,5},{5,4},{6,7},{7,6},{8,9},{9,8},{10,11... | collective-permute-start | bytes 196616 | tf_op jit(solution)/shard_map/ppermute | solution.py:288
  45.8 8.3 %collective-permute-start.7 = (bf16[8,32,128]{2,1,0:T(8,128)(2,1)S(1)}, bf16[8,32,128]{2,1,0:T(8,128)(2,1)S(1)}, u32[]{:S(2)}, u32[]{:S(2)}) collective-permute-start(bf16[8,32,128]{2,1,0:T(8,128)(2,1)S(1)} %get-tuple-element.52), channel_id=1, source_target_pairs={{0,4},{1,2},{2,1},{3,7},{4,0},{5,6},{6,5},{7,3},{8,12},{9,10},{10,... | collective-permute-start | bytes 196616 | tf_op jit(solution)/shard_map/ppermute | solution.py:287
  50.2 6.1 %collective-permute-start.8 = (bf16[8,32,128]{2,1,0:T(8,128)(2,1)S(1)}, bf16[8,32,128]{2,1,0:T(8,128)(2,1)S(1)}, u32[]{:S(2)}, u32[]{:S(2)}) collective-permute-start(bf16[8,32,128]{2,1,0:T(8,128)(2,1)S(1)} %get-tuple-element.53), channel_id=1, source_target_pairs={{0,4},{1,5},{2,6},{3,7},{4,0},{5,1},{6,2},{7,3},{8,12},{9,13},{10,... | collective-permute-start | bytes 196616 | tf_op jit(solution)/shard_map/ppermute | solution.py:289
  50.2 7.3 %collective-permute-start.9 = (bf16[8,32,128]{2,1,0:T(8,128)(2,1)S(1)}, bf16[8,32,128]{2,1,0:T(8,128)(2,1)S(1)}, u32[]{:S(2)}, u32[]{:S(2)}) collective-permute-start(bf16[8,32,128]{2,1,0:T(8,128)(2,1)S(1)} %get-tuple-element.54), channel_id=1, source_target_pairs={{0,1},{1,0},{2,3},{3,2},{4,8},{5,9},{6,10},{7,11},{8,4},{9,5},{10,... | collective-permute-start | bytes 196616 | tf_op jit(solution)/shard_map/ppermute | solution.py:290
  54.1 6.9 %collective-permute-start.10 = (bf16[2,32,128]{2,1,0:T(8,128)(2,1)S(1)}, bf16[2,32,128]{2,1,0:T(8,128)(2,1)S(1)}, u32[]{:S(2)}, u32[]{:S(2)}) collective-permute-start(bf16[2,32,128]{2,1,0:T(8,128)(2,1)S(1)} %get-tuple-element.57), channel_id=1, source_target_pairs={{0,4},{1,5},{2,6},{3,7},{4,0},{5,1},{6,2},{7,3},{8,12},{9,13},{10,... | collective-permute-start | bytes 49160 | tf_op jit(solution)/shard_map/ppermute | solution.py:295
  54.2 7.1 %collective-permute-start.11 = (bf16[2,32,128]{2,1,0:T(8,128)(2,1)S(1)}, bf16[2,32,128]{2,1,0:T(8,128)(2,1)S(1)}, u32[]{:S(2)}, u32[]{:S(2)}) collective-permute-start(bf16[2,32,128]{2,1,0:T(8,128)(2,1)S(1)} %get-tuple-element.58), channel_id=1, source_target_pairs={{0,1},{1,0},{2,3},{3,2},{4,8},{5,9},{6,10},{7,11},{8,4},{9,5},{10,... | collective-permute-start | bytes 49160 | tf_op jit(solution)/shard_map/ppermute | solution.py:295
  62.2 7.3 %collective-permute-start.12 = (bf16[8,32,128]{2,1,0:T(8,128)(2,1)S(1)}, bf16[8,32,128]{2,1,0:T(8,128)(2,1)S(1)}, u32[]{:S(2)}, u32[]{:S(2)}) collective-permute-start(bf16[8,32,128]{2,1,0:T(8,128)(2,1)S(1)} %get-tuple-element.60), channel_id=1, source_target_pairs={{0,1},{1,0},{2,3},{3,2},{4,5},{5,4},{6,7},{7,6},{8,9},{9,8},{10,11... | collective-permute-start | bytes 196616 | tf_op jit(solution)/shard_map/ppermute | solution.py:288
  62.3 7.7 %collective-permute-start.13 = (bf16[8,32,128]{2,1,0:T(8,128)(2,1)S(1)}, bf16[8,32,128]{2,1,0:T(8,128)(2,1)S(1)}, u32[]{:S(2)}, u32[]{:S(2)}) collective-permute-start(bf16[8,32,128]{2,1,0:T(8,128)(2,1)S(1)} %get-tuple-element.61), channel_id=1, source_target_pairs={{0,4},{1,2},{2,1},{3,7},{4,0},{5,6},{6,5},{7,3},{8,12},{9,10},{10,... | collective-permute-start | bytes 196616 | tf_op jit(solution)/shard_map/ppermute | solution.py:287
  68.0 5.9 %collective-permute-start.14 = (bf16[8,32,128]{2,1,0:T(8,128)(2,1)S(1)}, bf16[8,32,128]{2,1,0:T(8,128)(2,1)S(1)}, u32[]{:S(2)}, u32[]{:S(2)}) collective-permute-start(bf16[8,32,128]{2,1,0:T(8,128)(2,1)S(1)} %get-tuple-element.62), channel_id=1, source_target_pairs={{0,4},{1,5},{2,6},{3,7},{4,0},{5,1},{6,2},{7,3},{8,12},{9,13},{10,... | collective-permute-start | bytes 196616 | tf_op jit(solution)/shard_map/ppermute | solution.py:289
  68.0 7.5 %collective-permute-start.15 = (bf16[8,32,128]{2,1,0:T(8,128)(2,1)S(1)}, bf16[8,32,128]{2,1,0:T(8,128)(2,1)S(1)}, u32[]{:S(2)}, u32[]{:S(2)}) collective-permute-start(bf16[8,32,128]{2,1,0:T(8,128)(2,1)S(1)} %get-tuple-element.63), channel_id=1, source_target_pairs={{0,1},{1,0},{2,3},{3,2},{4,8},{5,9},{6,10},{7,11},{8,4},{9,5},{10,... | collective-permute-start | bytes 196616 | tf_op jit(solution)/shard_map/ppermute | solution.py:290
  70.0 9.9 %collective-permute-start.16 = (bf16[2,32,128]{2,1,0:T(8,128)(2,1)S(1)}, bf16[2,32,128]{2,1,0:T(8,128)(2,1)S(1)}, u32[]{:S(2)}, u32[]{:S(2)}) collective-permute-start(bf16[2,32,128]{2,1,0:T(8,128)(2,1)S(1)} %get-tuple-element.66), channel_id=1, source_target_pairs={{0,4},{1,5},{2,6},{3,7},{4,0},{5,1},{6,2},{7,3},{8,12},{9,13},{10,... | collective-permute-start | bytes 49160 | tf_op jit(solution)/shard_map/ppermute | solution.py:295
  70.1 9.8 %collective-permute-start.17 = (bf16[2,32,128]{2,1,0:T(8,128)(2,1)S(1)}, bf16[2,32,128]{2,1,0:T(8,128)(2,1)S(1)}, u32[]{:S(2)}, u32[]{:S(2)}) collective-permute-start(bf16[2,32,128]{2,1,0:T(8,128)(2,1)S(1)} %get-tuple-element.67), channel_id=1, source_target_pairs={{0,1},{1,0},{2,3},{3,2},{4,8},{5,9},{6,10},{7,11},{8,4},{9,5},{10,... | collective-permute-start | bytes 49160 | tf_op jit(solution)/shard_map/ppermute | solution.py:295

commit v3 on v2

--- a/solution.py
+++ b/solution.py
@@ -12,7 +12,9 @@
 WIDE = 10
 CORNERS = (0, 7, 56, 63)
 CORNER_HALOS = (0, 9, 90, 99)
-INNER = tuple(b for b in range(64) if b not in CORNERS)
+INTERIOR = tuple(b for b in range(64) if 0 < b // 8 < 7 and 0 < b % 8 < 7)
+EDGES = tuple(b for b in range(64) if b not in INTERIOR and b not in CORNERS)
+PLANE = 16
 
 dot_t = functools.partial(
     lax.dot_general,
@@ -66,17 +68,39 @@
     return copies
 
 
-def prepare(old, stream, x, everyone, to_near, to_far, to_mate, to_other, held, sems):
+def spread(stream, everyone, held, sem):
+    copy = pltpu.make_async_copy(stream, held, sem)
+    copy.start()
+    copy.wait()
+    row = held[0].astype(BF16)
+    for t in range(PLANE):
+        everyone[t] = row
+
+
+def prepare(old, x, to_near, to_far, held, sems):
     copies = bring_old(old, held, sems)
-    row = stream[0].astype(BF16)
-    for t in range(everyone.shape[0]):
-        everyone[t] = row
     rows = held.reshape(32 * 64, 128)
+    right = parity() == 0
     for r in range(8):
         copies[r].wait()
         for b in range(8 * r, 8 * r + 8):
             x[b] = rows[pl.ds(b, 32, stride=64), :].astype(BF16)
-    send_edges(lambda b: x[b], to_near, to_far, to_mate, to_other)
+        first, last = x[8 * r], x[8 * r + 7]
+        to_near[r] = jnp.where(right, last, first)
+        to_far[r] = jnp.where(right, first, last)
+
+
+def rows_to_send(x, from_near, from_far, to_mate, to_other):
+    right, even = parity() == 0, even_tile()
+    real = far_is_real()
+    rows = []
+    for r in (0, 7):
+        near, far = from_near[r], only_if(real, from_far[r])
+        rows.append([jnp.where(right, far, near), *(x[8 * r + c] for c in range(8)), jnp.where(right, near, far)])
+    for i in range(WIDE):
+        top, bottom = rows[0][i], rows[1][i]
+        to_mate[i] = jnp.where(even, bottom, top)
+        to_other[i] = jnp.where(even, top, bottom)
 
 
 def pass_corners(from_near, from_far, to_mate, to_other):
@@ -92,20 +116,23 @@
         to_other[i] = jnp.where(even, top, bottom)
 
 
-def widen(grid, x, corners, from_near, from_far, from_mate, from_other):
+def at(b):
+    return (b // 8 + 1) * WIDE + b % 8 + 1
+
+
+def widen(grid, from_near, from_far, from_mate, from_other):
     right, even = parity() == 0, even_tile()
     real, above, below = far_is_real(), above_is_real(), below_is_real()
     for r in range(8):
         near, far = from_near[r], only_if(real, from_far[r])
         grid[(r + 1) * WIDE] = jnp.where(right, far, near)
         grid[(r + 1) * WIDE + 9] = jnp.where(right, near, far)
-        mate, other = from_mate[r], from_other[r]
-        grid[1 + r] = only_if(above, jnp.where(even, other, mate))
-        grid[91 + r] = only_if(below, jnp.where(even, mate, other))
-        grid[pl.ds((r + 1) * WIDE + 1, 8)] = x[pl.ds(8 * r, 8)]
-    if corners is not None:
-        for i, b in enumerate(CORNERS):
-            grid[(b // 8 + 1) * WIDE + b % 8 + 1] = corners[i]
+    count = from_mate.shape[0]
+    first = (WIDE - count) // 2
+    for c in range(count):
+        mate, other = from_mate[c], from_other[c]
+        grid[first + c] = only_if(above, jnp.where(even, other, mate))
+        grid[90 + first + c] = only_if(below, jnp.where(even, mate, other))
 
 
 def sweep(ids, upstream, rhs, upwind, diag, store):
@@ -121,57 +148,100 @@
         store(ids[i + 1], conc[32:, 128:])
 
 
-def sweep_inner(neighbour, grid, rhs, upwind, diag, store, before=None, after=None):
-    def upstream(b):
-        return jnp.concatenate([grid[neighbour[3 * b + k]] for k in range(3)], axis=1)
-
-    for r in range(0, 8, 2):
-        if before is not None:
-            before(r)
-        sweep([b for b in range(8 * r, 8 * r + 16) if b in INNER], upstream, rhs, upwind, diag, store)
-        if after is not None:
-            after(r)
-
-
-def inner_first(
-    neighbour, well, row, where, rate, x, near, far, mate, other, rows, old, upwind_far, diag_far,
-    x_next, grid, rhs, upwind, diag, held, old_sems, sems,
+def from_grid(neighbour, grid):
+    return lambda b: jnp.concatenate([grid[neighbour[3 * b + k]] for k in range(3)], axis=1)
+
+
+def row_of(well, near_rows):
+    away = (well // PLANE) ^ (lax.axis_index("tile") // PLANE)
+    row = near_rows[0][well % PLANE]
+    for m in range(1, 4):
+        row = jnp.where(away == m, near_rows[m][well % PLANE], row)
+    return row.astype(F32)
+
+
+def sweep_first(
+    neighbour, well, row, where, rate, x, near, far, mate, other, rows0, rows1, rows2, rows3, old, upwind_far, diag_far,
+    x_next, rhs, upwind, diag, to_near, to_far, to_mate, to_other, grid, held, old_sems, sems,
 ):
     old_copies = bring_old(old, held, old_sems)
     copies = []
-    for r in range(0, 8, 2):
-        part = pl.ds(8 * r, 16)
-        copies.append(pltpu.make_async_copy(upwind_far.at[part], upwind.at[part], sems.at[r]))
-        copies.append(pltpu.make_async_copy(diag_far.at[part], diag.at[part], sems.at[r + 1]))
-    for copy in copies:
-        copy.start()
-    widen(grid, x, None, near, far, mate, other)
-    for copy in old_copies:
-        copy.wait()
+    for r in range(8):
+        part = pl.ds(8 * r, 8)
+        copies.append(
+            (
+                pltpu.make_async_copy(upwind_far.at[part], upwind.at[part], sems.at[2 * r]),
+                pltpu.make_async_copy(diag_far.at[part], diag.at[part], sems.at[2 * r + 1]),
+            )
+        )
+
+    def start(r):
+        for copy in copies[r]:
+            copy.start()
+
+    start(0)
+    start(1)
+    widen(grid, near, far, mate, other)
+    for b in range(64):
+        grid[at(b)] = x[b]
     old_rows = held.reshape(32 * 64, 128)
-    for b in range(64):
-        rhs[b] = old_rows[pl.ds(b, 32, stride=64), :]
+    for r in range(8):
+        old_copies[r].wait()
+        for b in range(8 * r, 8 * r + 8):
+            rhs[b] = old_rows[pl.ds(b, 32, stride=64), :]
     for p in range(4):
         b = where[0, 0, p]
-        rhs[b] = rhs[b] + rate[0, 0, p] * rows[row[well[0, 0, p]]].astype(F32)
+        rhs[b] = rhs[b] + rate[0, 0, p] * row_of(row[well[0, 0, p]], (rows0, rows1, rows2, rows3))
 
     def store(b, conc):
         x_next[b] = conc.astype(BF16)
 
-    def before(r):
-        copies[r].wait()
-        copies[r + 1].wait()
-
-    sweep_inner(neighbour, grid, rhs, upwind, diag, store, before)
-
-
-def inner(neighbour, x, corners, near, far, mate, other, rhs, upwind, diag, x_next, grid):
-    widen(grid, x, corners, near, far, mate, other)
-
-    def store(b, conc):
-        x_next[b] = conc.astype(BF16)
-
-    sweep_inner(neighbour, grid, rhs, upwind, diag, store)
+    upstream = from_grid(neighbour, grid)
+    for r in range(0, 8, 2):
+        for ahead in (r + 2, r + 3):
+            if ahead < 8:
+                start(ahead)
+        for copy in copies[r] + copies[r + 1]:
+            copy.wait()
+        sweep(range(8 * r, 8 * r + 16), upstream, rhs, upwind, diag, store)
+    send_edges(lambda b: x_next[b], to_near, to_far, to_mate, to_other)
+
+
+def fill(grid, parts):
+    if len(parts) == 1:
+        for b in range(64):
+            grid[at(b)] = parts[0][b]
+    else:
+        interior, edges, corners = parts
+        for b in INTERIOR:
+            grid[at(b)] = interior[b]
+        for b in EDGES:
+            grid[at(b)] = edges[b]
+        for i, b in enumerate(CORNERS):
+            grid[at(b)] = corners[i]
+
+
+def inner(count, dtype, neighbour, *refs):
+    parts, (rhs, upwind, diag, interior, grid) = refs[:count], refs[count:]
+    fill(grid, parts)
+
+    def store(b, conc):
+        interior[b] = conc.astype(dtype)
+
+    upstream = from_grid(neighbour, grid)
+    for i in range(0, 36, 18):
+        sweep(INTERIOR[i : i + 18], upstream, rhs, upwind, diag, store)
+
+
+def middle(neighbour, local, near, far, mate, other, rhs, upwind, diag, edges, grid):
+    for b in range(64):
+        grid[at(b)] = local[at(b)]
+    widen(grid, near, far, mate, other)
+
+    def store(b, conc):
+        edges[b] = conc.astype(BF16)
+
+    sweep(EDGES, from_grid(neighbour, grid), rhs, upwind, diag, store)
 
 
 def sweep_corners(neighbour, grid, mate, other, rhs, upwind, diag, store):
@@ -187,35 +257,36 @@
     sweep(CORNERS, upstream, rhs, upwind, diag, store)
 
 
-def outer(neighbour, x, grid, mate, other, rhs, upwind, diag, corners, to_near, to_far, to_mate, to_other):
+def outer(neighbour, edges, grid, mate, other, rhs, upwind, diag, corners, to_near, to_far, to_mate, to_other):
     def store(b, conc):
         corners[CORNERS.index(b)] = conc.astype(BF16)
 
     sweep_corners(neighbour, grid, mate, other, rhs, upwind, diag, store)
-    block = lambda b: corners[CORNERS.index(b)] if b in CORNERS else x[b]
+    block = lambda b: corners[CORNERS.index(b)] if b in CORNERS else edges[b]
     send_edges(block, to_near, to_far, to_mate, to_other)
 
 
-def inner_last(
-    neighbour, x, corners, near, far, mate, other, rhs, upwind, diag, out, ends, grid, held, sems
+def middle_last(
+    neighbour, local, interior, near, far, mate, other, rhs, upwind, diag, out, ends, grid, held, sems
 ):
-    widen(grid, x, corners, near, far, mate, other)
+    for b in range(64):
+        grid[at(b)] = local[at(b)]
+    widen(grid, near, far, mate, other)
     rows = held.reshape(32 * 64, 128)
+
+    def store(b, conc):
+        rows[pl.ds(b, 32, stride=64), :] = conc
+
+    sweep(EDGES, from_grid(neighbour, grid), rhs, upwind, diag, store)
+    for b in INTERIOR:
+        store(b, interior[b])
     copies = []
-
-    def store(b, conc):
-        rows[pl.ds(b, 32, stride=64), :] = conc
-
-    def after(r):
-        for s in (r, r + 1):
-            part = pl.ds(8 * s, 8)
-            if s in (0, 7):
-                ends[:, pl.ds(0 if s == 0 else 8, 8)] = held[:, part]
-            else:
-                copies.append(pltpu.make_async_copy(held.at[:, part], out.at[:, part], sems.at[s]))
-                copies[-1].start()
-
-    sweep_inner(neighbour, grid, rhs, upwind, diag, store, after=after)
+    for r in range(1, 7):
+        part = pl.ds(8 * r, 8)
+        copies.append(pltpu.make_async_copy(held.at[:, part], out.at[:, part], sems.at[r]))
+        copies[-1].start()
+    for i, r in enumerate((0, 7)):
+        ends[:, pl.ds(8 * i, 8)] = held[:, pl.ds(8 * r, 8)]
     for copy in copies:
         copy.wait()
 
@@ -239,20 +310,22 @@
 
 VMEM, SMEM, ANY, HBM = (pl.BlockSpec(memory_space=m) for m in (pltpu.VMEM, pltpu.SMEM, pl.ANY, pltpu.HBM))
 
+SMEM_FROM_HBM = "scalars"
+
 
 def call(kernel, outs, args, scratch=(), aliases=None, flops=0, moved=0):
     values = []
     for where, value in args:
         if where is VMEM:
             value = pltpu.with_memory_space_constraint(value, pltpu.VMEM)
-        if where is HBM:
+        if where in (HBM, SMEM_FROM_HBM):
             value = pltpu.with_memory_space_constraint(value, pltpu.HBM)
         values.append(value)
     shapes = [pltpu.VMEM(s.shape, s.dtype) if where is VMEM else s for where, s in outs]
     return pl.pallas_call(
         kernel,
         out_shape=shapes,
-        in_specs=[where for where, _ in args],
+        in_specs=[SMEM if where is SMEM_FROM_HBM else where for where, _ in args],
         out_specs=[where for where, _ in outs],
         scratch_shapes=list(scratch),
         input_output_aliases=aliases or {},
@@ -296,47 +369,69 @@
 
     dma = pltpu.SemaphoreType.DMA
     held = pltpu.VMEM((32, 64, 128), F32)
+    grid = pltpu.VMEM((100, 32, 128), BF16)
     edges = [blocks(8)] * 4
     neighbour = (SMEM, neighbours.reshape(-1))
     old = (HBM, old_conc.reshape(32, 64, 128))
     work = dict(flops=2 * 64 * 4 * 32 * 128 * 128, moved=9 * 2**20)
 
-    x, everyone, *sent = call(
-        prepare, [blocks(64), blocks(tiles), *edges], [old, (VMEM, streams)], [held, dma((8,))], moved=4 * 2**20
+    (everyone,) = call(spread, [blocks(PLANE)], [(HBM, streams)], [pltpu.VMEM((1, 32, 128), F32), dma(())])
+    planes = [list(range(z, z + PLANE)) for z in range(0, tiles, PLANE)]
+    rows = [lax.all_to_all(everyone, "tile", 0, 0, axis_index_groups=planes)]
+    for m in (1, 2, 3):
+        rows.append(lax.ppermute(rows[0], "tile", [(t, t ^ (m * PLANE)) for t in range(tiles)]))
+
+    x, to_near, to_far = call(
+        prepare, [blocks(64), blocks(8), blocks(8)], [old], [held, dma((8,))], moved=4 * 2**20
     )
-    rows = lax.all_to_all(everyone, "tile", 0, 0)
-    got = exchange(*sent)
-    ends = exchange_corners(*got[:2])
+    from_far = lax.ppermute(to_far, both, far_pairs)
+    from_near = lax.ppermute(to_near, "slab", on_chip)
+    to_mate, to_other = call(rows_to_send, [blocks(WIDE)] * 2, vmem(x, from_near, from_far))
+    got = from_near, from_far, lax.ppermute(to_mate, both, mates), lax.ppermute(to_other, both, others)
+
     upwind_shape = jax.ShapeDtypeStruct((64, 3, 128, 128), BF16)
     diag_shape = jax.ShapeDtypeStruct((64, 128, 128), BF16)
-    wells = [(SMEM, perf_well), (SMEM, injector_row), (SMEM, perf_block), (SMEM, perf_rate)]
-    x, grid, rhs, *weights = call(
-        inner_first,
-        [blocks(64), blocks(100), blocks(64, F32), (VMEM, upwind_shape), (VMEM, diag_shape)],
-        [neighbour, *wells, *vmem(x, *got, rows), old]
+    wells = [(SMEM_FROM_HBM, v) for v in (perf_well, injector_row, perf_block, perf_rate)]
+    x, rhs, *rest = call(
+        sweep_first,
+        [blocks(64), blocks(64, F32), (VMEM, upwind_shape), (VMEM, diag_shape), *edges],
+        [neighbour, *wells, *vmem(x, *got, *rows), old]
         + [(HBM, upwind.reshape(upwind_shape.shape)), (HBM, diag_inverse.reshape(diag_shape.shape))],
-        [held, dma((8,)), dma((8,))],
+        [grid, held, dma((8,)), dma((16,))],
         **work,
     )
+    weights, sent = rest[:2], rest[2:]
+    parts = [x]
     for last in (False, True):
-        corners, *sent = call(outer, [blocks(4), *edges], [neighbour, *vmem(x, grid, *ends, rhs, *weights)])
         got = exchange(*sent)
+        interior, local = call(
+            functools.partial(inner, len(parts), F32 if last else BF16),
+            [blocks(64, F32 if last else BF16), blocks(100)],
+            [neighbour, *vmem(*parts, rhs, *weights)],
+            **work,
+        )
         ends = exchange_corners(*got[:2])
-        args = [neighbour, *vmem(x, corners, *got, rhs, *weights)]
-        if not last:
-            x, grid = call(inner, [blocks(64), blocks(100)], args, **work)
+        if last:
+            break
+        edge_blocks, whole_grid = call(
+            middle, [blocks(64), blocks(100)], [neighbour, *vmem(local, *got, rhs, *weights)], **work
+        )
+        corners, *sent = call(
+            outer, [blocks(4), *edges], [neighbour, *vmem(edge_blocks, whole_grid, *ends, rhs, *weights)]
+        )
+        parts = [interior, edge_blocks, corners]
     whole = (ANY, jax.ShapeDtypeStruct((32, 64, 128), F32))
-    partial, border, grid = call(
-        inner_last,
+    partial, border, whole_grid = call(
+        middle_last,
         [whole, (VMEM, jax.ShapeDtypeStruct((32, 16, 128), F32)), blocks(100)],
-        args,
-        [held, pltpu.SemaphoreType.DMA((8,))],
+        [neighbour, *vmem(local, interior, *got, rhs, *weights)],
+        [held, dma((8,))],
         **work,
     )
     (out,) = call(
         outer_last,
         [whole],
-        [neighbour, (ANY, partial), *vmem(grid, *ends, rhs, *weights, border)],
+        [neighbour, (ANY, partial), *vmem(whole_grid, *ends, rhs, *weights, border)],
         [pltpu.VMEM((32, 16, 128), F32), pltpu.SemaphoreType.DMA((2,))],
         {1: 0},
     )

time: 82.2 us -> 79.6 us (0.968)
  starting transfers between devices: 44.7 us -> 39 us
  waiting for transfers between devices: 10.4 us -> 16.1 us
  local copies, waits for them, and re-layouts: 4.29 us -> 0.95 us
  Pallas kernels: 22 us -> 22.9 us
    ppermute x0 -> x7, starting transfers between devices: none -> 14.2 us  [the longest x1 5.1 us: body(): from_far = lax.ppermute(to_far, both, far_pairs)]
    ppermute x0 -> x7, waiting for transfers between devices: none -> 11.7 us  [the longest x1 11.1 us: body(): lax.ppermute(to_other, both, others)]
    ppermute x3 -> x2, starting transfers between devices: 14.3 us -> 5.44 us  [exchange(): from_far = lax.ppermute(to_far, both, far_pairs)]
    ppermute x3 -> x2, waiting for transfers between devices: 5.9 us -> 0.01 us  [exchange(): from_other = lax.ppermute(to_other, both, others)]
    ppermute x3 -> x2, waiting for transfers between devices: 4.2 us -> 0.11 us  [exchange(): from_far = lax.ppermute(to_far, both, far_pairs)]
    all_to_all x1, starting transfers between devices: 10.8 us -> 6.77 us  [body(): rows = [lax.all_to_all(everyone, 'tile', 0, 0, axis_index_groups=planes)]]
    ppermute x3 -> x2, starting transfers between devices: 8.43 us -> 4.5 us  [exchange_corners(): lax.ppermute(to_other, both, others)]
    ppermute x3 -> x2, waiting for transfers between devices: 0.27 us -> 4.19 us  [exchange_corners(): lax.ppermute(to_other, both, others)]
  transfers between devices with their start and end apart: 19 -> 20, of which waited for: 7 -> 5; matrix products, arithmetic and copies ran while one was open for 1% -> 1% of each run, Pallas kernels for 20% -> 15%
where the time goes in v3:
time: 79.6 us; the launch traced here: 79.3 us
  starting transfers between devices  39 us (49%)
  Pallas kernels  22.9 us (29%)
  waiting for transfers between devices  16.1 us (20%)
  local copies, waits for them, and re-layouts  0.95 us (1%)
    pallas_call x12, Pallas kernels, call(): pl.pallas_call(kernel, out_shape=shapes, in_specs=[SMEM if where is SMEM_...  22.9 us
    ppermute x1, waiting for transfers between devices, body(): lax.ppermute(to_other, both, others)  11.1 us
    ppermute x2, starting transfers between devices, exchange(): from_other = lax.ppermute(to_other, both, others)  7.34 us
    all_to_all x1, starting transfers between devices, body(): rows = [lax.all_to_all(everyone, 'tile', 0, 0, axis_index_groups=planes)]  6.77 us
    ppermute x2, starting transfers between devices, exchange(): from_far = lax.ppermute(to_far, both, far_pairs)  5.44 us
    ppermute x1, starting transfers between devices, body(): from_far = lax.ppermute(to_far, both, far_pairs)  5.1 us
    ppermute x2, starting transfers between devices, exchange_corners(): lax.ppermute(to_other, both, others)  4.5 us
    ppermute x2, waiting for transfers between devices, exchange_corners(): lax.ppermute(to_other, both, others)  4.19 us
  transfers between devices with their start and end apart: 20, of which 5 were waited for; matrix products, arithmetic and copies ran while one was open for 1% of the time, Pallas kernels for 15%

profile of v3, /device:TPU:65, one launch (start us, length us, event | category | flops | bytes accessed | tf_op | source)
XLA Modules:
  0.0 79.3 jit_solution(5442288024741787715)
XLA Ops:
  0.0 1.4 %shard_map.93 = bf16[16,32,128]{2,1,0:T(8,128)(2,1)} custom-call(f32[1,32,128]{2,1,0:T(8,128)} %stream.1), custom_call_target="tpu_custom_call" | custom-call | tf_op jit(solution)/shard_map/pallas_call | solution.py:325
  1.4 6.8 %all-to-all-start = ((bf16[16,32,128]{2,1,0:T(8,128)(2,1)}), bf16[16,32,128]{2,1,0:T(8,128)(2,1)S(1)}, u32[]{:S(2)}, u32[]{:S(2)}) async-start(bf16[16,32,128]{2,1,0:T(8,128)(2,1)} %shard_map.93), calls=%async_computation | async-start | bytes 262144 | tf_op jit(solution)/shard_map/all_to_all | solution.py:380
  8.2 1.7 %shard_map.91 = (bf16[64,32,128]{2,1,0:T(8,128)(2,1)S(1)}, bf16[8,32,128]{2,1,0:T(8,128)(2,1)S(1)}, bf16[8,32,128]{2,1,0:T(8,128)(2,1)S(1)}) custom-call(f32[32,64,128]{2,1,0:T(8,128)} %bitcast.5), custom_call_target="tpu_custom_call" | custom-call | bytes 4194304 | tf_op jit(solution)/shard_map/pallas_call | solution.py:325
  9.9 1.0 %collective-permute-start = (bf16[8,32,128]{2,1,0:T(8,128)(2,1)S(1)}, bf16[8,32,128]{2,1,0:T(8,128)(2,1)S(1)}, u32[]{:S(2)}, u32[]{:S(2)}) collective-permute-start(bf16[8,32,128]{2,1,0:T(8,128)(2,1)S(1)} %get-tuple-element.37), channel_id=1, source_target_pairs={{0,1},{1,0},{2,3},{3,2},{4,5},{5,4},{6,7},{7,6},{8,9},{9,8},{10,11... | collective-permute-start | bytes 196616 | tf_op jit(solution)/shard_map/ppermute | solution.py:388
  10.9 5.1 %collective-permute-start.1 = (bf16[8,32,128]{2,1,0:T(8,128)(2,1)S(1)}, bf16[8,32,128]{2,1,0:T(8,128)(2,1)S(1)}, u32[]{:S(2)}, u32[]{:S(2)}) collective-permute-start(bf16[8,32,128]{2,1,0:T(8,128)(2,1)S(1)} %get-tuple-element.38), channel_id=1, source_target_pairs={{0,4},{1,2},{2,1},{3,7},{4,0},{5,6},{6,5},{7,3},{8,12},{9,10},{10,... | collective-permute-start | bytes 196616 | tf_op jit(solution)/shard_map/ppermute | solution.py:387
  16.0 0.0 all-to-all-done.rows0
  16.0 0.7 collective-permute-start.4
  16.7 1.2 %collective-permute-start.5 = (bf16[16,32,128]{2,1,0:T(8,128)(2,1)S(1)}, bf16[16,32,128]{2,1,0:T(8,128)(2,1)S(1)}, u32[]{:S(2)}, u32[]{:S(2)}) collective-permute-start(bf16[16,32,128]{2,1,0:T(8,128)(2,1)S(1)} %all-to-all-done.rows0), channel_id=1, source_target_pairs={{0,128},{4,132},{8,136},{12,140},{16,144},{20,148},{24,152},{28,15... | collective-permute-start | bytes 393224 | tf_op jit(solution)/shard_map/ppermute | solution.py:382
  17.9 0.7 collective-permute-start.6
  18.6 0.0 collective-permute-done.from_near.near
  18.6 0.7 collective-permute-done.1.from_far.far
  19.3 1.7 %collective-permute-start.2 = (bf16[10,32,128]{2,1,0:T(8,128)(2,1)S(1)}, bf16[10,32,128]{2,1,0:T(8,128)(2,1)S(1)}, u32[]{:S(2)}, u32[]{:S(2)}) collective-permute-start(bf16[10,32,128]{2,1,0:T(8,128)(2,1)S(1)} %get-tuple-element.39), channel_id=1, source_target_pairs={{0,4},{1,5},{2,6},{3,7},{4,0},{5,1},{6,2},{7,3},{8,12},{9,13},{10,... | collective-permute-start | bytes 245768 | tf_op jit(solution)/shard_map/ppermute | solution.py:390
  21.1 3.7 %collective-permute-start.3 = (bf16[10,32,128]{2,1,0:T(8,128)(2,1)S(1)}, bf16[10,32,128]{2,1,0:T(8,128)(2,1)S(1)}, u32[]{:S(2)}, u32[]{:S(2)}) collective-permute-start(bf16[10,32,128]{2,1,0:T(8,128)(2,1)S(1)} %get-tuple-element.40), channel_id=1, source_target_pairs={{0,1},{1,0},{2,3},{3,2},{4,8},{5,9},{6,10},{7,11},{8,4},{9,5},{10,... | collective-permute-start | bytes 245768 | tf_op jit(solution)/shard_map/ppermute | solution.py:390
  24.8 0.8 %copy.11 = s32[8,8,3]{2,1,0:T(8,128)S(1)} copy(s32[8,8,3]{1,0,2:T(8,128)} %param.12) | data formatting | bytes 1536 | tf_op args[3]
  25.6 0.1 reshape.15.neighbour
  25.7 0.0 collective-permute-done.2.mate
  25.7 11.1 %collective-permute-done.3.other = bf16[10,32,128]{2,1,0:T(8,128)(2,1)S(1)} collective-permute-done((bf16[10,32,128]{2,1,0:T(8,128)(2,1)S(1)}, bf16[10,32,128]{2,1,0:T(8,128)(2,1)S(1)}, u32[]{:S(2)}, u32[]{:S(2)}) %collective-permute-start.3) | collective-permute-done | bytes 81952 | tf_op jit(solution)/shard_map/ppermute | solution.py:390
  36.8 0.0 collective-permute-done.4.rows1
  36.8 0.0 collective-permute-done.5.rows2
  36.8 0.0 collective-permute-done.6.rows3
  36.8 7.3 %shard_map.94 = (bf16[64,32,128]{2,1,0:T(8,128)(2,1)S(1)}, f32[64,32,128]{2,1,0:T(8,128)S(1)}, bf16[64,3,128,128]{3,2,1,0:T(8,128)(2,1)S(1)}, bf16[64,128,128]{2...) custom-call(s32[192]{0:T(256)S(1)} %reshape.15.neighbour, ...), custom_call_target="tpu_custom_call" | custom-call | flops 268435456 | bytes 9437184 | tf_op jit(solution)/shard_map/pallas_call | solution.py:325
  44.2 0.5 collective-permute-start.7
  44.6 2.0 %collective-permute-start.8 = (bf16[8,32,128]{2,1,0:T(8,128)(2,1)S(1)}, bf16[8,32,128]{2,1,0:T(8,128)(2,1)S(1)}, u32[]{:S(2)}, u32[]{:S(2)}) collective-permute-start(bf16[8,32,128]{2,1,0:T(8,128)(2,1)S(1)} %get-tuple-element.48), channel_id=1, source_target_pairs={{0,4},{1,2},{2,1},{3,7},{4,0},{5,6},{6,5},{7,3},{8,12},{9,10},{10,... | collective-permute-start | bytes 196616 | tf_op jit(solution)/shard_map/ppermute | solution.py:360
  46.7 0.0 collective-permute-start.9
  46.7 3.1 %collective-permute-start.10 = (bf16[8,32,128]{2,1,0:T(8,128)(2,1)S(1)}, bf16[8,32,128]{2,1,0:T(8,128)(2,1)S(1)}, u32[]{:S(2)}, u32[]{:S(2)}) collective-permute-start(bf16[8,32,128]{2,1,0:T(8,128)(2,1)S(1)} %get-tuple-element.50), channel_id=1, source_target_pairs={{0,1},{1,0},{2,3},{3,2},{4,8},{5,9},{6,10},{7,11},{8,4},{9,5},{10,... | collective-permute-start | bytes 196616 | tf_op jit(solution)/shard_map/ppermute | solution.py:363
  49.8 2.3 %shard_map.95 = (bf16[64,32,128]{2,1,0:T(8,128)(2,1)S(1)}, bf16[100,32,128]{2,1,0:T(8,128)(2,1)S(1)}) custom-call(s32[192]{0:T(256)S(1)} %reshape.15.neighbour, bf16[64,32,128]{2,1,0:T(8,128)(2,1)S(1)} %get-tuple-element.41.refs_0_, f32[64,32,128]{2,1,0:T(8,128)S(1)} %get-tuple-element.42.refs_1_.rhs.refs_3_, ...), custom_call_target="tpu_custom_call" | custom-call | flops 268435456 | bytes 9437184 | tf_op jit(solution)/shard_map/pallas_call | solution.py:325
  52.1 0.0 collective-permute-done.7.near.from_near
  52.1 0.1 collective-permute-done.8.far.from_far
  52.3 0.1 collective-permute-start.11
  52.4 2.7 %collective-permute-start.12 = (bf16[2,32,128]{2,1,0:T(8,128)(2,1)S(1)}, bf16[2,32,128]{2,1,0:T(8,128)(2,1)S(1)}, u32[]{:S(2)}, u32[]{:S(2)}) collective-permute-start(bf16[2,32,128]{2,1,0:T(8,128)(2,1)S(1)} %get-tuple-element.54), channel_id=1, source_target_pairs={{0,1},{1,0},{2,3},{3,2},{4,8},{5,9},{6,10},{7,11},{8,4},{9,5},{10,... | collective-permute-start | bytes 49160 | tf_op jit(solution)/shard_map/ppermute | solution.py:368
  55.1 0.0 collective-permute-done.9.mate
  55.1 0.0 collective-permute-done.10.other
  55.1 1.8 %shard_map.96 = (bf16[64,32,128]{2,1,0:T(8,128)(2,1)S(1)}, bf16[100,32,128]{2,1,0:T(8,128)(2,1)S(1)}) custom-call(s32[192]{0:T(256)S(1)} %reshape.15.neighbour, bf16[100,32,128]{2,1,0:T(8,128)(2,1)S(1)} %get-tuple-element.46.local, bf16[8,32,128]{2,1,0:T(8,128)(2,1)S(1)} %collective-permute-done.7.near.from_near, ...), custom_call_target="tpu_custom_call" | custom-call | flops 268435456 | bytes 9437184 | tf_op jit(solution)/shard_map/pallas_call | solution.py:325
  56.9 0.0 collective-permute-done.11.mate
  56.9 2.5 %collective-permute-done.12.other = bf16[2,32,128]{2,1,0:T(8,128)(2,1)S(1)} collective-permute-done((bf16[2,32,128]{2,1,0:T(8,128)(2,1)S(1)}, bf16[2,32,128]{2,1,0:T(8,128)(2,1)S(1)}, u32[]{:S(2)}, u32[]{:S(2)}) %collective-permute-start.12) | collective-permute-done | bytes 16416 | tf_op jit(solution)/shard_map/ppermute | solution.py:368
  59.4 0.9 %shard_map.98 = (bf16[4,32,128]{2,1,0:T(8,128)(2,1)S(1)}, bf16[8,32,128]{2,1,0:T(8,128)(2,1)S(1)}, bf16[8,32,128]{2,1,0:T(8,128)(2,1)S(1)}, bf16[8,32,128]{2,1,0:T(8,128)(2,1)S(1)}, bf16[8,32,128]{2,1,0:T(8,128)(2,1)S(1)}) custom-call(s32[192]{0:T(256)S(1)} %reshape.15.neighbour, bf16[64,32,128]{2,1,0:T(8,128)(2,1)S(1)} %get-tuple-element.51.edges.refs_1_, ...), custom_call_target="tpu_custom_call" | custom-call | tf_op jit(solution)/shard_map/pallas_call | solution.py:325
  60.4 0.1 collective-permute-start.13
  60.5 3.4 %collective-permute-start.14 = (bf16[8,32,128]{2,1,0:T(8,128)(2,1)S(1)}, bf16[8,32,128]{2,1,0:T(8,128)(2,1)S(1)}, u32[]{:S(2)}, u32[]{:S(2)}) collective-permute-start(bf16[8,32,128]{2,1,0:T(8,128)(2,1)S(1)} %get-tuple-element.59), channel_id=1, source_target_pairs={{0,4},{1,2},{2,1},{3,7},{4,0},{5,6},{6,5},{7,3},{8,12},{9,10},{10,... | collective-permute-start | bytes 196616 | tf_op jit(solution)/shard_map/ppermute | solution.py:360
  63.9 0.0 collective-permute-start.15
  63.9 4.2 %collective-permute-start.16 = (bf16[8,32,128]{2,1,0:T(8,128)(2,1)S(1)}, bf16[8,32,128]{2,1,0:T(8,128)(2,1)S(1)}, u32[]{:S(2)}, u32[]{:S(2)}) collective-permute-start(bf16[8,32,128]{2,1,0:T(8,128)(2,1)S(1)} %get-tuple-element.61), channel_id=1, source_target_pairs={{0,1},{1,0},{2,3},{3,2},{4,8},{5,9},{6,10},{7,11},{8,4},{9,5},{10,... | collective-permute-start | bytes 196616 | tf_op jit(solution)/shard_map/ppermute | solution.py:363
  68.1 2.3 %shard_map.99 = (f32[64,32,128]{2,1,0:T(8,128)S(1)}, bf16[100,32,128]{2,1,0:T(8,128)(2,1)S(1)}) custom-call(s32[192]{0:T(256)S(1)} %reshape.15.neighbour, bf16[64,32,128]{2,1,0:T(8,128)(2,1)S(1)} %get-tuple-element.45.refs_0_, bf16[64,32,128]{2,1,0:T(8,128)(2,1)S(1)} %get-tuple-element.51.edges.refs_1_, bf16[4,32,128]{2,1,0:T(8,128)(2,1)S(1)} %get-tuple-element.55.refs_2_, ...), custom_call_target="tpu_custom_call" | custom-call | flops 268435456 | bytes 9437184 | tf_op jit(solution)/shard_map/pallas_call | solution.py:325
  70.4 0.0 collective-permute-done.13.near.from_near
  70.4 0.0 collective-permute-done.14.far.from_far
  70.5 0.1 collective-permute-start.17
  70.6 1.8 %collective-permute-start.18 = (bf16[2,32,128]{2,1,0:T(8,128)(2,1)S(1)}, bf16[2,32,128]{2,1,0:T(8,128)(2,1)S(1)}, u32[]{:S(2)}, u32[]{:S(2)}) collective-permute-start(bf16[2,32,128]{2,1,0:T(8,128)(2,1)S(1)} %get-tuple-element.65), channel_id=1, source_target_pairs={{0,1},{1,0},{2,3},{3,2},{4,8},{5,9},{6,10},{7,11},{8,4},{9,5},{10,... | collective-permute-start | bytes 49160 | tf_op jit(solution)/shard_map/ppermute | solution.py:368
  72.3 0.0 collective-permute-done.15.mate
  72.3 0.0 collective-permute-done.16.other
  72.3 3.4 %shard_map.100 = (f32[32,64,128]{2,1,0:T(8,128)}, f32[32,16,128]{2,1,0:T(8,128)S(1)}, bf16[100,32,128]{2,1,0:T(8,128)(2,1)S(1)}) custom-call(s32[192]{0:T(256)S(1)} %reshape.15.neighbour, bf16[100,32,128]{2,1,0:T(8,128)(2,1)S(1)} %get-tuple-element.56.local, f32[64,32,128]{2,1,0:T(8,128)S(1)} %get-tuple-element.57.interior, ...), custom_call_target="tpu_custom_call" | custom-call | flops 268435456 | bytes 9437184 | tf_op jit(solution)/shard_map/pallas_call | solution.py:325
  75.8 0.0 collective-permute-done.17.mate
  75.8 1.7 %collective-permute-done.18.other = bf16[2,32,128]{2,1,0:T(8,128)(2,1)S(1)} collective-permute-done((bf16[2,32,128]{2,1,0:T(8,128)(2,1)S(1)}, bf16[2,32,128]{2,1,0:T(8,128)(2,1)S(1)}, u32[]{:S(2)}, u32[]{:S(2)}) %collective-permute-start.18) | collective-permute-done | bytes 16416 | tf_op jit(solution)/shard_map/ppermute | solution.py:368
  77.5 1.6 %shard_map.102 = f32[32,64,128]{2,1,0:T(8,128)} custom-call(s32[192]{0:T(256)S(1)} %reshape.15.neighbour, f32[32,64,128]{2,1,0:T(8,128)} %get-tuple-element.62.partial, bf16[100,32,128]{2,1,0:T(8,128)(2,1)S(1)} %get-tuple-element.63.grid, bf16[2,32,128]{2,1,0:T(8,128)(2,1)S(1)} %collective-permute-done.17.mate, ...), custom_call_target="tpu_custom_call", output_to_operand_aliasing={{}: (1, {})} | custom-call | tf_op jit(solution)/shard_map/pallas_call | solution.py:325
  (3 shorter events, 0.1 us)
Async XLA Ops:
  1.4 14.6 %all-to-all-start = ((bf16[16,32,128]{2,1,0:T(8,128)(2,1)}), bf16[16,32,128]{2,1,0:T(8,128)(2,1)S(1)}, u32[]{:S(2)}, u32[]{:S(2)}) async-start(bf16[16,32,128]{2,1,0:T(8,128)(2,1)} %shard_map.93), calls=%async_computation | async-start | bytes 262144 | tf_op jit(solution)/shard_map/all_to_all | solution.py:380
  9.9 8.8 %collective-permute-start = (bf16[8,32,128]{2,1,0:T(8,128)(2,1)S(1)}, bf16[8,32,128]{2,1,0:T(8,128)(2,1)S(1)}, u32[]{:S(2)}, u32[]{:S(2)}) collective-permute-start(bf16[8,32,128]{2,1,0:T(8,128)(2,1)S(1)} %get-tuple-element.37), channel_id=1, source_target_pairs={{0,1},{1,0},{2,3},{3,2},{4,5},{5,4},{6,7},{7,6},{8,9},{9,8},{10,11... | collective-permute-start | bytes 196616 | tf_op jit(solution)/shard_map/ppermute | solution.py:388
  10.9 8.4 %collective-permute-start.1 = (bf16[8,32,128]{2,1,0:T(8,128)(2,1)S(1)}, bf16[8,32,128]{2,1,0:T(8,128)(2,1)S(1)}, u32[]{:S(2)}, u32[]{:S(2)}) collective-permute-start(bf16[8,32,128]{2,1,0:T(8,128)(2,1)S(1)} %get-tuple-element.38), channel_id=1, source_target_pairs={{0,4},{1,2},{2,1},{3,7},{4,0},{5,6},{6,5},{7,3},{8,12},{9,10},{10,... | collective-permute-start | bytes 196616 | tf_op jit(solution)/shard_map/ppermute | solution.py:387
  16.0 20.8 %collective-permute-start.4 = (bf16[16,32,128]{2,1,0:T(8,128)(2,1)S(1)}, bf16[16,32,128]{2,1,0:T(8,128)(2,1)S(1)}, u32[]{:S(2)}, u32[]{:S(2)}) collective-permute-start(bf16[16,32,128]{2,1,0:T(8,128)(2,1)S(1)} %all-to-all-done.rows0), channel_id=1, source_target_pairs={{0,64},{4,68},{8,72},{12,76},{16,80},{20,84},{24,88},{28,92},{32,9... | collective-permute-start | bytes 393224 | tf_op jit(solution)/shard_map/ppermute | solution.py:382
  16.7 20.1 %collective-permute-start.5 = (bf16[16,32,128]{2,1,0:T(8,128)(2,1)S(1)}, bf16[16,32,128]{2,1,0:T(8,128)(2,1)S(1)}, u32[]{:S(2)}, u32[]{:S(2)}) collective-permute-start(bf16[16,32,128]{2,1,0:T(8,128)(2,1)S(1)} %all-to-all-done.rows0), channel_id=1, source_target_pairs={{0,128},{4,132},{8,136},{12,140},{16,144},{20,148},{24,152},{28,15... | collective-permute-start | bytes 393224 | tf_op jit(solution)/shard_map/ppermute | solution.py:382
  17.9 18.9 %collective-permute-start.6 = (bf16[16,32,128]{2,1,0:T(8,128)(2,1)S(1)}, bf16[16,32,128]{2,1,0:T(8,128)(2,1)S(1)}, u32[]{:S(2)}, u32[]{:S(2)}) collective-permute-start(bf16[16,32,128]{2,1,0:T(8,128)(2,1)S(1)} %all-to-all-done.rows0), channel_id=1, source_target_pairs={{0,192},{4,196},{8,200},{12,204},{16,208},{20,212},{24,216},{28,22... | collective-permute-start | bytes 393224 | tf_op jit(solution)/shard_map/ppermute | solution.py:382
  19.3 6.4 %collective-permute-start.2 = (bf16[10,32,128]{2,1,0:T(8,128)(2,1)S(1)}, bf16[10,32,128]{2,1,0:T(8,128)(2,1)S(1)}, u32[]{:S(2)}, u32[]{:S(2)}) collective-permute-start(bf16[10,32,128]{2,1,0:T(8,128)(2,1)S(1)} %get-tuple-element.39), channel_id=1, source_target_pairs={{0,4},{1,5},{2,6},{3,7},{4,0},{5,1},{6,2},{7,3},{8,12},{9,13},{10,... | collective-permute-start | bytes 245768 | tf_op jit(solution)/shard_map/ppermute | solution.py:390
  21.1 15.8 %collective-permute-start.3 = (bf16[10,32,128]{2,1,0:T(8,128)(2,1)S(1)}, bf16[10,32,128]{2,1,0:T(8,128)(2,1)S(1)}, u32[]{:S(2)}, u32[]{:S(2)}) collective-permute-start(bf16[10,32,128]{2,1,0:T(8,128)(2,1)S(1)} %get-tuple-element.40), channel_id=1, source_target_pairs={{0,1},{1,0},{2,3},{3,2},{4,8},{5,9},{6,10},{7,11},{8,4},{9,5},{10,... | collective-permute-start | bytes 245768 | tf_op jit(solution)/shard_map/ppermute | solution.py:390
  44.2 8.0 %collective-permute-start.7 = (bf16[8,32,128]{2,1,0:T(8,128)(2,1)S(1)}, bf16[8,32,128]{2,1,0:T(8,128)(2,1)S(1)}, u32[]{:S(2)}, u32[]{:S(2)}) collective-permute-start(bf16[8,32,128]{2,1,0:T(8,128)(2,1)S(1)} %get-tuple-element.47), channel_id=1, source_target_pairs={{0,1},{1,0},{2,3},{3,2},{4,5},{5,4},{6,7},{7,6},{8,9},{9,8},{10,11... | collective-permute-start | bytes 196616 | tf_op jit(solution)/shard_map/ppermute | solution.py:361
  44.6 7.6 %collective-permute-start.8 = (bf16[8,32,128]{2,1,0:T(8,128)(2,1)S(1)}, bf16[8,32,128]{2,1,0:T(8,128)(2,1)S(1)}, u32[]{:S(2)}, u32[]{:S(2)}) collective-permute-start(bf16[8,32,128]{2,1,0:T(8,128)(2,1)S(1)} %get-tuple-element.48), channel_id=1, source_target_pairs={{0,4},{1,2},{2,1},{3,7},{4,0},{5,6},{6,5},{7,3},{8,12},{9,10},{10,... | collective-permute-start | bytes 196616 | tf_op jit(solution)/shard_map/ppermute | solution.py:360
  46.7 8.4 %collective-permute-start.9 = (bf16[8,32,128]{2,1,0:T(8,128)(2,1)S(1)}, bf16[8,32,128]{2,1,0:T(8,128)(2,1)S(1)}, u32[]{:S(2)}, u32[]{:S(2)}) collective-permute-start(bf16[8,32,128]{2,1,0:T(8,128)(2,1)S(1)} %get-tuple-element.49), channel_id=1, source_target_pairs={{0,4},{1,5},{2,6},{3,7},{4,0},{5,1},{6,2},{7,3},{8,12},{9,13},{10,... | collective-permute-start | bytes 196616 | tf_op jit(solution)/shard_map/ppermute | solution.py:362
  46.7 8.4 %collective-permute-start.10 = (bf16[8,32,128]{2,1,0:T(8,128)(2,1)S(1)}, bf16[8,32,128]{2,1,0:T(8,128)(2,1)S(1)}, u32[]{:S(2)}, u32[]{:S(2)}) collective-permute-start(bf16[8,32,128]{2,1,0:T(8,128)(2,1)S(1)} %get-tuple-element.50), channel_id=1, source_target_pairs={{0,1},{1,0},{2,3},{3,2},{4,8},{5,9},{6,10},{7,11},{8,4},{9,5},{10,... | collective-permute-start | bytes 196616 | tf_op jit(solution)/shard_map/ppermute | solution.py:363
  52.3 4.7 %collective-permute-start.11 = (bf16[2,32,128]{2,1,0:T(8,128)(2,1)S(1)}, bf16[2,32,128]{2,1,0:T(8,128)(2,1)S(1)}, u32[]{:S(2)}, u32[]{:S(2)}) collective-permute-start(bf16[2,32,128]{2,1,0:T(8,128)(2,1)S(1)} %get-tuple-element.53), channel_id=1, source_target_pairs={{0,4},{1,5},{2,6},{3,7},{4,0},{5,1},{6,2},{7,3},{8,12},{9,13},{10,... | collective-permute-start | bytes 49160 | tf_op jit(solution)/shard_map/ppermute | solution.py:368
  52.4 7.1 %collective-permute-start.12 = (bf16[2,32,128]{2,1,0:T(8,128)(2,1)S(1)}, bf16[2,32,128]{2,1,0:T(8,128)(2,1)S(1)}, u32[]{:S(2)}, u32[]{:S(2)}) collective-permute-start(bf16[2,32,128]{2,1,0:T(8,128)(2,1)S(1)} %get-tuple-element.54), channel_id=1, source_target_pairs={{0,1},{1,0},{2,3},{3,2},{4,8},{5,9},{6,10},{7,11},{8,4},{9,5},{10,... | collective-permute-start | bytes 49160 | tf_op jit(solution)/shard_map/ppermute | solution.py:368
  60.4 10.1 %collective-permute-start.13 = (bf16[8,32,128]{2,1,0:T(8,128)(2,1)S(1)}, bf16[8,32,128]{2,1,0:T(8,128)(2,1)S(1)}, u32[]{:S(2)}, u32[]{:S(2)}) collective-permute-start(bf16[8,32,128]{2,1,0:T(8,128)(2,1)S(1)} %get-tuple-element.58), channel_id=1, source_target_pairs={{0,1},{1,0},{2,3},{3,2},{4,5},{5,4},{6,7},{7,6},{8,9},{9,8},{10,11... | collective-permute-start | bytes 196616 | tf_op jit(solution)/shard_map/ppermute | solution.py:361
  60.5 10.0 %collective-permute-start.14 = (bf16[8,32,128]{2,1,0:T(8,128)(2,1)S(1)}, bf16[8,32,128]{2,1,0:T(8,128)(2,1)S(1)}, u32[]{:S(2)}, u32[]{:S(2)}) collective-permute-start(bf16[8,32,128]{2,1,0:T(8,128)(2,1)S(1)} %get-tuple-element.59), channel_id=1, source_target_pairs={{0,4},{1,2},{2,1},{3,7},{4,0},{5,6},{6,5},{7,3},{8,12},{9,10},{10,... | collective-permute-start | bytes 196616 | tf_op jit(solution)/shard_map/ppermute | solution.py:360
  63.9 8.4 %collective-permute-start.15 = (bf16[8,32,128]{2,1,0:T(8,128)(2,1)S(1)}, bf16[8,32,128]{2,1,0:T(8,128)(2,1)S(1)}, u32[]{:S(2)}, u32[]{:S(2)}) collective-permute-start(bf16[8,32,128]{2,1,0:T(8,128)(2,1)S(1)} %get-tuple-element.60), channel_id=1, source_target_pairs={{0,4},{1,5},{2,6},{3,7},{4,0},{5,1},{6,2},{7,3},{8,12},{9,13},{10,... | collective-permute-start | bytes 196616 | tf_op jit(solution)/shard_map/ppermute | solution.py:362
  63.9 8.4 %collective-permute-start.16 = (bf16[8,32,128]{2,1,0:T(8,128)(2,1)S(1)}, bf16[8,32,128]{2,1,0:T(8,128)(2,1)S(1)}, u32[]{:S(2)}, u32[]{:S(2)}) collective-permute-start(bf16[8,32,128]{2,1,0:T(8,128)(2,1)S(1)} %get-tuple-element.61), channel_id=1, source_target_pairs={{0,1},{1,0},{2,3},{3,2},{4,8},{5,9},{6,10},{7,11},{8,4},{9,5},{10,... | collective-permute-start | bytes 196616 | tf_op jit(solution)/shard_map/ppermute | solution.py:363
  70.5 5.3 %collective-permute-start.17 = (bf16[2,32,128]{2,1,0:T(8,128)(2,1)S(1)}, bf16[2,32,128]{2,1,0:T(8,128)(2,1)S(1)}, u32[]{:S(2)}, u32[]{:S(2)}) collective-permute-start(bf16[2,32,128]{2,1,0:T(8,128)(2,1)S(1)} %get-tuple-element.64), channel_id=1, source_target_pairs={{0,4},{1,5},{2,6},{3,7},{4,0},{5,1},{6,2},{7,3},{8,12},{9,13},{10,... | collective-permute-start | bytes 49160 | tf_op jit(solution)/shard_map/ppermute | solution.py:368
  70.6 6.9 %collective-permute-start.18 = (bf16[2,32,128]{2,1,0:T(8,128)(2,1)S(1)}, bf16[2,32,128]{2,1,0:T(8,128)(2,1)S(1)}, u32[]{:S(2)}, u32[]{:S(2)}) collective-permute-start(bf16[2,32,128]{2,1,0:T(8,128)(2,1)S(1)} %get-tuple-element.65), channel_id=1, source_target_pairs={{0,1},{1,0},{2,3},{3,2},{4,8},{5,9},{6,10},{7,11},{8,4},{9,5},{10,... | collective-permute-start | bytes 49160 | tf_op jit(solution)/shard_map/ppermute | solution.py:368

commit v4 on v3

--- a/solution.py
+++ b/solution.py
@@ -14,7 +14,6 @@
 CORNER_HALOS = (0, 9, 90, 99)
 INTERIOR = tuple(b for b in range(64) if 0 < b // 8 < 7 and 0 < b % 8 < 7)
 EDGES = tuple(b for b in range(64) if b not in INTERIOR and b not in CORNERS)
-PLANE = 16
 
 dot_t = functools.partial(
     lax.dot_general,
@@ -68,13 +67,17 @@
     return copies
 
 
-def spread(stream, everyone, held, sem):
+def spread(stream, row, held, sem):
     copy = pltpu.make_async_copy(stream, held, sem)
     copy.start()
     copy.wait()
-    row = held[0].astype(BF16)
-    for t in range(PLANE):
-        everyone[t] = row
+    row[...] = held[...].astype(BF16)
+
+
+def join(part0, part1, part2, part3, whole):
+    count = part0.shape[0]
+    for m, part in enumerate((part0, part1, part2, part3)):
+        whole[pl.ds(m * count, count)] = part[...]
 
 
 def prepare(old, x, to_near, to_far, held, sems):
@@ -152,17 +155,17 @@
     return lambda b: jnp.concatenate([grid[neighbour[3 * b + k]] for k in range(3)], axis=1)
 
 
-def row_of(well, near_rows):
-    away = (well // PLANE) ^ (lax.axis_index("tile") // PLANE)
-    row = near_rows[0][well % PLANE]
+def row_of(well, parts):
+    away = well ^ lax.axis_index("tile")
+    place = (away // 4) % 4 * 4 + away // 16
+    row = parts[0][place]
     for m in range(1, 4):
-        row = jnp.where(away == m, near_rows[m][well % PLANE], row)
+        row = jnp.where(away % 4 == m, parts[m][place], row)
     return row.astype(F32)
 
 
 def sweep_first(
-    neighbour, well, row, where, rate, x, near, far, mate, other, rows0, rows1, rows2, rows3, old, upwind_far, diag_far,
-    x_next, rhs, upwind, diag, to_near, to_far, to_mate, to_other, grid, held, old_sems, sems,
+    neighbour, x, near, far, mate, other, old, upwind_far, diag_far, x_next, rhs, upwind, diag, grid, held, old_sems, sems
 ):
     old_copies = bring_old(old, held, old_sems)
     copies = []
@@ -179,8 +182,8 @@
         for copy in copies[r]:
             copy.start()
 
-    start(0)
-    start(1)
+    for r in range(4):
+        start(r)
     widen(grid, near, far, mate, other)
     for b in range(64):
         grid[at(b)] = x[b]
@@ -189,22 +192,35 @@
         old_copies[r].wait()
         for b in range(8 * r, 8 * r + 8):
             rhs[b] = old_rows[pl.ds(b, 32, stride=64), :]
-    for p in range(4):
-        b = where[0, 0, p]
-        rhs[b] = rhs[b] + rate[0, 0, p] * row_of(row[well[0, 0, p]], (rows0, rows1, rows2, rows3))
 
     def store(b, conc):
         x_next[b] = conc.astype(BF16)
 
     upstream = from_grid(neighbour, grid)
     for r in range(0, 8, 2):
-        for ahead in (r + 2, r + 3):
+        for ahead in (r + 4, r + 5):
             if ahead < 8:
                 start(ahead)
         for copy in copies[r] + copies[r + 1]:
             copy.wait()
         sweep(range(8 * r, 8 * r + 16), upstream, rhs, upwind, diag, store)
-    send_edges(lambda b: x_next[b], to_near, to_far, to_mate, to_other)
+
+
+def inject(
+    neighbour, well, row, where, rate, rows0, rows1, rows2, rows3, x_in, rhs_in, grid, upwind, diag,
+    x, rhs, to_near, to_far, to_mate, to_other,
+):
+    x[...] = x_in[...]
+    rhs[...] = rhs_in[...]
+    for p in range(4):
+        b = where[0, 0, p]
+        rhs[b] = rhs[b] + rate[0, 0, p] * row_of(row[well[0, 0, p]], (rows0, rows1, rows2, rows3))
+
+    def store(b, conc):
+        x[b] = conc.astype(BF16)
+
+    sweep([where[0, 0, p] for p in range(4)], from_grid(neighbour, grid), rhs, upwind, diag, store)
+    send_edges(lambda b: x[b], to_near, to_far, to_mate, to_other)
 
 
 def fill(grid, parts):
@@ -266,44 +282,39 @@
     send_edges(block, to_near, to_far, to_mate, to_other)
 
 
-def middle_last(
-    neighbour, local, interior, near, far, mate, other, rhs, upwind, diag, out, ends, grid, held, sems
-):
+def middle_last(neighbour, local, interior, near, far, mate, other, rhs, upwind, diag, out, grid, held, sems):
+    copies = []
+
+    def send(block, b):
+        copies.append(pltpu.make_async_copy(block, out.at[:, b], sems.at[b]))
+        copies[-1].start()
+
+    for b in INTERIOR:
+        send(interior.at[b], b)
     for b in range(64):
         grid[at(b)] = local[at(b)]
     widen(grid, near, far, mate, other)
-    rows = held.reshape(32 * 64, 128)
-
-    def store(b, conc):
-        rows[pl.ds(b, 32, stride=64), :] = conc
+
+    def store(b, conc):
+        held[EDGES.index(b)] = conc
 
     sweep(EDGES, from_grid(neighbour, grid), rhs, upwind, diag, store)
-    for b in INTERIOR:
-        store(b, interior[b])
-    copies = []
-    for r in range(1, 7):
-        part = pl.ds(8 * r, 8)
-        copies.append(pltpu.make_async_copy(held.at[:, part], out.at[:, part], sems.at[r]))
-        copies[-1].start()
-    for i, r in enumerate((0, 7)):
-        ends[:, pl.ds(8 * i, 8)] = held[:, pl.ds(8 * r, 8)]
+    for i, b in enumerate(EDGES):
+        send(held.at[i], b)
     for copy in copies:
         copy.wait()
 
 
-def outer_last(neighbour, partial, grid, mate, other, rhs, upwind, diag, ends, out, held, sems):
+def outer_last(neighbour, partial, grid, mate, other, rhs, upwind, diag, out, held, sems):
     del partial
-    held[...] = ends[...]
-    rows = held.reshape(32 * 16, 128)
-
-    def store(b, conc):
-        rows[pl.ds(b if b < 8 else b - 48, 32, stride=16), :] = conc
+
+    def store(b, conc):
+        held[CORNERS.index(b)] = conc
 
     sweep_corners(neighbour, grid, mate, other, rhs, upwind, diag, store)
-    copies = []
-    for i, r in enumerate((0, 7)):
-        copies.append(pltpu.make_async_copy(held.at[:, pl.ds(8 * i, 8)], out.at[:, pl.ds(8 * r, 8)], sems.at[i]))
-        copies[-1].start()
+    copies = [pltpu.make_async_copy(held.at[i], out.at[:, b], sems.at[i]) for i, b in enumerate(CORNERS)]
+    for copy in copies:
+        copy.start()
     for copy in copies:
         copy.wait()
 
@@ -321,7 +332,13 @@
         if where in (HBM, SMEM_FROM_HBM):
             value = pltpu.with_memory_space_constraint(value, pltpu.HBM)
         values.append(value)
-    shapes = [pltpu.VMEM(s.shape, s.dtype) if where is VMEM else s for where, s in outs]
+    shapes = []
+    for where, s in outs:
+        if where is VMEM:
+            s = pltpu.VMEM(s.shape, s.dtype)
+        if where is HBM:
+            s = pltpu.HBM(s.shape, s.dtype)
+        shapes.append(s)
     return pl.pallas_call(
         kernel,
         out_shape=shapes,
@@ -375,11 +392,13 @@
     old = (HBM, old_conc.reshape(32, 64, 128))
     work = dict(flops=2 * 64 * 4 * 32 * 128 * 128, moved=9 * 2**20)
 
-    (everyone,) = call(spread, [blocks(PLANE)], [(HBM, streams)], [pltpu.VMEM((1, 32, 128), F32), dma(())])
-    planes = [list(range(z, z + PLANE)) for z in range(0, tiles, PLANE)]
-    rows = [lax.all_to_all(everyone, "tile", 0, 0, axis_index_groups=planes)]
-    for m in (1, 2, 3):
-        rows.append(lax.ppermute(rows[0], "tile", [(t, t ^ (m * PLANE)) for t in range(tiles)]))
+    def swaps(part, step):
+        return [part] + [lax.ppermute(part, "tile", [(t, t ^ (m * step)) for t in range(tiles)]) for m in (1, 2, 3)]
+
+    (part,) = call(spread, [blocks(1)], [(HBM, streams)], [pltpu.VMEM((1, 32, 128), F32), dma(())])
+    for step in (16, 4):
+        (part,) = call(join, [blocks(4 * part.shape[0])], vmem(*swaps(part, step)))
+    rows = swaps(part, 1)
 
     x, to_near, to_far = call(
         prepare, [blocks(64), blocks(8), blocks(8)], [old], [held, dma((8,))], moved=4 * 2**20
@@ -392,15 +411,19 @@
     upwind_shape = jax.ShapeDtypeStruct((64, 3, 128, 128), BF16)
     diag_shape = jax.ShapeDtypeStruct((64, 128, 128), BF16)
     wells = [(SMEM_FROM_HBM, v) for v in (perf_well, injector_row, perf_block, perf_rate)]
-    x, rhs, *rest = call(
+    x, rhs, *weights, whole_grid = call(
         sweep_first,
-        [blocks(64), blocks(64, F32), (VMEM, upwind_shape), (VMEM, diag_shape), *edges],
-        [neighbour, *wells, *vmem(x, *got, *rows), old]
+        [blocks(64), blocks(64, F32), (VMEM, upwind_shape), (VMEM, diag_shape), blocks(100)],
+        [neighbour, *vmem(x, *got), old]
         + [(HBM, upwind.reshape(upwind_shape.shape)), (HBM, diag_inverse.reshape(diag_shape.shape))],
-        [grid, held, dma((8,)), dma((16,))],
+        [held, dma((8,)), dma((16,))],
         **work,
     )
-    weights, sent = rest[:2], rest[2:]
+    x, rhs, *sent = call(
+        inject,
+        [blocks(64), blocks(64, F32), *edges],
+        [neighbour, *wells, *vmem(*rows, x, rhs, whole_grid, *weights)],
+    )
     parts = [x]
     for last in (False, True):
         got = exchange(*sent)
@@ -421,18 +444,18 @@
         )
         parts = [interior, edge_blocks, corners]
     whole = (ANY, jax.ShapeDtypeStruct((32, 64, 128), F32))
-    partial, border, whole_grid = call(
+    partial, whole_grid = call(
         middle_last,
-        [whole, (VMEM, jax.ShapeDtypeStruct((32, 16, 128), F32)), blocks(100)],
+        [whole, blocks(100)],
         [neighbour, *vmem(local, interior, *got, rhs, *weights)],
-        [held, dma((8,))],
+        [pltpu.VMEM((24, 32, 128), F32), dma((64,))],
         **work,
     )
     (out,) = call(
         outer_last,
         [whole],
-        [neighbour, (ANY, partial), *vmem(whole_grid, *ends, rhs, *weights, border)],
-        [pltpu.VMEM((32, 16, 128), F32), pltpu.SemaphoreType.DMA((2,))],
+        [neighbour, (ANY, partial), *vmem(whole_grid, *ends, rhs, *weights)],
+        [pltpu.VMEM((4, 32, 128), F32), dma((4,))],
         {1: 0},
     )
     return out.reshape(old_conc.shape)

time: 79.6 us -> 81.2 us (1.020)
  the two profiles are of different devices: /device:TPU:65 before, /device:TPU:33 now
where the time goes in v4:
time: 81.2 us; the launch traced here: 80.9 us
  starting transfers between devices  44.1 us (54%)
  Pallas kernels  22.4 us (28%)
  waiting for transfers between devices  13 us (16%)
  local copies, waits for them, and re-layouts  0.95 us (1%)
    pallas_call x15, Pallas kernels, call(): pl.pallas_call(kernel, out_shape=shapes, in_specs=[SMEM if where is SMEM_...  22.4 us
    ppermute x9, starting transfers between devices, swaps(): lax.ppermute(part, 'tile', [(t, t ^ m * step) for t in range(tiles)])  10.6 us
    ppermute x2, starting transfers between devices, exchange(): from_other = lax.ppermute(to_other, both, others)  8.77 us
    ppermute x2, starting transfers between devices, exchange(): from_far = lax.ppermute(to_far, both, far_pairs)  7.2 us
    ppermute x1, starting transfers between devices, body(): from_far = lax.ppermute(to_far, both, far_pairs)  6 us
    ppermute x9, waiting for transfers between devices, swaps(): lax.ppermute(part, 'tile', [(t, t ^ m * step) for t in range(tiles)])  5.75 us
    ppermute x2, waiting for transfers between devices, exchange_corners(): lax.ppermute(to_other, both, others)  5.19 us
    ppermute x1, starting transfers between devices, body(): lax.ppermute(to_other, both, others)  4.64 us
  transfers between devices with their start and end apart: 25, of which 7 were waited for; matrix products, arithmetic and copies ran while one was open for 1% of the time, Pallas kernels for 21%

profile of v4, /device:TPU:33, one launch (start us, length us, event | category | flops | bytes accessed | tf_op | source)
XLA Modules:
  0.0 80.9 jit_solution(17607668680162455254)
XLA Ops:
  0.0 1.7 %shard_map.94 = (bf16[64,32,128]{2,1,0:T(8,128)(2,1)S(1)}, bf16[8,32,128]{2,1,0:T(8,128)(2,1)S(1)}, bf16[8,32,128]{2,1,0:T(8,128)(2,1)S(1)}) custom-call(f32[32,64,128]{2,1,0:T(8,128)} %bitcast.5), custom_call_target="tpu_custom_call" | custom-call | bytes 4194304 | tf_op jit(solution)/shard_map/pallas_call | solution.py:342
  1.7 0.8 collective-permute-start.9
  2.4 6.0 %collective-permute-start.10 = (bf16[8,32,128]{2,1,0:T(8,128)(2,1)S(1)}, bf16[8,32,128]{2,1,0:T(8,128)(2,1)S(1)}, u32[]{:S(2)}, u32[]{:S(2)}) collective-permute-start(bf16[8,32,128]{2,1,0:T(8,128)(2,1)S(1)} %get-tuple-element.40), channel_id=1, source_target_pairs={{0,4},{1,2},{2,1},{3,7},{4,0},{5,6},{6,5},{7,3},{8,12},{9,10},{10,... | collective-permute-start | bytes 196616 | tf_op jit(solution)/shard_map/ppermute | solution.py:406
  8.4 0.7 shard_map.91.part0
  9.2 0.8 %collective-permute-start = (bf16[1,32,128]{2,1,0:T(8,128)(2,1)S(1)}, bf16[1,32,128]{2,1,0:T(8,128)(2,1)S(1)}, u32[]{:S(2)}, u32[]{:S(2)}) collective-permute-start(bf16[1,32,128]{2,1,0:T(8,128)(2,1)S(1)} %shard_map.91.part0), channel_id=1, source_target_pairs={{0,64},{4,68},{8,72},{12,76},{16,80},{20,84},{24,88},{28,92},{32,9... | collective-permute-start | bytes 24584 | tf_op jit(solution)/shard_map/ppermute | solution.py:396
  10.0 1.2 %collective-permute-start.1 = (bf16[1,32,128]{2,1,0:T(8,128)(2,1)S(1)}, bf16[1,32,128]{2,1,0:T(8,128)(2,1)S(1)}, u32[]{:S(2)}, u32[]{:S(2)}) collective-permute-start(bf16[1,32,128]{2,1,0:T(8,128)(2,1)S(1)} %shard_map.91.part0), channel_id=1, source_target_pairs={{0,128},{4,132},{8,136},{12,140},{16,144},{20,148},{24,152},{28,15... | collective-permute-start | bytes 24584 | tf_op jit(solution)/shard_map/ppermute | solution.py:396
  11.2 0.7 collective-permute-start.2
  11.9 0.0 collective-permute-done.part1
  11.9 1.5 %collective-permute-done.1.part2 = bf16[1,32,128]{2,1,0:T(8,128)(2,1)S(1)} collective-permute-done((bf16[1,32,128]{2,1,0:T(8,128)(2,1)S(1)}, bf16[1,32,128]{2,1,0:T(8,128)(2,1)S(1)}, u32[]{:S(2)}, u32[]{:S(2)}) %collective-permute-start.1) | collective-permute-done | bytes 8224 | tf_op jit(solution)/shard_map/ppermute | solution.py:396
  13.4 0.3 collective-permute-done.2.part3
  13.7 1.3 %collective-permute-start.3 = (bf16[4,32,128]{2,1,0:T(8,128)(2,1)S(1)}, bf16[4,32,128]{2,1,0:T(8,128)(2,1)S(1)}, u32[]{:S(2)}, u32[]{:S(2)}) collective-permute-start(bf16[4,32,128]{2,1,0:T(8,128)(2,1)S(1)} %shard_map.92.part0), channel_id=1, source_target_pairs={{0,16},{4,20},{8,24},{12,28},{16,0},{20,4},{24,8},{28,12},{32,48},... | collective-permute-start | bytes 98312 | tf_op jit(solution)/shard_map/ppermute | solution.py:396
  15.0 2.6 %collective-permute-start.4 = (bf16[4,32,128]{2,1,0:T(8,128)(2,1)S(1)}, bf16[4,32,128]{2,1,0:T(8,128)(2,1)S(1)}, u32[]{:S(2)}, u32[]{:S(2)}) collective-permute-start(bf16[4,32,128]{2,1,0:T(8,128)(2,1)S(1)} %shard_map.92.part0), channel_id=1, source_target_pairs={{0,32},{4,36},{8,40},{12,44},{16,48},{20,52},{24,56},{28,60},{32,0... | collective-permute-start | bytes 98312 | tf_op jit(solution)/shard_map/ppermute | solution.py:396
  17.6 0.0 collective-permute-start.5
  17.6 0.0 collective-permute-done.3.part1
  17.6 1.6 %collective-permute-done.4.part2 = bf16[4,32,128]{2,1,0:T(8,128)(2,1)S(1)} collective-permute-done((bf16[4,32,128]{2,1,0:T(8,128)(2,1)S(1)}, bf16[4,32,128]{2,1,0:T(8,128)(2,1)S(1)}, u32[]{:S(2)}, u32[]{:S(2)}) %collective-permute-start.4) | collective-permute-done | bytes 32800 | tf_op jit(solution)/shard_map/ppermute | solution.py:396
  19.3 2.3 %collective-permute-done.5.part3 = bf16[4,32,128]{2,1,0:T(8,128)(2,1)S(1)} collective-permute-done((bf16[4,32,128]{2,1,0:T(8,128)(2,1)S(1)}, bf16[4,32,128]{2,1,0:T(8,128)(2,1)S(1)}, u32[]{:S(2)}, u32[]{:S(2)}) %collective-permute-start.5) | collective-permute-done | bytes 32800 | tf_op jit(solution)/shard_map/ppermute | solution.py:396
  21.6 1.3 %collective-permute-start.6 = (bf16[16,32,128]{2,1,0:T(8,128)(2,1)S(1)}, bf16[16,32,128]{2,1,0:T(8,128)(2,1)S(1)}, u32[]{:S(2)}, u32[]{:S(2)}) collective-permute-start(bf16[16,32,128]{2,1,0:T(8,128)(2,1)S(1)} %shard_map.93.rows0), channel_id=1, source_target_pairs={{0,4},{4,0},{8,12},{12,8},{16,20},{20,16},{24,28},{28,24},{32,36},... | collective-permute-start | bytes 393224 | tf_op jit(solution)/shard_map/ppermute | solution.py:396
  22.9 2.5 %collective-permute-start.7 = (bf16[16,32,128]{2,1,0:T(8,128)(2,1)S(1)}, bf16[16,32,128]{2,1,0:T(8,128)(2,1)S(1)}, u32[]{:S(2)}, u32[]{:S(2)}) collective-permute-start(bf16[16,32,128]{2,1,0:T(8,128)(2,1)S(1)} %shard_map.93.rows0), channel_id=1, source_target_pairs={{0,8},{4,12},{8,0},{12,4},{16,24},{20,28},{24,16},{28,20},{32,40},... | collective-permute-start | bytes 393224 | tf_op jit(solution)/shard_map/ppermute | solution.py:396
  25.3 0.2 collective-permute-start.8
  25.6 0.0 collective-permute-done.9.from_near.near
  25.6 0.0 collective-permute-done.10.from_far.far
  25.6 0.1 collective-permute-start.11
  25.7 4.6 %collective-permute-start.12 = (bf16[10,32,128]{2,1,0:T(8,128)(2,1)S(1)}, bf16[10,32,128]{2,1,0:T(8,128)(2,1)S(1)}, u32[]{:S(2)}, u32[]{:S(2)}) collective-permute-start(bf16[10,32,128]{2,1,0:T(8,128)(2,1)S(1)} %get-tuple-element.42), channel_id=1, source_target_pairs={{0,1},{1,0},{2,3},{3,2},{4,8},{5,9},{6,10},{7,11},{8,4},{9,5},{10,... | collective-permute-start | bytes 245768 | tf_op jit(solution)/shard_map/ppermute | solution.py:409
  30.4 0.8 %copy.11 = s32[8,8,3]{2,1,0:T(8,128)S(1)} copy(s32[8,8,3]{1,0,2:T(8,128)} %param.12) | data formatting | bytes 1536 | tf_op args[3]
  31.2 0.1 reshape.15.neighbour
  31.3 0.0 collective-permute-done.11.mate
  31.4 2.0 %collective-permute-done.12.other = bf16[10,32,128]{2,1,0:T(8,128)(2,1)S(1)} collective-permute-done((bf16[10,32,128]{2,1,0:T(8,128)(2,1)S(1)}, bf16[10,32,128]{2,1,0:T(8,128)(2,1)S(1)}, u32[]{:S(2)}, u32[]{:S(2)}) %collective-permute-start.12) | collective-permute-done | bytes 81952 | tf_op jit(solution)/shard_map/ppermute | solution.py:409
  33.4 6.7 %shard_map.96 = (bf16[64,32,128]{2,1,0:T(8,128)(2,1)S(1)}, f32[64,32,128]{2,1,0:T(8,128)S(1)}, bf16[64,3,128,128]{3,2,1,0:T(8,128)(2,1)S(1)}, bf16[64,128,128]{2,1,0:T(8,128)(2,1)S(1)}, bf16[100,32,128]{2,1,0:T(8,128)(2,1)S(1)}) custom-call(s32[192]{0:T(256)S(1)} %reshape.15.neighbour, bf16[64,32,128]{2,1,0:T(8,128)(2,1)S(1)} %get-tuple-element.38.x, ...), custom_call_target="tpu_custom_call" | custom-call | flops 268435456 | bytes 9437184 | tf_op jit(solution)/shard_map/pallas_call | solution.py:342
  40.0 0.0 collective-permute-done.6.rows1
  40.0 0.0 collective-permute-done.7.rows2
  40.1 0.0 collective-permute-done.8.rows3
  40.1 1.2 %shard_map.97 = (bf16[64,32,128]{2,1,0:T(8,128)(2,1)S(1)}, f32[64,32,128]{2,1,0:T(8,128)S(1)}, bf16[8,32,128]{2,1,0:T(8,128)(2,1)S(1)}, bf16[8,32,128]{2,1,0:T(8...) custom-call(s32[192]{0:T(256)S(1)} %reshape.15.neighbour, s32[1,1,4]{2,1,0:T(1,128)} %well.1, ...), custom_call_target="tpu_custom_call" | custom-call | tf_op jit(solution)/shard_map/pallas_call | solution.py:342
  41.2 2.1 %collective-permute-start.13 = (bf16[8,32,128]{2,1,0:T(8,128)(2,1)S(1)}, bf16[8,32,128]{2,1,0:T(8,128)(2,1)S(1)}, u32[]{:S(2)}, u32[]{:S(2)}) collective-permute-start(bf16[8,32,128]{2,1,0:T(8,128)(2,1)S(1)} %get-tuple-element.52), channel_id=1, source_target_pairs={{0,1},{1,0},{2,3},{3,2},{4,5},{5,4},{6,7},{7,6},{8,9},{9,8},{10,11... | collective-permute-start | bytes 196616 | tf_op jit(solution)/shard_map/ppermute | solution.py:378
  43.4 4.6 %collective-permute-start.14 = (bf16[8,32,128]{2,1,0:T(8,128)(2,1)S(1)}, bf16[8,32,128]{2,1,0:T(8,128)(2,1)S(1)}, u32[]{:S(2)}, u32[]{:S(2)}) collective-permute-start(bf16[8,32,128]{2,1,0:T(8,128)(2,1)S(1)} %get-tuple-element.53), channel_id=1, source_target_pairs={{0,4},{1,2},{2,1},{3,7},{4,0},{5,6},{6,5},{7,3},{8,12},{9,10},{10,... | collective-permute-start | bytes 196616 | tf_op jit(solution)/shard_map/ppermute | solution.py:377
  47.9 0.0 collective-permute-start.15
  47.9 4.8 %collective-permute-start.16 = (bf16[8,32,128]{2,1,0:T(8,128)(2,1)S(1)}, bf16[8,32,128]{2,1,0:T(8,128)(2,1)S(1)}, u32[]{:S(2)}, u32[]{:S(2)}) collective-permute-start(bf16[8,32,128]{2,1,0:T(8,128)(2,1)S(1)} %get-tuple-element.55), channel_id=1, source_target_pairs={{0,1},{1,0},{2,3},{3,2},{4,8},{5,9},{6,10},{7,11},{8,4},{9,5},{10,... | collective-permute-start | bytes 196616 | tf_op jit(solution)/shard_map/ppermute | solution.py:380
  52.8 2.3 %shard_map.98 = (bf16[64,32,128]{2,1,0:T(8,128)(2,1)S(1)}, bf16[100,32,128]{2,1,0:T(8,128)(2,1)S(1)}) custom-call(s32[192]{0:T(256)S(1)} %reshape.15.neighbour, bf16[64,32,128]{2,1,0:T(8,128)(2,1)S(1)} %get-tuple-element.48.refs_0_, f32[64,32,128]{2,1,0:T(8,128)S(1)} %get-tuple-element.49.refs_1_.rhs.refs_3_, ...), custom_call_target="tpu_custom_call" | custom-call | flops 268435456 | bytes 9437184 | tf_op jit(solution)/shard_map/pallas_call | solution.py:342
  55.1 0.0 collective-permute-done.13.near.from_near
  55.1 0.0 collective-permute-done.14.far.from_far
  55.2 0.1 collective-permute-start.17
  55.3 1.7 %collective-permute-start.18 = (bf16[2,32,128]{2,1,0:T(8,128)(2,1)S(1)}, bf16[2,32,128]{2,1,0:T(8,128)(2,1)S(1)}, u32[]{:S(2)}, u32[]{:S(2)}) collective-permute-start(bf16[2,32,128]{2,1,0:T(8,128)(2,1)S(1)} %get-tuple-element.59), channel_id=1, source_target_pairs={{0,1},{1,0},{2,3},{3,2},{4,8},{5,9},{6,10},{7,11},{8,4},{9,5},{10,... | collective-permute-start | bytes 49160 | tf_op jit(solution)/shard_map/ppermute | solution.py:385
  57.0 0.0 collective-permute-done.15.mate
  57.0 0.0 collective-permute-done.16.other
  57.0 1.8 %shard_map.99 = (bf16[64,32,128]{2,1,0:T(8,128)(2,1)S(1)}, bf16[100,32,128]{2,1,0:T(8,128)(2,1)S(1)}) custom-call(s32[192]{0:T(256)S(1)} %reshape.15.neighbour, bf16[100,32,128]{2,1,0:T(8,128)(2,1)S(1)} %get-tuple-element.51.local, bf16[8,32,128]{2,1,0:T(8,128)(2,1)S(1)} %collective-permute-done.13.near.from_near, ...), custom_call_target="tpu_custom_call" | custom-call | flops 268435456 | bytes 9437184 | tf_op jit(solution)/shard_map/pallas_call | solution.py:342
  58.8 0.0 collective-permute-done.17.mate
  58.8 3.3 %collective-permute-done.18.other = bf16[2,32,128]{2,1,0:T(8,128)(2,1)S(1)} collective-permute-done((bf16[2,32,128]{2,1,0:T(8,128)(2,1)S(1)}, bf16[2,32,128]{2,1,0:T(8,128)(2,1)S(1)}, u32[]{:S(2)}, u32[]{:S(2)}) %collective-permute-start.18) | collective-permute-done | bytes 16416 | tf_op jit(solution)/shard_map/ppermute | solution.py:385
  62.1 0.9 %shard_map.101 = (bf16[4,32,128]{2,1,0:T(8,128)(2,1)S(1)}, bf16[8,32,128]{2,1,0:T(8,128)(2,1)S(1)}, bf16[8,32,128]{2,1,0:T(8,128)(2,1)S(1)}, bf16[8,32,128]{2,1,0:T(8,128)(2,1)S(1)}, bf16[8,32,128]{2,1,0:T(8,128)(2,1)S(1)}) custom-call(s32[192]{0:T(256)S(1)} %reshape.15.neighbour, bf16[64,32,128]{2,1,0:T(8,128)(2,1)S(1)} %get-tuple-element.56.edges.refs_1_, ...), custom_call_target="tpu_custom_call" | custom-call | tf_op jit(solution)/shard_map/pallas_call | solution.py:342
  63.1 0.1 collective-permute-start.19
  63.2 2.6 %collective-permute-start.20 = (bf16[8,32,128]{2,1,0:T(8,128)(2,1)S(1)}, bf16[8,32,128]{2,1,0:T(8,128)(2,1)S(1)}, u32[]{:S(2)}, u32[]{:S(2)}) collective-permute-start(bf16[8,32,128]{2,1,0:T(8,128)(2,1)S(1)} %get-tuple-element.64), channel_id=1, source_target_pairs={{0,4},{1,2},{2,1},{3,7},{4,0},{5,6},{6,5},{7,3},{8,12},{9,10},{10,... | collective-permute-start | bytes 196616 | tf_op jit(solution)/shard_map/ppermute | solution.py:377
  65.8 0.0 collective-permute-start.21
  65.8 3.9 %collective-permute-start.22 = (bf16[8,32,128]{2,1,0:T(8,128)(2,1)S(1)}, bf16[8,32,128]{2,1,0:T(8,128)(2,1)S(1)}, u32[]{:S(2)}, u32[]{:S(2)}) collective-permute-start(bf16[8,32,128]{2,1,0:T(8,128)(2,1)S(1)} %get-tuple-element.66), channel_id=1, source_target_pairs={{0,1},{1,0},{2,3},{3,2},{4,8},{5,9},{6,10},{7,11},{8,4},{9,5},{10,... | collective-permute-start | bytes 196616 | tf_op jit(solution)/shard_map/ppermute | solution.py:380
  69.8 2.3 %shard_map.102 = (f32[64,32,128]{2,1,0:T(8,128)S(1)}, bf16[100,32,128]{2,1,0:T(8,128)(2,1)S(1)}) custom-call(s32[192]{0:T(256)S(1)} %reshape.15.neighbour, bf16[64,32,128]{2,1,0:T(8,128)(2,1)S(1)} %get-tuple-element.50.refs_0_, bf16[64,32,128]{2,1,0:T(8,128)(2,1)S(1)} %get-tuple-element.56.edges.refs_1_, bf16[4,32,128]{2,1,0:T(8,128)(2,1)S(1)} %get-tuple-element.60.refs_2_, ...), custom_call_target="tpu_custom_call" | custom-call | flops 268435456 | bytes 9437184 | tf_op jit(solution)/shard_map/pallas_call | solution.py:342
  72.1 0.0 collective-permute-done.19.near.from_near
  72.1 0.0 collective-permute-done.20.far.from_far
  72.1 0.1 collective-permute-start.23
  72.2 1.8 %collective-permute-start.24 = (bf16[2,32,128]{2,1,0:T(8,128)(2,1)S(1)}, bf16[2,32,128]{2,1,0:T(8,128)(2,1)S(1)}, u32[]{:S(2)}, u32[]{:S(2)}) collective-permute-start(bf16[2,32,128]{2,1,0:T(8,128)(2,1)S(1)} %get-tuple-element.70), channel_id=1, source_target_pairs={{0,1},{1,0},{2,3},{3,2},{4,8},{5,9},{6,10},{7,11},{8,4},{9,5},{10,... | collective-permute-start | bytes 49160 | tf_op jit(solution)/shard_map/ppermute | solution.py:385
  74.1 0.0 collective-permute-done.21.mate
  74.1 0.0 collective-permute-done.22.other
  74.1 3.1 %shard_map.103 = (f32[32,64,128]{2,1,0:T(8,128)}, bf16[100,32,128]{2,1,0:T(8,128)(2,1)S(1)}) custom-call(s32[192]{0:T(256)S(1)} %reshape.15.neighbour, bf16[100,32,128]{2,1,0:T(8,128)(2,1)S(1)} %get-tuple-element.61.local, f32[64,32,128]{2,1,0:T(8,128)S(1)} %get-tuple-element.62.interior, bf16[8,32,128]{2,1,0:T(8,128)(2,1)S(1)} %collective-permute-done.19.near.from_near, ...), custom_call_target="tpu_custom_call" | custom-call | flops 268435456 | bytes 9437184 | tf_op jit(solution)/shard_map/pallas_call | solution.py:342
  77.3 0.0 collective-permute-done.23.mate
  77.3 1.9 %collective-permute-done.24.other = bf16[2,32,128]{2,1,0:T(8,128)(2,1)S(1)} collective-permute-done((bf16[2,32,128]{2,1,0:T(8,128)(2,1)S(1)}, bf16[2,32,128]{2,1,0:T(8,128)(2,1)S(1)}, u32[]{:S(2)}, u32[]{:S(2)}) %collective-permute-start.24) | collective-permute-done | bytes 16416 | tf_op jit(solution)/shard_map/ppermute | solution.py:385
  79.1 1.6 %shard_map.105 = f32[32,64,128]{2,1,0:T(8,128)} custom-call(s32[192]{0:T(256)S(1)} %reshape.15.neighbour, f32[32,64,128]{2,1,0:T(8,128)} %get-tuple-element.67.partial, bf16[100,32,128]{2,1,0:T(8,128)(2,1)S(1)} %get-tuple-element.68.grid, bf16[2,32,128]{2,1,0:T(8,128)(2,1)S(1)} %collective-permute-done.23.mate, ...), custom_call_target="tpu_custom_call", output_to_operand_aliasing={{}: (1, {})} | custom-call | tf_op jit(solution)/shard_map/pallas_call | solution.py:342
  (5 shorter events, 0.1 us)
Async XLA Ops:
  1.7 23.9 %collective-permute-start.9 = (bf16[8,32,128]{2,1,0:T(8,128)(2,1)S(1)}, bf16[8,32,128]{2,1,0:T(8,128)(2,1)S(1)}, u32[]{:S(2)}, u32[]{:S(2)}) collective-permute-start(bf16[8,32,128]{2,1,0:T(8,128)(2,1)S(1)} %get-tuple-element.39), channel_id=1, source_target_pairs={{0,1},{1,0},{2,3},{3,2},{4,5},{5,4},{6,7},{7,6},{8,9},{9,8},{10,11... | collective-permute-start | bytes 196616 | tf_op jit(solution)/shard_map/ppermute | solution.py:407
  2.4 23.1 %collective-permute-start.10 = (bf16[8,32,128]{2,1,0:T(8,128)(2,1)S(1)}, bf16[8,32,128]{2,1,0:T(8,128)(2,1)S(1)}, u32[]{:S(2)}, u32[]{:S(2)}) collective-permute-start(bf16[8,32,128]{2,1,0:T(8,128)(2,1)S(1)} %get-tuple-element.40), channel_id=1, source_target_pairs={{0,4},{1,2},{2,1},{3,7},{4,0},{5,6},{6,5},{7,3},{8,12},{9,10},{10,... | collective-permute-start | bytes 196616 | tf_op jit(solution)/shard_map/ppermute | solution.py:406
  9.2 2.7 %collective-permute-start = (bf16[1,32,128]{2,1,0:T(8,128)(2,1)S(1)}, bf16[1,32,128]{2,1,0:T(8,128)(2,1)S(1)}, u32[]{:S(2)}, u32[]{:S(2)}) collective-permute-start(bf16[1,32,128]{2,1,0:T(8,128)(2,1)S(1)} %shard_map.91.part0), channel_id=1, source_target_pairs={{0,64},{4,68},{8,72},{12,76},{16,80},{20,84},{24,88},{28,92},{32,9... | collective-permute-start | bytes 24584 | tf_op jit(solution)/shard_map/ppermute | solution.py:396
  10.0 3.4 %collective-permute-start.1 = (bf16[1,32,128]{2,1,0:T(8,128)(2,1)S(1)}, bf16[1,32,128]{2,1,0:T(8,128)(2,1)S(1)}, u32[]{:S(2)}, u32[]{:S(2)}) collective-permute-start(bf16[1,32,128]{2,1,0:T(8,128)(2,1)S(1)} %shard_map.91.part0), channel_id=1, source_target_pairs={{0,128},{4,132},{8,136},{12,140},{16,144},{20,148},{24,152},{28,15... | collective-permute-start | bytes 24584 | tf_op jit(solution)/shard_map/ppermute | solution.py:396
  11.2 2.5 %collective-permute-start.2 = (bf16[1,32,128]{2,1,0:T(8,128)(2,1)S(1)}, bf16[1,32,128]{2,1,0:T(8,128)(2,1)S(1)}, u32[]{:S(2)}, u32[]{:S(2)}) collective-permute-start(bf16[1,32,128]{2,1,0:T(8,128)(2,1)S(1)} %shard_map.91.part0), channel_id=1, source_target_pairs={{0,192},{4,196},{8,200},{12,204},{16,208},{20,212},{24,216},{28,22... | collective-permute-start | bytes 24584 | tf_op jit(solution)/shard_map/ppermute | solution.py:396
  13.7 3.9 %collective-permute-start.3 = (bf16[4,32,128]{2,1,0:T(8,128)(2,1)S(1)}, bf16[4,32,128]{2,1,0:T(8,128)(2,1)S(1)}, u32[]{:S(2)}, u32[]{:S(2)}) collective-permute-start(bf16[4,32,128]{2,1,0:T(8,128)(2,1)S(1)} %shard_map.92.part0), channel_id=1, source_target_pairs={{0,16},{4,20},{8,24},{12,28},{16,0},{20,4},{24,8},{28,12},{32,48},... | collective-permute-start | bytes 98312 | tf_op jit(solution)/shard_map/ppermute | solution.py:396
  15.0 4.3 %collective-permute-start.4 = (bf16[4,32,128]{2,1,0:T(8,128)(2,1)S(1)}, bf16[4,32,128]{2,1,0:T(8,128)(2,1)S(1)}, u32[]{:S(2)}, u32[]{:S(2)}) collective-permute-start(bf16[4,32,128]{2,1,0:T(8,128)(2,1)S(1)} %shard_map.92.part0), channel_id=1, source_target_pairs={{0,32},{4,36},{8,40},{12,44},{16,48},{20,52},{24,56},{28,60},{32,0... | collective-permute-start | bytes 98312 | tf_op jit(solution)/shard_map/ppermute | solution.py:396
  17.6 4.0 %collective-permute-start.5 = (bf16[4,32,128]{2,1,0:T(8,128)(2,1)S(1)}, bf16[4,32,128]{2,1,0:T(8,128)(2,1)S(1)}, u32[]{:S(2)}, u32[]{:S(2)}) collective-permute-start(bf16[4,32,128]{2,1,0:T(8,128)(2,1)S(1)} %shard_map.92.part0), channel_id=1, source_target_pairs={{0,48},{4,52},{8,56},{12,60},{16,32},{20,36},{24,40},{28,44},{32,1... | collective-permute-start | bytes 98312 | tf_op jit(solution)/shard_map/ppermute | solution.py:396
  21.6 18.4 %collective-permute-start.6 = (bf16[16,32,128]{2,1,0:T(8,128)(2,1)S(1)}, bf16[16,32,128]{2,1,0:T(8,128)(2,1)S(1)}, u32[]{:S(2)}, u32[]{:S(2)}) collective-permute-start(bf16[16,32,128]{2,1,0:T(8,128)(2,1)S(1)} %shard_map.93.rows0), channel_id=1, source_target_pairs={{0,4},{4,0},{8,12},{12,8},{16,20},{20,16},{24,28},{28,24},{32,36},... | collective-permute-start | bytes 393224 | tf_op jit(solution)/shard_map/ppermute | solution.py:396
  22.9 17.2 %collective-permute-start.7 = (bf16[16,32,128]{2,1,0:T(8,128)(2,1)S(1)}, bf16[16,32,128]{2,1,0:T(8,128)(2,1)S(1)}, u32[]{:S(2)}, u32[]{:S(2)}) collective-permute-start(bf16[16,32,128]{2,1,0:T(8,128)(2,1)S(1)} %shard_map.93.rows0), channel_id=1, source_target_pairs={{0,8},{4,12},{8,0},{12,4},{16,24},{20,28},{24,16},{28,20},{32,40},... | collective-permute-start | bytes 393224 | tf_op jit(solution)/shard_map/ppermute | solution.py:396
  25.3 14.7 %collective-permute-start.8 = (bf16[16,32,128]{2,1,0:T(8,128)(2,1)S(1)}, bf16[16,32,128]{2,1,0:T(8,128)(2,1)S(1)}, u32[]{:S(2)}, u32[]{:S(2)}) collective-permute-start(bf16[16,32,128]{2,1,0:T(8,128)(2,1)S(1)} %shard_map.93.rows0), channel_id=1, source_target_pairs={{0,12},{4,8},{8,4},{12,0},{16,28},{20,24},{24,20},{28,16},{32,44},... | collective-permute-start | bytes 393224 | tf_op jit(solution)/shard_map/ppermute | solution.py:396
  25.6 5.7 %collective-permute-start.11 = (bf16[10,32,128]{2,1,0:T(8,128)(2,1)S(1)}, bf16[10,32,128]{2,1,0:T(8,128)(2,1)S(1)}, u32[]{:S(2)}, u32[]{:S(2)}) collective-permute-start(bf16[10,32,128]{2,1,0:T(8,128)(2,1)S(1)} %get-tuple-element.41), channel_id=1, source_target_pairs={{0,4},{1,5},{2,6},{3,7},{4,0},{5,1},{6,2},{7,3},{8,12},{9,13},{10,... | collective-permute-start | bytes 245768 | tf_op jit(solution)/shard_map/ppermute | solution.py:409
  25.7 7.7 %collective-permute-start.12 = (bf16[10,32,128]{2,1,0:T(8,128)(2,1)S(1)}, bf16[10,32,128]{2,1,0:T(8,128)(2,1)S(1)}, u32[]{:S(2)}, u32[]{:S(2)}) collective-permute-start(bf16[10,32,128]{2,1,0:T(8,128)(2,1)S(1)} %get-tuple-element.42), channel_id=1, source_target_pairs={{0,1},{1,0},{2,3},{3,2},{4,8},{5,9},{6,10},{7,11},{8,4},{9,5},{10,... | collective-permute-start | bytes 245768 | tf_op jit(solution)/shard_map/ppermute | solution.py:409
  41.2 13.9 %collective-permute-start.13 = (bf16[8,32,128]{2,1,0:T(8,128)(2,1)S(1)}, bf16[8,32,128]{2,1,0:T(8,128)(2,1)S(1)}, u32[]{:S(2)}, u32[]{:S(2)}) collective-permute-start(bf16[8,32,128]{2,1,0:T(8,128)(2,1)S(1)} %get-tuple-element.52), channel_id=1, source_target_pairs={{0,1},{1,0},{2,3},{3,2},{4,5},{5,4},{6,7},{7,6},{8,9},{9,8},{10,11... | collective-permute-start | bytes 196616 | tf_op jit(solution)/shard_map/ppermute | solution.py:378
  43.4 11.7 %collective-permute-start.14 = (bf16[8,32,128]{2,1,0:T(8,128)(2,1)S(1)}, bf16[8,32,128]{2,1,0:T(8,128)(2,1)S(1)}, u32[]{:S(2)}, u32[]{:S(2)}) collective-permute-start(bf16[8,32,128]{2,1,0:T(8,128)(2,1)S(1)} %get-tuple-element.53), channel_id=1, source_target_pairs={{0,4},{1,2},{2,1},{3,7},{4,0},{5,6},{6,5},{7,3},{8,12},{9,10},{10,... | collective-permute-start | bytes 196616 | tf_op jit(solution)/shard_map/ppermute | solution.py:377
  47.9 9.1 %collective-permute-start.15 = (bf16[8,32,128]{2,1,0:T(8,128)(2,1)S(1)}, bf16[8,32,128]{2,1,0:T(8,128)(2,1)S(1)}, u32[]{:S(2)}, u32[]{:S(2)}) collective-permute-start(bf16[8,32,128]{2,1,0:T(8,128)(2,1)S(1)} %get-tuple-element.54), channel_id=1, source_target_pairs={{0,4},{1,5},{2,6},{3,7},{4,0},{5,1},{6,2},{7,3},{8,12},{9,13},{10,... | collective-permute-start | bytes 196616 | tf_op jit(solution)/shard_map/ppermute | solution.py:379
  47.9 9.1 %collective-permute-start.16 = (bf16[8,32,128]{2,1,0:T(8,128)(2,1)S(1)}, bf16[8,32,128]{2,1,0:T(8,128)(2,1)S(1)}, u32[]{:S(2)}, u32[]{:S(2)}) collective-permute-start(bf16[8,32,128]{2,1,0:T(8,128)(2,1)S(1)} %get-tuple-element.55), channel_id=1, source_target_pairs={{0,1},{1,0},{2,3},{3,2},{4,8},{5,9},{6,10},{7,11},{8,4},{9,5},{10,... | collective-permute-start | bytes 196616 | tf_op jit(solution)/shard_map/ppermute | solution.py:380
  55.2 3.7 %collective-permute-start.17 = (bf16[2,32,128]{2,1,0:T(8,128)(2,1)S(1)}, bf16[2,32,128]{2,1,0:T(8,128)(2,1)S(1)}, u32[]{:S(2)}, u32[]{:S(2)}) collective-permute-start(bf16[2,32,128]{2,1,0:T(8,128)(2,1)S(1)} %get-tuple-element.58), channel_id=1, source_target_pairs={{0,4},{1,5},{2,6},{3,7},{4,0},{5,1},{6,2},{7,3},{8,12},{9,13},{10,... | collective-permute-start | bytes 49160 | tf_op jit(solution)/shard_map/ppermute | solution.py:385
  55.3 6.9 %collective-permute-start.18 = (bf16[2,32,128]{2,1,0:T(8,128)(2,1)S(1)}, bf16[2,32,128]{2,1,0:T(8,128)(2,1)S(1)}, u32[]{:S(2)}, u32[]{:S(2)}) collective-permute-start(bf16[2,32,128]{2,1,0:T(8,128)(2,1)S(1)} %get-tuple-element.59), channel_id=1, source_target_pairs={{0,1},{1,0},{2,3},{3,2},{4,8},{5,9},{6,10},{7,11},{8,4},{9,5},{10,... | collective-permute-start | bytes 49160 | tf_op jit(solution)/shard_map/ppermute | solution.py:385
  63.1 9.0 %collective-permute-start.19 = (bf16[8,32,128]{2,1,0:T(8,128)(2,1)S(1)}, bf16[8,32,128]{2,1,0:T(8,128)(2,1)S(1)}, u32[]{:S(2)}, u32[]{:S(2)}) collective-permute-start(bf16[8,32,128]{2,1,0:T(8,128)(2,1)S(1)} %get-tuple-element.63), channel_id=1, source_target_pairs={{0,1},{1,0},{2,3},{3,2},{4,5},{5,4},{6,7},{7,6},{8,9},{9,8},{10,11... | collective-permute-start | bytes 196616 | tf_op jit(solution)/shard_map/ppermute | solution.py:378
  63.2 8.9 %collective-permute-start.20 = (bf16[8,32,128]{2,1,0:T(8,128)(2,1)S(1)}, bf16[8,32,128]{2,1,0:T(8,128)(2,1)S(1)}, u32[]{:S(2)}, u32[]{:S(2)}) collective-permute-start(bf16[8,32,128]{2,1,0:T(8,128)(2,1)S(1)} %get-tuple-element.64), channel_id=1, source_target_pairs={{0,4},{1,2},{2,1},{3,7},{4,0},{5,6},{6,5},{7,3},{8,12},{9,10},{10,... | collective-permute-start | bytes 196616 | tf_op jit(solution)/shard_map/ppermute | solution.py:377
  65.8 8.3 %collective-permute-start.21 = (bf16[8,32,128]{2,1,0:T(8,128)(2,1)S(1)}, bf16[8,32,128]{2,1,0:T(8,128)(2,1)S(1)}, u32[]{:S(2)}, u32[]{:S(2)}) collective-permute-start(bf16[8,32,128]{2,1,0:T(8,128)(2,1)S(1)} %get-tuple-element.65), channel_id=1, source_target_pairs={{0,4},{1,5},{2,6},{3,7},{4,0},{5,1},{6,2},{7,3},{8,12},{9,13},{10,... | collective-permute-start | bytes 196616 | tf_op jit(solution)/shard_map/ppermute | solution.py:379
  65.8 8.3 %collective-permute-start.22 = (bf16[8,32,128]{2,1,0:T(8,128)(2,1)S(1)}, bf16[8,32,128]{2,1,0:T(8,128)(2,1)S(1)}, u32[]{:S(2)}, u32[]{:S(2)}) collective-permute-start(bf16[8,32,128]{2,1,0:T(8,128)(2,1)S(1)} %get-tuple-element.66), channel_id=1, source_target_pairs={{0,1},{1,0},{2,3},{3,2},{4,8},{5,9},{6,10},{7,11},{8,4},{9,5},{10,... | collective-permute-start | bytes 196616 | tf_op jit(solution)/shard_map/ppermute | solution.py:380
  72.1 5.1 %collective-permute-start.23 = (bf16[2,32,128]{2,1,0:T(8,128)(2,1)S(1)}, bf16[2,32,128]{2,1,0:T(8,128)(2,1)S(1)}, u32[]{:S(2)}, u32[]{:S(2)}) collective-permute-start(bf16[2,32,128]{2,1,0:T(8,128)(2,1)S(1)} %get-tuple-element.69), channel_id=1, source_target_pairs={{0,4},{1,5},{2,6},{3,7},{4,0},{5,1},{6,2},{7,3},{8,12},{9,13},{10,... | collective-permute-start | bytes 49160 | tf_op jit(solution)/shard_map/ppermute | solution.py:385
  72.2 6.9 %collective-permute-start.24 = (bf16[2,32,128]{2,1,0:T(8,128)(2,1)S(1)}, bf16[2,32,128]{2,1,0:T(8,128)(2,1)S(1)}, u32[]{:S(2)}, u32[]{:S(2)}) collective-permute-start(bf16[2,32,128]{2,1,0:T(8,128)(2,1)S(1)} %get-tuple-element.70), channel_id=1, source_target_pairs={{0,1},{1,0},{2,3},{3,2},{4,8},{5,9},{6,10},{7,11},{8,4},{9,5},{10,... | collective-permute-start | bytes 49160 | tf_op jit(solution)/shard_map/ppermute | solution.py:385

commit v5 on v4

--- a/solution.py
+++ b/solution.py
@@ -12,8 +12,7 @@
 WIDE = 10
 CORNERS = (0, 7, 56, 63)
 CORNER_HALOS = (0, 9, 90, 99)
-INTERIOR = tuple(b for b in range(64) if 0 < b // 8 < 7 and 0 < b % 8 < 7)
-EDGES = tuple(b for b in range(64) if b not in INTERIOR and b not in CORNERS)
+INNER = tuple(b for b in range(64) if b not in CORNERS)
 
 dot_t = functools.partial(
     lax.dot_general,
@@ -67,30 +66,29 @@
     return copies
 
 
-def spread(stream, row, held, sem):
-    copy = pltpu.make_async_copy(stream, held, sem)
-    copy.start()
-    copy.wait()
-    row[...] = held[...].astype(BF16)
-
-
-def join(part0, part1, part2, part3, whole):
-    count = part0.shape[0]
+def join(part0, part1, part2, part3, *after_and_whole):
+    count, whole = part0.shape[0], after_and_whole[-1]
     for m, part in enumerate((part0, part1, part2, part3)):
         whole[pl.ds(m * count, count)] = part[...]
 
 
-def prepare(old, x, to_near, to_far, held, sems):
+def prepare(old, stream, x, rhs, to_near, to_far, row, held, held_row, sems):
     copies = bring_old(old, held, sems)
+    row_copy = pltpu.make_async_copy(stream, held_row, sems.at[8])
+    row_copy.start()
     rows = held.reshape(32 * 64, 128)
     right = parity() == 0
     for r in range(8):
         copies[r].wait()
         for b in range(8 * r, 8 * r + 8):
-            x[b] = rows[pl.ds(b, 32, stride=64), :].astype(BF16)
+            block = rows[pl.ds(b, 32, stride=64), :]
+            rhs[b] = block
+            x[b] = block.astype(BF16)
         first, last = x[8 * r], x[8 * r + 7]
         to_near[r] = jnp.where(right, last, first)
         to_far[r] = jnp.where(right, first, last)
+    row_copy.wait()
+    row[...] = held_row[...].astype(BF16)
 
 
 def rows_to_send(x, from_near, from_far, to_mate, to_other):
@@ -164,46 +162,28 @@
     return row.astype(F32)
 
 
-def sweep_first(
-    neighbour, x, near, far, mate, other, old, upwind_far, diag_far, x_next, rhs, upwind, diag, grid, held, old_sems, sems
-):
-    old_copies = bring_old(old, held, old_sems)
-    copies = []
-    for r in range(8):
-        part = pl.ds(8 * r, 8)
-        copies.append(
-            (
-                pltpu.make_async_copy(upwind_far.at[part], upwind.at[part], sems.at[2 * r]),
-                pltpu.make_async_copy(diag_far.at[part], diag.at[part], sems.at[2 * r + 1]),
-            )
-        )
-
-    def start(r):
-        for copy in copies[r]:
-            copy.start()
-
-    for r in range(4):
-        start(r)
+def load(after, upwind_far, diag_far, upwind, diag, sems):
+    del after
+    copies = [
+        pltpu.make_async_copy(upwind_far, upwind, sems.at[0]),
+        pltpu.make_async_copy(diag_far, diag, sems.at[1]),
+    ]
+    for copy in copies:
+        copy.start()
+    for copy in copies:
+        copy.wait()
+
+
+def sweep_first(neighbour, x, near, far, mate, other, rhs, upwind, diag, x_next, grid):
+    fill(grid, x, ())
     widen(grid, near, far, mate, other)
-    for b in range(64):
-        grid[at(b)] = x[b]
-    old_rows = held.reshape(32 * 64, 128)
-    for r in range(8):
-        old_copies[r].wait()
-        for b in range(8 * r, 8 * r + 8):
-            rhs[b] = old_rows[pl.ds(b, 32, stride=64), :]
 
     def store(b, conc):
         x_next[b] = conc.astype(BF16)
 
     upstream = from_grid(neighbour, grid)
-    for r in range(0, 8, 2):
-        for ahead in (r + 4, r + 5):
-            if ahead < 8:
-                start(ahead)
-        for copy in copies[r] + copies[r + 1]:
-            copy.wait()
-        sweep(range(8 * r, 8 * r + 16), upstream, rhs, upwind, diag, store)
+    for i in range(0, 64, 16):
+        sweep(range(i, i + 16), upstream, rhs, upwind, diag, store)
 
 
 def inject(
@@ -223,41 +203,25 @@
     send_edges(lambda b: x[b], to_near, to_far, to_mate, to_other)
 
 
-def fill(grid, parts):
-    if len(parts) == 1:
-        for b in range(64):
-            grid[at(b)] = parts[0][b]
-    else:
-        interior, edges, corners = parts
-        for b in INTERIOR:
-            grid[at(b)] = interior[b]
-        for b in EDGES:
-            grid[at(b)] = edges[b]
-        for i, b in enumerate(CORNERS):
-            grid[at(b)] = corners[i]
-
-
-def inner(count, dtype, neighbour, *refs):
-    parts, (rhs, upwind, diag, interior, grid) = refs[:count], refs[count:]
-    fill(grid, parts)
-
-    def store(b, conc):
-        interior[b] = conc.astype(dtype)
+def fill(grid, x, corners):
+    for b in range(64):
+        if corners and b in CORNERS:
+            grid[at(b)] = corners[0][CORNERS.index(b)]
+        else:
+            grid[at(b)] = x[b]
+
+
+def middle(count, neighbour, x, *refs):
+    corners, (near, far, mate, other, rhs, upwind, diag, x_next, grid) = refs[:count], refs[count:]
+    fill(grid, x, corners)
+    widen(grid, near, far, mate, other)
+
+    def store(b, conc):
+        x_next[b] = conc.astype(BF16)
 
     upstream = from_grid(neighbour, grid)
-    for i in range(0, 36, 18):
-        sweep(INTERIOR[i : i + 18], upstream, rhs, upwind, diag, store)
-
-
-def middle(neighbour, local, near, far, mate, other, rhs, upwind, diag, edges, grid):
-    for b in range(64):
-        grid[at(b)] = local[at(b)]
-    widen(grid, near, far, mate, other)
-
-    def store(b, conc):
-        edges[b] = conc.astype(BF16)
-
-    sweep(EDGES, from_grid(neighbour, grid), rhs, upwind, diag, store)
+    for i in range(0, 60, 20):
+        sweep(INNER[i : i + 20], upstream, rhs, upwind, diag, store)
 
 
 def sweep_corners(neighbour, grid, mate, other, rhs, upwind, diag, store):
@@ -282,25 +246,20 @@
     send_edges(block, to_near, to_far, to_mate, to_other)
 
 
-def middle_last(neighbour, local, interior, near, far, mate, other, rhs, upwind, diag, out, grid, held, sems):
+def middle_last(neighbour, x, corners, near, far, mate, other, rhs, upwind, diag, out, grid, held, sems):
+    fill(grid, x, [corners])
+    widen(grid, near, far, mate, other)
     copies = []
 
-    def send(block, b):
-        copies.append(pltpu.make_async_copy(block, out.at[:, b], sems.at[b]))
-        copies[-1].start()
-
-    for b in INTERIOR:
-        send(interior.at[b], b)
-    for b in range(64):
-        grid[at(b)] = local[at(b)]
-    widen(grid, near, far, mate, other)
-
-    def store(b, conc):
-        held[EDGES.index(b)] = conc
-
-    sweep(EDGES, from_grid(neighbour, grid), rhs, upwind, diag, store)
-    for i, b in enumerate(EDGES):
-        send(held.at[i], b)
+    def store(b, conc):
+        held[b] = conc
+
+    upstream = from_grid(neighbour, grid)
+    for ids in (INNER[:24], INNER[24:48], INNER[48:]):
+        sweep(ids, upstream, rhs, upwind, diag, store)
+        for b in ids:
+            copies.append(pltpu.make_async_copy(held.at[b], out.at[:, b], sems.at[b]))
+            copies[-1].start()
     for copy in copies:
         copy.wait()
 
@@ -395,60 +354,58 @@
     def swaps(part, step):
         return [part] + [lax.ppermute(part, "tile", [(t, t ^ (m * step)) for t in range(tiles)]) for m in (1, 2, 3)]
 
-    (part,) = call(spread, [blocks(1)], [(HBM, streams)], [pltpu.VMEM((1, 32, 128), F32), dma(())])
-    for step in (16, 4):
-        (part,) = call(join, [blocks(4 * part.shape[0])], vmem(*swaps(part, step)))
-    rows = swaps(part, 1)
-
-    x, to_near, to_far = call(
-        prepare, [blocks(64), blocks(8), blocks(8)], [old], [held, dma((8,))], moved=4 * 2**20
+    x, rhs, to_near, to_far, part = call(
+        prepare,
+        [blocks(64), blocks(64, F32), blocks(8), blocks(8), blocks(1)],
+        [old, (HBM, streams)],
+        [held, pltpu.VMEM((1, 32, 128), F32), dma((9,))],
+        moved=4 * 2**20,
+    )
+    upwind_shape = jax.ShapeDtypeStruct((64, 3, 128, 128), BF16)
+    diag_shape = jax.ShapeDtypeStruct((64, 128, 128), BF16)
+    weights = call(
+        load,
+        [(VMEM, upwind_shape), (VMEM, diag_shape)],
+        [neighbour, (HBM, upwind.reshape(upwind_shape.shape)), (HBM, diag_inverse.reshape(diag_shape.shape))],
+        [dma((2,))],
+        moved=8 * 2**20,
     )
     from_far = lax.ppermute(to_far, both, far_pairs)
     from_near = lax.ppermute(to_near, "slab", on_chip)
     to_mate, to_other = call(rows_to_send, [blocks(WIDE)] * 2, vmem(x, from_near, from_far))
+    (part,) = call(join, [blocks(4)], vmem(*swaps(part, 16)))
+    (part,) = call(join, [blocks(16)], vmem(*swaps(part, 4), weights[1], to_mate))
+    rows = swaps(part, 1)
+
     got = from_near, from_far, lax.ppermute(to_mate, both, mates), lax.ppermute(to_other, both, others)
 
-    upwind_shape = jax.ShapeDtypeStruct((64, 3, 128, 128), BF16)
-    diag_shape = jax.ShapeDtypeStruct((64, 128, 128), BF16)
     wells = [(SMEM_FROM_HBM, v) for v in (perf_well, injector_row, perf_block, perf_rate)]
-    x, rhs, *weights, whole_grid = call(
-        sweep_first,
-        [blocks(64), blocks(64, F32), (VMEM, upwind_shape), (VMEM, diag_shape), blocks(100)],
-        [neighbour, *vmem(x, *got), old]
-        + [(HBM, upwind.reshape(upwind_shape.shape)), (HBM, diag_inverse.reshape(diag_shape.shape))],
-        [held, dma((8,)), dma((16,))],
-        **work,
+    x, whole_grid = call(
+        sweep_first, [blocks(64), blocks(100)], [neighbour, *vmem(x, *got, rhs, *weights)], **work
     )
     x, rhs, *sent = call(
         inject,
         [blocks(64), blocks(64, F32), *edges],
         [neighbour, *wells, *vmem(*rows, x, rhs, whole_grid, *weights)],
     )
-    parts = [x]
+    corners = []
     for last in (False, True):
         got = exchange(*sent)
-        interior, local = call(
-            functools.partial(inner, len(parts), F32 if last else BF16),
-            [blocks(64, F32 if last else BF16), blocks(100)],
-            [neighbour, *vmem(*parts, rhs, *weights)],
-            **work,
-        )
         ends = exchange_corners(*got[:2])
+        args = [neighbour, *vmem(x, *corners, *got, rhs, *weights)]
         if last:
             break
-        edge_blocks, whole_grid = call(
-            middle, [blocks(64), blocks(100)], [neighbour, *vmem(local, *got, rhs, *weights)], **work
+        x, whole_grid = call(functools.partial(middle, len(corners)), [blocks(64), blocks(100)], args, **work)
+        corner, *sent = call(
+            outer, [blocks(4), *edges], [neighbour, *vmem(x, whole_grid, *ends, rhs, *weights)]
         )
-        corners, *sent = call(
-            outer, [blocks(4), *edges], [neighbour, *vmem(edge_blocks, whole_grid, *ends, rhs, *weights)]
-        )
-        parts = [interior, edge_blocks, corners]
+        corners = [corner]
     whole = (ANY, jax.ShapeDtypeStruct((32, 64, 128), F32))
     partial, whole_grid = call(
         middle_last,
         [whole, blocks(100)],
-        [neighbour, *vmem(local, interior, *got, rhs, *weights)],
-        [pltpu.VMEM((24, 32, 128), F32), dma((64,))],
+        args,
+        [pltpu.VMEM((64, 32, 128), F32), dma((64,))],
         **work,
     )
     (out,) = call(

time: 81.2 us -> 76.7 us (0.945)
  the two profiles are of different devices: /device:TPU:33 before, /device:TPU:65 now
where the time goes in v5:
time: 76.7 us; the launch traced here: 75.9 us
  starting transfers between devices  41.9 us (55%)
  Pallas kernels  21.3 us (28%)
  waiting for transfers between devices  11.3 us (15%)
  local copies, waits for them, and re-layouts  0.95 us (1%)
    pallas_call x13, Pallas kernels, call(): pl.pallas_call(kernel, out_shape=shapes, in_specs=[SMEM if where is SMEM_...  21.3 us
    ppermute x9, starting transfers between devices, swaps(): lax.ppermute(part, 'tile', [(t, t ^ m * step) for t in range(tiles)])  9.48 us
    ppermute x2, starting transfers between devices, exchange(): from_other = lax.ppermute(to_other, both, others)  7.88 us
    ppermute x2, starting transfers between devices, exchange(): from_far = lax.ppermute(to_far, both, far_pairs)  6.36 us
    ppermute x1, starting transfers between devices, body(): lax.ppermute(to_other, both, others)  5.3 us
    ppermute x1, starting transfers between devices, body(): from_far = lax.ppermute(to_far, both, far_pairs)  5.1 us
    ppermute x2, starting transfers between devices, exchange_corners(): lax.ppermute(to_other, both, others)  4.72 us
    ppermute x2, waiting for transfers between devices, exchange(): from_other = lax.ppermute(to_other, both, others)  4.16 us
  transfers between devices with their start and end apart: 25, of which 8 were waited for; matrix products, arithmetic and copies ran while one was open for 1% of the time, Pallas kernels for 21%

profile of v5, /device:TPU:65, one launch (start us, length us, event | category | flops | bytes accessed | tf_op | source)
XLA Modules:
  0.0 75.9 jit_solution(14345894830021572407)
XLA Ops:
  0.0 1.7 %shard_map.91 = (bf16[64,32,128]{2,1,0:T(8,128)(2,1)S(1)}, f32[64,32,128]{2,1,0:T(8,128)S(1)}, bf16[8,32,128]{2,1,0:T(8,128)(2,1)S(1)}, bf16[8,32,128]{2,1,0:T(8,128)(2,1)S(1)}, bf16[1,32,128]{2,1,0:T(8,128)(2,1)S(1)}) custom-call(f32[32,64,128]{2,1,0:T(8,128)} %bitcast.6, f32[1,32,128]{2,1,0:T(8,128)} %stream.1), custom_call_target="tpu_custom_call" | custom-call | bytes 4194304 | tf_op jit(solution)/shard_map/pallas_call | solution.py:301
  1.7 0.8 %collective-permute-start.6 = (bf16[8,32,128]{2,1,0:T(8,128)(2,1)S(1)}, bf16[8,32,128]{2,1,0:T(8,128)(2,1)S(1)}, u32[]{:S(2)}, u32[]{:S(2)}) collective-permute-start(bf16[8,32,128]{2,1,0:T(8,128)(2,1)S(1)} %get-tuple-element.38), channel_id=1, source_target_pairs={{0,1},{1,0},{2,3},{3,2},{4,5},{5,4},{6,7},{7,6},{8,9},{9,8},{10,11... | collective-permute-start | bytes 196616 | tf_op jit(solution)/shard_map/ppermute | solution.py:374
  2.5 5.1 %collective-permute-start.7 = (bf16[8,32,128]{2,1,0:T(8,128)(2,1)S(1)}, bf16[8,32,128]{2,1,0:T(8,128)(2,1)S(1)}, u32[]{:S(2)}, u32[]{:S(2)}) collective-permute-start(bf16[8,32,128]{2,1,0:T(8,128)(2,1)S(1)} %get-tuple-element.39), channel_id=1, source_target_pairs={{0,4},{1,2},{2,1},{3,7},{4,0},{5,6},{6,5},{7,3},{8,12},{9,10},{10,... | collective-permute-start | bytes 196616 | tf_op jit(solution)/shard_map/ppermute | solution.py:373
  7.6 0.7 collective-permute-start.2
  8.3 2.1 %collective-permute-start.1 = (bf16[1,32,128]{2,1,0:T(8,128)(2,1)S(1)}, bf16[1,32,128]{2,1,0:T(8,128)(2,1)S(1)}, u32[]{:S(2)}, u32[]{:S(2)}) collective-permute-start(bf16[1,32,128]{2,1,0:T(8,128)(2,1)S(1)} %get-tuple-element.35.part0), channel_id=1, source_target_pairs={{0,128},{4,132},{8,136},{12,140},{16,144},{20,148},{24,152},{28,15... | collective-permute-start | bytes 24584 | tf_op jit(solution)/shard_map/ppermute | solution.py:355
  10.4 0.0 collective-permute-start
  10.4 0.0 collective-permute-done.2.part3
  10.4 1.3 %collective-permute-done.1.part2 = bf16[1,32,128]{2,1,0:T(8,128)(2,1)S(1)} collective-permute-done((bf16[1,32,128]{2,1,0:T(8,128)(2,1)S(1)}, bf16[1,32,128]{2,1,0:T(8,128)(2,1)S(1)}, u32[]{:S(2)}, u32[]{:S(2)}) %collective-permute-start.1) | collective-permute-done | bytes 8224 | tf_op jit(solution)/shard_map/ppermute | solution.py:355
  11.7 1.2 %collective-permute-done.part1 = bf16[1,32,128]{2,1,0:T(8,128)(2,1)S(1)} collective-permute-done((bf16[1,32,128]{2,1,0:T(8,128)(2,1)S(1)}, bf16[1,32,128]{2,1,0:T(8,128)(2,1)S(1)}, u32[]{:S(2)}, u32[]{:S(2)}) %collective-permute-start) | collective-permute-done | bytes 8224 | tf_op jit(solution)/shard_map/ppermute | solution.py:355
  12.9 2.7 %collective-permute-start.5 = (bf16[4,32,128]{2,1,0:T(8,128)(2,1)S(1)}, bf16[4,32,128]{2,1,0:T(8,128)(2,1)S(1)}, u32[]{:S(2)}, u32[]{:S(2)}) collective-permute-start(bf16[4,32,128]{2,1,0:T(8,128)(2,1)S(1)} %shard_map.92.part0), channel_id=1, source_target_pairs={{0,48},{4,52},{8,56},{12,60},{16,32},{20,36},{24,40},{28,44},{32,1... | collective-permute-start | bytes 98312 | tf_op jit(solution)/shard_map/ppermute | solution.py:355
  15.7 0.3 collective-permute-start.4
  16.0 0.2 collective-permute-start.3
  16.2 0.8 %copy.11 = s32[8,8,3]{2,1,0:T(8,128)S(1)} copy(s32[8,8,3]{1,0,2:T(8,128)} %param.12) | data formatting | bytes 1536 | tf_op args[3]
  17.1 0.1 reshape.15.after.neighbour
  17.2 4.0 %shard_map.93 = (bf16[64,3,128,128]{3,2,1,0:T(8,128)(2,1)S(1)}, bf16[64,128,128]{2,1,0:T(8,128)(2,1)S(1)}) custom-call(s32[192]{0:T(256)S(1)} %reshape.15.after.neighbour, bf16[64,3,128,128]{3,2,1,0:T(8,128)(2,1)} %bitcast.4, bf16[64,128,128]{2,1,0:T(8,128)(2,1)} %bitcast.5), custom_call_target="tpu_custom_call" | custom-call | bytes 8388608 | tf_op jit(solution)/shard_map/pallas_call | solution.py:301
  21.2 0.0 collective-permute-done.6.from_near.near
  21.2 0.0 collective-permute-done.7.from_far.far
  21.3 0.0 collective-permute-done.5.part3
  21.3 0.0 collective-permute-done.4.part2
  21.3 0.0 collective-permute-done.3.part1
  21.3 2.6 %collective-permute-start.10 = (bf16[16,32,128]{2,1,0:T(8,128)(2,1)S(1)}, bf16[16,32,128]{2,1,0:T(8,128)(2,1)S(1)}, u32[]{:S(2)}, u32[]{:S(2)}) collective-permute-start(bf16[16,32,128]{2,1,0:T(8,128)(2,1)S(1)} %shard_map.95.rows0), channel_id=1, source_target_pairs={{0,12},{4,8},{8,4},{12,0},{16,28},{20,24},{24,20},{28,16},{32,44},... | collective-permute-start | bytes 393224 | tf_op jit(solution)/shard_map/ppermute | solution.py:355
  23.9 0.5 collective-permute-start.9
  24.4 0.3 collective-permute-start.8
  24.7 5.3 %collective-permute-start.12 = (bf16[10,32,128]{2,1,0:T(8,128)(2,1)S(1)}, bf16[10,32,128]{2,1,0:T(8,128)(2,1)S(1)}, u32[]{:S(2)}, u32[]{:S(2)}) collective-permute-start(bf16[10,32,128]{2,1,0:T(8,128)(2,1)S(1)} %get-tuple-element.41), channel_id=1, source_target_pairs={{0,1},{1,0},{2,3},{3,2},{4,8},{5,9},{6,10},{7,11},{8,4},{9,5},{10,... | collective-permute-start | bytes 245768 | tf_op jit(solution)/shard_map/ppermute | solution.py:380
  30.0 0.0 collective-permute-start.11
  30.0 3.1 %collective-permute-done.12.other = bf16[10,32,128]{2,1,0:T(8,128)(2,1)S(1)} collective-permute-done((bf16[10,32,128]{2,1,0:T(8,128)(2,1)S(1)}, bf16[10,32,128]{2,1,0:T(8,128)(2,1)S(1)}, u32[]{:S(2)}, u32[]{:S(2)}) %collective-permute-start.12) | collective-permute-done | bytes 81952 | tf_op jit(solution)/shard_map/ppermute | solution.py:380
  33.1 0.5 collective-permute-done.11.mate
  33.5 3.7 %shard_map.96 = (bf16[64,32,128]{2,1,0:T(8,128)(2,1)S(1)}, bf16[100,32,128]{2,1,0:T(8,128)(2,1)S(1)}) custom-call(s32[192]{0:T(256)S(1)} %reshape.15.after.neighbour, bf16[64,32,128]{2,1,0:T(8,128)(2,1)S(1)} %get-tuple-element.37.x, bf16[8,32,128]{2,1,0:T(8,128)(2,1)S(1)} %collective-permute-done.6.from_near.near, ...), custom_call_target="tpu_custom_call" | custom-call | flops 268435456 | bytes 9437184 | tf_op jit(solution)/shard_map/pallas_call | solution.py:301
  37.2 0.0 collective-permute-done.10.rows3
  37.2 0.0 collective-permute-done.9.rows2
  37.2 0.0 collective-permute-done.8.rows1
  37.2 1.2 %shard_map.97 = (bf16[64,32,128]{2,1,0:T(8,128)(2,1)S(1)}, f32[64,32,128]{2,1,0:T(8,128)S(1)}, bf16[8,32,128]{2,1,0:T(8,128)(2,1)S(1)}, bf16[8,32,128]{2,1,0:T(8...) custom-call(s32[192]{0:T(256)S(1)} %reshape.15.after.neighbour, s32[1,1,4]{2,1,0:T(1,128)} %well.1, ...), custom_call_target="tpu_custom_call" | custom-call | tf_op jit(solution)/shard_map/pallas_call | solution.py:301
  38.4 2.0 %collective-permute-start.13 = (bf16[8,32,128]{2,1,0:T(8,128)(2,1)S(1)}, bf16[8,32,128]{2,1,0:T(8,128)(2,1)S(1)}, u32[]{:S(2)}, u32[]{:S(2)}) collective-permute-start(bf16[8,32,128]{2,1,0:T(8,128)(2,1)S(1)} %get-tuple-element.47), channel_id=1, source_target_pairs={{0,1},{1,0},{2,3},{3,2},{4,5},{5,4},{6,7},{7,6},{8,9},{9,8},{10,11... | collective-permute-start | bytes 196616 | tf_op jit(solution)/shard_map/ppermute | solution.py:337
  40.4 3.0 %collective-permute-start.14 = (bf16[8,32,128]{2,1,0:T(8,128)(2,1)S(1)}, bf16[8,32,128]{2,1,0:T(8,128)(2,1)S(1)}, u32[]{:S(2)}, u32[]{:S(2)}) collective-permute-start(bf16[8,32,128]{2,1,0:T(8,128)(2,1)S(1)} %get-tuple-element.48), channel_id=1, source_target_pairs={{0,4},{1,2},{2,1},{3,7},{4,0},{5,6},{6,5},{7,3},{8,12},{9,10},{10,... | collective-permute-start | bytes 196616 | tf_op jit(solution)/shard_map/ppermute | solution.py:336
  43.4 0.0 collective-permute-start.15
  43.4 3.9 %collective-permute-start.16 = (bf16[8,32,128]{2,1,0:T(8,128)(2,1)S(1)}, bf16[8,32,128]{2,1,0:T(8,128)(2,1)S(1)}, u32[]{:S(2)}, u32[]{:S(2)}) collective-permute-start(bf16[8,32,128]{2,1,0:T(8,128)(2,1)S(1)} %get-tuple-element.50), channel_id=1, source_target_pairs={{0,1},{1,0},{2,3},{3,2},{4,8},{5,9},{6,10},{7,11},{8,4},{9,5},{10,... | collective-permute-start | bytes 196616 | tf_op jit(solution)/shard_map/ppermute | solution.py:339
  47.4 0.0 collective-permute-done.13.refs_0_.from_near
  47.4 0.7 collective-permute-done.14.refs_1_.from_far
  48.0 0.1 collective-permute-start.17
  48.1 2.3 %collective-permute-start.18 = (bf16[2,32,128]{2,1,0:T(8,128)(2,1)S(1)}, bf16[2,32,128]{2,1,0:T(8,128)(2,1)S(1)}, u32[]{:S(2)}, u32[]{:S(2)}) collective-permute-start(bf16[2,32,128]{2,1,0:T(8,128)(2,1)S(1)} %get-tuple-element.55), channel_id=1, source_target_pairs={{0,1},{1,0},{2,3},{3,2},{4,8},{5,9},{6,10},{7,11},{8,4},{9,5},{10,... | collective-permute-start | bytes 49160 | tf_op jit(solution)/shard_map/ppermute | solution.py:344
  50.5 0.0 collective-permute-done.15.refs_2_
  50.5 1.9 %collective-permute-done.16.refs_3_ = bf16[8,32,128]{2,1,0:T(8,128)(2,1)S(1)} collective-permute-done((bf16[8,32,128]{2,1,0:T(8,128)(2,1)S(1)}, bf16[8,32,128]{2,1,0:T(8,128)(2,1)S(1)}, u32[]{:S(2)}, u32[]{:S(2)}) %collective-permute-start.16) | collective-permute-done | bytes 65568 | tf_op jit(solution)/shard_map/ppermute | solution.py:339
  52.4 3.5 %shard_map.98 = (bf16[64,32,128]{2,1,0:T(8,128)(2,1)S(1)}, bf16[100,32,128]{2,1,0:T(8,128)(2,1)S(1)}) custom-call(s32[192]{0:T(256)S(1)} %reshape.15.after.neighbour, bf16[64,32,128]{2,1,0:T(8,128)(2,1)S(1)} %get-tuple-element.46.x, bf16[8,32,128]{2,1,0:T(8,128)(2,1)S(1)} %collective-permute-done.13.refs_0_.from_near, ...), custom_call_target="tpu_custom_call" | custom-call | flops 268435456 | bytes 9437184 | tf_op jit(solution)/shard_map/pallas_call | solution.py:301
  55.9 0.0 collective-permute-done.17.mate
  55.9 0.0 collective-permute-done.18.other
  55.9 0.9 %shard_map.100 = (bf16[4,32,128]{2,1,0:T(8,128)(2,1)S(1)}, bf16[8,32,128]{2,1,0:T(8,128)(2,1)S(1)}, bf16[8,32,128]{2,1,0:T(8,128)(2,1)S(1)}, bf16[8,32,128]{2,1,0:T(8,128)(2,1)S(1)}, bf16[8,32,128]{2,1,0:T(8,128)(2,1)S(1)}) custom-call(s32[192]{0:T(256)S(1)} %reshape.15.after.neighbour, bf16[64,32,128]{2,1,0:T(8,128)(2,1)S(1)} %get-tuple-element.52.edges.x, ...), custom_call_target="tpu_custom_call" | custom-call | tf_op jit(solution)/shard_map/pallas_call | solution.py:301
  56.8 0.1 collective-permute-start.19
  56.9 3.4 %collective-permute-start.20 = (bf16[8,32,128]{2,1,0:T(8,128)(2,1)S(1)}, bf16[8,32,128]{2,1,0:T(8,128)(2,1)S(1)}, u32[]{:S(2)}, u32[]{:S(2)}) collective-permute-start(bf16[8,32,128]{2,1,0:T(8,128)(2,1)S(1)} %get-tuple-element.58), channel_id=1, source_target_pairs={{0,4},{1,2},{2,1},{3,7},{4,0},{5,6},{6,5},{7,3},{8,12},{9,10},{10,... | collective-permute-start | bytes 196616 | tf_op jit(solution)/shard_map/ppermute | solution.py:336
  60.3 0.0 collective-permute-start.21
  60.3 3.9 %collective-permute-start.22 = (bf16[8,32,128]{2,1,0:T(8,128)(2,1)S(1)}, bf16[8,32,128]{2,1,0:T(8,128)(2,1)S(1)}, u32[]{:S(2)}, u32[]{:S(2)}) collective-permute-start(bf16[8,32,128]{2,1,0:T(8,128)(2,1)S(1)} %get-tuple-element.60), channel_id=1, source_target_pairs={{0,1},{1,0},{2,3},{3,2},{4,8},{5,9},{6,10},{7,11},{8,4},{9,5},{10,... | collective-permute-start | bytes 196616 | tf_op jit(solution)/shard_map/ppermute | solution.py:339
  64.3 0.0 collective-permute-done.19.near.from_near
  64.3 0.4 collective-permute-done.20.far.from_far
  64.7 0.1 collective-permute-start.23
  64.8 2.4 %collective-permute-start.24 = (bf16[2,32,128]{2,1,0:T(8,128)(2,1)S(1)}, bf16[2,32,128]{2,1,0:T(8,128)(2,1)S(1)}, u32[]{:S(2)}, u32[]{:S(2)}) collective-permute-start(bf16[2,32,128]{2,1,0:T(8,128)(2,1)S(1)} %get-tuple-element.64), channel_id=1, source_target_pairs={{0,1},{1,0},{2,3},{3,2},{4,8},{5,9},{6,10},{7,11},{8,4},{9,5},{10,... | collective-permute-start | bytes 49160 | tf_op jit(solution)/shard_map/ppermute | solution.py:344
  67.1 0.0 collective-permute-done.21.mate
  67.1 2.2 %collective-permute-done.22.other = bf16[8,32,128]{2,1,0:T(8,128)(2,1)S(1)} collective-permute-done((bf16[8,32,128]{2,1,0:T(8,128)(2,1)S(1)}, bf16[8,32,128]{2,1,0:T(8,128)(2,1)S(1)}, u32[]{:S(2)}, u32[]{:S(2)}) %collective-permute-start.22) | collective-permute-done | bytes 65568 | tf_op jit(solution)/shard_map/ppermute | solution.py:339
  69.4 4.7 %shard_map.101 = (f32[32,64,128]{2,1,0:T(8,128)}, bf16[100,32,128]{2,1,0:T(8,128)(2,1)S(1)}) custom-call(s32[192]{0:T(256)S(1)} %reshape.15.after.neighbour, bf16[64,32,128]{2,1,0:T(8,128)(2,1)S(1)} %get-tuple-element.52.edges.x, bf16[4,32,128]{2,1,0:T(8,128)(2,1)S(1)} %get-tuple-element.56.corners, ...), custom_call_target="tpu_custom_call" | custom-call | flops 268435456 | bytes 9437184 | tf_op jit(solution)/shard_map/pallas_call | solution.py:301
  74.1 0.0 collective-permute-done.23.mate
  74.1 0.0 collective-permute-done.24.other
  74.1 1.6 %shard_map.103 = f32[32,64,128]{2,1,0:T(8,128)} custom-call(s32[192]{0:T(256)S(1)} %reshape.15.after.neighbour, f32[32,64,128]{2,1,0:T(8,128)} %get-tuple-element.61.partial, bf16[100,32,128]{2,1,0:T(8,128)(2,1)S(1)} %get-tuple-element.62.grid, bf16[2,32,128]{2,1,0:T(8,128)(2,1)S(1)} %collective-permute-done.23.mate, ...), custom_call_target="tpu_custom_call", output_to_operand_aliasing={{}: (1, {})} | custom-call | tf_op jit(solution)/shard_map/pallas_call | solution.py:301
  (5 shorter events, 0.1 us)
Async XLA Ops:
  1.7 19.4 %collective-permute-start.6 = (bf16[8,32,128]{2,1,0:T(8,128)(2,1)S(1)}, bf16[8,32,128]{2,1,0:T(8,128)(2,1)S(1)}, u32[]{:S(2)}, u32[]{:S(2)}) collective-permute-start(bf16[8,32,128]{2,1,0:T(8,128)(2,1)S(1)} %get-tuple-element.38), channel_id=1, source_target_pairs={{0,1},{1,0},{2,3},{3,2},{4,5},{5,4},{6,7},{7,6},{8,9},{9,8},{10,11... | collective-permute-start | bytes 196616 | tf_op jit(solution)/shard_map/ppermute | solution.py:374
  2.5 18.7 %collective-permute-start.7 = (bf16[8,32,128]{2,1,0:T(8,128)(2,1)S(1)}, bf16[8,32,128]{2,1,0:T(8,128)(2,1)S(1)}, u32[]{:S(2)}, u32[]{:S(2)}) collective-permute-start(bf16[8,32,128]{2,1,0:T(8,128)(2,1)S(1)} %get-tuple-element.39), channel_id=1, source_target_pairs={{0,4},{1,2},{2,1},{3,7},{4,0},{5,6},{6,5},{7,3},{8,12},{9,10},{10,... | collective-permute-start | bytes 196616 | tf_op jit(solution)/shard_map/ppermute | solution.py:373
  7.6 2.8 %collective-permute-start.2 = (bf16[1,32,128]{2,1,0:T(8,128)(2,1)S(1)}, bf16[1,32,128]{2,1,0:T(8,128)(2,1)S(1)}, u32[]{:S(2)}, u32[]{:S(2)}) collective-permute-start(bf16[1,32,128]{2,1,0:T(8,128)(2,1)S(1)} %get-tuple-element.35.part0), channel_id=1, source_target_pairs={{0,192},{4,196},{8,200},{12,204},{16,208},{20,212},{24,216},{28,22... | collective-permute-start | bytes 24584 | tf_op jit(solution)/shard_map/ppermute | solution.py:355
  8.3 3.4 %collective-permute-start.1 = (bf16[1,32,128]{2,1,0:T(8,128)(2,1)S(1)}, bf16[1,32,128]{2,1,0:T(8,128)(2,1)S(1)}, u32[]{:S(2)}, u32[]{:S(2)}) collective-permute-start(bf16[1,32,128]{2,1,0:T(8,128)(2,1)S(1)} %get-tuple-element.35.part0), channel_id=1, source_target_pairs={{0,128},{4,132},{8,136},{12,140},{16,144},{20,148},{24,152},{28,15... | collective-permute-start | bytes 24584 | tf_op jit(solution)/shard_map/ppermute | solution.py:355
  10.4 2.5 %collective-permute-start = (bf16[1,32,128]{2,1,0:T(8,128)(2,1)S(1)}, bf16[1,32,128]{2,1,0:T(8,128)(2,1)S(1)}, u32[]{:S(2)}, u32[]{:S(2)}) collective-permute-start(bf16[1,32,128]{2,1,0:T(8,128)(2,1)S(1)} %get-tuple-element.35.part0), channel_id=1, source_target_pairs={{0,64},{4,68},{8,72},{12,76},{16,80},{20,84},{24,88},{28,92},{32,9... | collective-permute-start | bytes 24584 | tf_op jit(solution)/shard_map/ppermute | solution.py:355
  12.9 8.3 %collective-permute-start.5 = (bf16[4,32,128]{2,1,0:T(8,128)(2,1)S(1)}, bf16[4,32,128]{2,1,0:T(8,128)(2,1)S(1)}, u32[]{:S(2)}, u32[]{:S(2)}) collective-permute-start(bf16[4,32,128]{2,1,0:T(8,128)(2,1)S(1)} %shard_map.92.part0), channel_id=1, source_target_pairs={{0,48},{4,52},{8,56},{12,60},{16,32},{20,36},{24,40},{28,44},{32,1... | collective-permute-start | bytes 98312 | tf_op jit(solution)/shard_map/ppermute | solution.py:355
  15.7 5.6 %collective-permute-start.4 = (bf16[4,32,128]{2,1,0:T(8,128)(2,1)S(1)}, bf16[4,32,128]{2,1,0:T(8,128)(2,1)S(1)}, u32[]{:S(2)}, u32[]{:S(2)}) collective-permute-start(bf16[4,32,128]{2,1,0:T(8,128)(2,1)S(1)} %shard_map.92.part0), channel_id=1, source_target_pairs={{0,32},{4,36},{8,40},{12,44},{16,48},{20,52},{24,56},{28,60},{32,0... | collective-permute-start | bytes 98312 | tf_op jit(solution)/shard_map/ppermute | solution.py:355
  16.0 5.3 %collective-permute-start.3 = (bf16[4,32,128]{2,1,0:T(8,128)(2,1)S(1)}, bf16[4,32,128]{2,1,0:T(8,128)(2,1)S(1)}, u32[]{:S(2)}, u32[]{:S(2)}) collective-permute-start(bf16[4,32,128]{2,1,0:T(8,128)(2,1)S(1)} %shard_map.92.part0), channel_id=1, source_target_pairs={{0,16},{4,20},{8,24},{12,28},{16,0},{20,4},{24,8},{28,12},{32,48},... | collective-permute-start | bytes 98312 | tf_op jit(solution)/shard_map/ppermute | solution.py:355
  21.3 15.9 %collective-permute-start.10 = (bf16[16,32,128]{2,1,0:T(8,128)(2,1)S(1)}, bf16[16,32,128]{2,1,0:T(8,128)(2,1)S(1)}, u32[]{:S(2)}, u32[]{:S(2)}) collective-permute-start(bf16[16,32,128]{2,1,0:T(8,128)(2,1)S(1)} %shard_map.95.rows0), channel_id=1, source_target_pairs={{0,12},{4,8},{8,4},{12,0},{16,28},{20,24},{24,20},{28,16},{32,44},... | collective-permute-start | bytes 393224 | tf_op jit(solution)/shard_map/ppermute | solution.py:355
  23.9 13.3 %collective-permute-start.9 = (bf16[16,32,128]{2,1,0:T(8,128)(2,1)S(1)}, bf16[16,32,128]{2,1,0:T(8,128)(2,1)S(1)}, u32[]{:S(2)}, u32[]{:S(2)}) collective-permute-start(bf16[16,32,128]{2,1,0:T(8,128)(2,1)S(1)} %shard_map.95.rows0), channel_id=1, source_target_pairs={{0,8},{4,12},{8,0},{12,4},{16,24},{20,28},{24,16},{28,20},{32,40},... | collective-permute-start | bytes 393224 | tf_op jit(solution)/shard_map/ppermute | solution.py:355
  24.4 12.8 %collective-permute-start.8 = (bf16[16,32,128]{2,1,0:T(8,128)(2,1)S(1)}, bf16[16,32,128]{2,1,0:T(8,128)(2,1)S(1)}, u32[]{:S(2)}, u32[]{:S(2)}) collective-permute-start(bf16[16,32,128]{2,1,0:T(8,128)(2,1)S(1)} %shard_map.95.rows0), channel_id=1, source_target_pairs={{0,4},{4,0},{8,12},{12,8},{16,20},{20,16},{24,28},{28,24},{32,36},... | collective-permute-start | bytes 393224 | tf_op jit(solution)/shard_map/ppermute | solution.py:355
  24.7 8.4 %collective-permute-start.12 = (bf16[10,32,128]{2,1,0:T(8,128)(2,1)S(1)}, bf16[10,32,128]{2,1,0:T(8,128)(2,1)S(1)}, u32[]{:S(2)}, u32[]{:S(2)}) collective-permute-start(bf16[10,32,128]{2,1,0:T(8,128)(2,1)S(1)} %get-tuple-element.41), channel_id=1, source_target_pairs={{0,1},{1,0},{2,3},{3,2},{4,8},{5,9},{6,10},{7,11},{8,4},{9,5},{10,... | collective-permute-start | bytes 245768 | tf_op jit(solution)/shard_map/ppermute | solution.py:380
  30.0 3.6 %collective-permute-start.11 = (bf16[10,32,128]{2,1,0:T(8,128)(2,1)S(1)}, bf16[10,32,128]{2,1,0:T(8,128)(2,1)S(1)}, u32[]{:S(2)}, u32[]{:S(2)}) collective-permute-start(bf16[10,32,128]{2,1,0:T(8,128)(2,1)S(1)} %get-tuple-element.40.after_and_whole_1_), channel_id=1, source_target_pairs={{0,4},{1,5},{2,6},{3,7},{4,0},{5,1},{6,2},{7,3},{8,12},{9,13},{10,... | collective-permute-start | bytes 245768 | tf_op jit(solution)/shard_map/ppermute | solution.py:380
  38.4 9.0 %collective-permute-start.13 = (bf16[8,32,128]{2,1,0:T(8,128)(2,1)S(1)}, bf16[8,32,128]{2,1,0:T(8,128)(2,1)S(1)}, u32[]{:S(2)}, u32[]{:S(2)}) collective-permute-start(bf16[8,32,128]{2,1,0:T(8,128)(2,1)S(1)} %get-tuple-element.47), channel_id=1, source_target_pairs={{0,1},{1,0},{2,3},{3,2},{4,5},{5,4},{6,7},{7,6},{8,9},{9,8},{10,11... | collective-permute-start | bytes 196616 | tf_op jit(solution)/shard_map/ppermute | solution.py:337
  40.4 7.6 %collective-permute-start.14 = (bf16[8,32,128]{2,1,0:T(8,128)(2,1)S(1)}, bf16[8,32,128]{2,1,0:T(8,128)(2,1)S(1)}, u32[]{:S(2)}, u32[]{:S(2)}) collective-permute-start(bf16[8,32,128]{2,1,0:T(8,128)(2,1)S(1)} %get-tuple-element.48), channel_id=1, source_target_pairs={{0,4},{1,2},{2,1},{3,7},{4,0},{5,6},{6,5},{7,3},{8,12},{9,10},{10,... | collective-permute-start | bytes 196616 | tf_op jit(solution)/shard_map/ppermute | solution.py:336
  43.4 7.1 %collective-permute-start.15 = (bf16[8,32,128]{2,1,0:T(8,128)(2,1)S(1)}, bf16[8,32,128]{2,1,0:T(8,128)(2,1)S(1)}, u32[]{:S(2)}, u32[]{:S(2)}) collective-permute-start(bf16[8,32,128]{2,1,0:T(8,128)(2,1)S(1)} %get-tuple-element.49), channel_id=1, source_target_pairs={{0,4},{1,5},{2,6},{3,7},{4,0},{5,1},{6,2},{7,3},{8,12},{9,13},{10,... | collective-permute-start | bytes 196616 | tf_op jit(solution)/shard_map/ppermute | solution.py:338
  43.4 9.0 %collective-permute-start.16 = (bf16[8,32,128]{2,1,0:T(8,128)(2,1)S(1)}, bf16[8,32,128]{2,1,0:T(8,128)(2,1)S(1)}, u32[]{:S(2)}, u32[]{:S(2)}) collective-permute-start(bf16[8,32,128]{2,1,0:T(8,128)(2,1)S(1)} %get-tuple-element.50), channel_id=1, source_target_pairs={{0,1},{1,0},{2,3},{3,2},{4,8},{5,9},{6,10},{7,11},{8,4},{9,5},{10,... | collective-permute-start | bytes 196616 | tf_op jit(solution)/shard_map/ppermute | solution.py:339
  48.0 7.8 %collective-permute-start.17 = (bf16[2,32,128]{2,1,0:T(8,128)(2,1)S(1)}, bf16[2,32,128]{2,1,0:T(8,128)(2,1)S(1)}, u32[]{:S(2)}, u32[]{:S(2)}) collective-permute-start(bf16[2,32,128]{2,1,0:T(8,128)(2,1)S(1)} %get-tuple-element.54), channel_id=1, source_target_pairs={{0,4},{1,5},{2,6},{3,7},{4,0},{5,1},{6,2},{7,3},{8,12},{9,13},{10,... | collective-permute-start | bytes 49160 | tf_op jit(solution)/shard_map/ppermute | solution.py:344
  48.1 7.7 %collective-permute-start.18 = (bf16[2,32,128]{2,1,0:T(8,128)(2,1)S(1)}, bf16[2,32,128]{2,1,0:T(8,128)(2,1)S(1)}, u32[]{:S(2)}, u32[]{:S(2)}) collective-permute-start(bf16[2,32,128]{2,1,0:T(8,128)(2,1)S(1)} %get-tuple-element.55), channel_id=1, source_target_pairs={{0,1},{1,0},{2,3},{3,2},{4,8},{5,9},{6,10},{7,11},{8,4},{9,5},{10,... | collective-permute-start | bytes 49160 | tf_op jit(solution)/shard_map/ppermute | solution.py:344
  56.8 7.4 %collective-permute-start.19 = (bf16[8,32,128]{2,1,0:T(8,128)(2,1)S(1)}, bf16[8,32,128]{2,1,0:T(8,128)(2,1)S(1)}, u32[]{:S(2)}, u32[]{:S(2)}) collective-permute-start(bf16[8,32,128]{2,1,0:T(8,128)(2,1)S(1)} %get-tuple-element.57), channel_id=1, source_target_pairs={{0,1},{1,0},{2,3},{3,2},{4,5},{5,4},{6,7},{7,6},{8,9},{9,8},{10,11... | collective-permute-start | bytes 196616 | tf_op jit(solution)/shard_map/ppermute | solution.py:337
  56.9 7.7 %collective-permute-start.20 = (bf16[8,32,128]{2,1,0:T(8,128)(2,1)S(1)}, bf16[8,32,128]{2,1,0:T(8,128)(2,1)S(1)}, u32[]{:S(2)}, u32[]{:S(2)}) collective-permute-start(bf16[8,32,128]{2,1,0:T(8,128)(2,1)S(1)} %get-tuple-element.58), channel_id=1, source_target_pairs={{0,4},{1,2},{2,1},{3,7},{4,0},{5,6},{6,5},{7,3},{8,12},{9,10},{10,... | collective-permute-start | bytes 196616 | tf_op jit(solution)/shard_map/ppermute | solution.py:336
  60.3 6.8 %collective-permute-start.21 = (bf16[8,32,128]{2,1,0:T(8,128)(2,1)S(1)}, bf16[8,32,128]{2,1,0:T(8,128)(2,1)S(1)}, u32[]{:S(2)}, u32[]{:S(2)}) collective-permute-start(bf16[8,32,128]{2,1,0:T(8,128)(2,1)S(1)} %get-tuple-element.59), channel_id=1, source_target_pairs={{0,4},{1,5},{2,6},{3,7},{4,0},{5,1},{6,2},{7,3},{8,12},{9,13},{10,... | collective-permute-start | bytes 196616 | tf_op jit(solution)/shard_map/ppermute | solution.py:338
  60.3 9.1 %collective-permute-start.22 = (bf16[8,32,128]{2,1,0:T(8,128)(2,1)S(1)}, bf16[8,32,128]{2,1,0:T(8,128)(2,1)S(1)}, u32[]{:S(2)}, u32[]{:S(2)}) collective-permute-start(bf16[8,32,128]{2,1,0:T(8,128)(2,1)S(1)} %get-tuple-element.60), channel_id=1, source_target_pairs={{0,1},{1,0},{2,3},{3,2},{4,8},{5,9},{6,10},{7,11},{8,4},{9,5},{10,... | collective-permute-start | bytes 196616 | tf_op jit(solution)/shard_map/ppermute | solution.py:339
  64.7 9.4 %collective-permute-start.23 = (bf16[2,32,128]{2,1,0:T(8,128)(2,1)S(1)}, bf16[2,32,128]{2,1,0:T(8,128)(2,1)S(1)}, u32[]{:S(2)}, u32[]{:S(2)}) collective-permute-start(bf16[2,32,128]{2,1,0:T(8,128)(2,1)S(1)} %get-tuple-element.63), channel_id=1, source_target_pairs={{0,4},{1,5},{2,6},{3,7},{4,0},{5,1},{6,2},{7,3},{8,12},{9,13},{10,... | collective-permute-start | bytes 49160 | tf_op jit(solution)/shard_map/ppermute | solution.py:344
  64.8 9.4 %collective-permute-start.24 = (bf16[2,32,128]{2,1,0:T(8,128)(2,1)S(1)}, bf16[2,32,128]{2,1,0:T(8,128)(2,1)S(1)}, u32[]{:S(2)}, u32[]{:S(2)}) collective-permute-start(bf16[2,32,128]{2,1,0:T(8,128)(2,1)S(1)} %get-tuple-element.64), channel_id=1, source_target_pairs={{0,1},{1,0},{2,3},{3,2},{4,8},{5,9},{6,10},{7,11},{8,4},{9,5},{10,... | collective-permute-start | bytes 49160 | tf_op jit(solution)/shard_map/ppermute | solution.py:344

commit v6 on v5

--- a/solution.py
+++ b/solution.py
@@ -138,9 +138,12 @@
 
 def sweep(ids, upstream, rhs, upwind, diag, store):
     remainders = []
-    for b in ids:
-        weights = jnp.concatenate([upwind[b, k] for k in range(3)], axis=1)
-        remainders.append((rhs[b] - dot_t(upstream(b), weights)).astype(BF16))
+    for b, c in zip(ids[::2], ids[1::2], strict=True):
+        both = jnp.concatenate([upstream(b), upstream(c)], axis=0)
+        weights = [jnp.concatenate([upwind[d, k] for k in range(3)], axis=1) for d in (b, c)]
+        coupled = dot_t(both, jnp.concatenate(weights, axis=0))
+        remainders.append((rhs[b] - coupled[:32, :128]).astype(BF16))
+        remainders.append((rhs[c] - coupled[32:, 128:]).astype(BF16))
     for i in range(0, len(ids), 2):
         both = jnp.concatenate(remainders[i : i + 2], axis=0)
         weights = jnp.concatenate([diag[ids[i]], diag[ids[i + 1]]], axis=0)
@@ -162,14 +165,18 @@
     return row.astype(F32)
 
 
-def load(after, upwind_far, diag_far, upwind, diag, sems):
-    del after
+def load(neighbour_in, upwind_far, diag_far, upwind, diag, neighbour, sems):
     copies = [
         pltpu.make_async_copy(upwind_far, upwind, sems.at[0]),
         pltpu.make_async_copy(diag_far, diag, sems.at[1]),
     ]
     for copy in copies:
         copy.start()
+
+    @pl.loop(0, neighbour.shape[0])
+    def _(i):
+        neighbour[i] = neighbour_in[i]
+
     for copy in copies:
         copy.wait()
 
@@ -182,8 +189,8 @@
         x_next[b] = conc.astype(BF16)
 
     upstream = from_grid(neighbour, grid)
-    for i in range(0, 64, 16):
-        sweep(range(i, i + 16), upstream, rhs, upwind, diag, store)
+    for i in range(0, 64, 32):
+        sweep(range(i, i + 32), upstream, rhs, upwind, diag, store)
 
 
 def inject(
@@ -220,8 +227,8 @@
         x_next[b] = conc.astype(BF16)
 
     upstream = from_grid(neighbour, grid)
-    for i in range(0, 60, 20):
-        sweep(INNER[i : i + 20], upstream, rhs, upwind, diag, store)
+    for i in range(0, 60, 30):
+        sweep(INNER[i : i + 30], upstream, rhs, upwind, diag, store)
 
 
 def sweep_corners(neighbour, grid, mate, other, rhs, upwind, diag, store):
@@ -280,7 +287,7 @@
 
 VMEM, SMEM, ANY, HBM = (pl.BlockSpec(memory_space=m) for m in (pltpu.VMEM, pltpu.SMEM, pl.ANY, pltpu.HBM))
 
-SMEM_FROM_HBM = "scalars"
+SMEM_FROM_HBM, SMEM_KEPT = "scalars", "kept scalars"
 
 
 def call(kernel, outs, args, scratch=(), aliases=None, flops=0, moved=0):
@@ -288,6 +295,8 @@
     for where, value in args:
         if where is VMEM:
             value = pltpu.with_memory_space_constraint(value, pltpu.VMEM)
+        if where is SMEM_KEPT:
+            value = pltpu.with_memory_space_constraint(value, pltpu.SMEM)
         if where in (HBM, SMEM_FROM_HBM):
             value = pltpu.with_memory_space_constraint(value, pltpu.HBM)
         values.append(value)
@@ -297,11 +306,13 @@
             s = pltpu.VMEM(s.shape, s.dtype)
         if where is HBM:
             s = pltpu.HBM(s.shape, s.dtype)
+        if where is SMEM:
+            s = pltpu.SMEM(s.shape, s.dtype)
         shapes.append(s)
     return pl.pallas_call(
         kernel,
         out_shape=shapes,
-        in_specs=[SMEM if where is SMEM_FROM_HBM else where for where, _ in args],
+        in_specs=[SMEM if isinstance(where, str) else where for where, _ in args],
         out_specs=[where for where, _ in outs],
         scratch_shapes=list(scratch),
         input_output_aliases=aliases or {},
@@ -363,13 +374,14 @@
     )
     upwind_shape = jax.ShapeDtypeStruct((64, 3, 128, 128), BF16)
     diag_shape = jax.ShapeDtypeStruct((64, 128, 128), BF16)
-    weights = call(
+    *weights, neighbour_here = call(
         load,
-        [(VMEM, upwind_shape), (VMEM, diag_shape)],
+        [(VMEM, upwind_shape), (VMEM, diag_shape), (SMEM, jax.ShapeDtypeStruct((192,), jnp.int32))],
         [neighbour, (HBM, upwind.reshape(upwind_shape.shape)), (HBM, diag_inverse.reshape(diag_shape.shape))],
         [dma((2,))],
         moved=8 * 2**20,
     )
+    neighbour = (SMEM_KEPT, neighbour_here)
     from_far = lax.ppermute(to_far, both, far_pairs)
     from_near = lax.ppermute(to_near, "slab", on_chip)
     to_mate, to_other = call(rows_to_send, [blocks(WIDE)] * 2, vmem(x, from_near, from_far))

time: 76.7 us -> 73.9 us (0.963)
  Pallas kernels: 21.3 us -> 17.8 us
    pallas_call x13, Pallas kernels: 21.3 us -> 17.8 us  [call(): pl.pallas_call(kernel, out_shape=shapes, in_specs=[SMEM if isinstance(whe...]
    ppermute x2, starting transfers between devices: 6.36 us -> 7.14 us  [exchange(): from_far = lax.ppermute(to_far, both, far_pairs)]
  transfers between devices with their start and end apart: 25 -> 25, of which waited for: 8 -> 7; matrix products, arithmetic and copies ran while one was open for 1% -> 1% of each run, Pallas kernels for 21% -> 19%
where the time goes in v6:
time: 73.9 us; the launch traced here: 73.1 us
  starting transfers between devices  42.3 us (57%)
  Pallas kernels  17.8 us (24%)
  waiting for transfers between devices  11.5 us (16%)
  local copies, waits for them, and re-layouts  0.95 us (1%)
    pallas_call x13, Pallas kernels, call(): pl.pallas_call(kernel, out_shape=shapes, in_specs=[SMEM if isinstance(whe...  17.8 us
    ppermute x9, starting transfers between devices, swaps(): lax.ppermute(part, 'tile', [(t, t ^ m * step) for t in range(tiles)])  9.48 us
    ppermute x2, starting transfers between devices, exchange(): from_other = lax.ppermute(to_other, both, others)  7.9 us
    ppermute x2, starting transfers between devices, exchange(): from_far = lax.ppermute(to_far, both, far_pairs)  7.14 us
    ppermute x1, starting transfers between devices, body(): lax.ppermute(to_other, both, others)  5.3 us
    ppermute x1, starting transfers between devices, body(): from_far = lax.ppermute(to_far, both, far_pairs)  5.1 us
    ppermute x2, waiting for transfers between devices, exchange(): from_other = lax.ppermute(to_other, both, others)  4.77 us
    ppermute x2, starting transfers between devices, exchange_corners(): lax.ppermute(to_other, both, others)  4.36 us
  transfers between devices with their start and end apart: 25, of which 7 were waited for; matrix products, arithmetic and copies ran while one was open for 1% of the time, Pallas kernels for 19%

profile of v6, /device:TPU:65, one launch (start us, length us, event | category | flops | bytes accessed | tf_op | source)
XLA Modules:
  0.0 73.1 jit_solution(1263451145688984655)
XLA Ops:
  0.0 1.7 %shard_map.92 = (bf16[64,32,128]{2,1,0:T(8,128)(2,1)S(1)}, f32[64,32,128]{2,1,0:T(8,128)S(1)}, bf16[8,32,128]{2,1,0:T(8,128)(2,1)S(1)}, bf16[8,32,128]{2,1,0:T(8,128)(2,1)S(1)}, bf16[1,32,128]{2,1,0:T(8,128)(2,1)S(1)}) custom-call(f32[32,64,128]{2,1,0:T(8,128)} %bitcast.6, f32[1,32,128]{2,1,0:T(8,128)} %stream.1), custom_call_target="tpu_custom_call" | custom-call | bytes 4194304 | tf_op jit(solution)/shard_map/pallas_call | solution.py:312
  1.7 0.8 %collective-permute-start.6 = (bf16[8,32,128]{2,1,0:T(8,128)(2,1)S(1)}, bf16[8,32,128]{2,1,0:T(8,128)(2,1)S(1)}, u32[]{:S(2)}, u32[]{:S(2)}) collective-permute-start(bf16[8,32,128]{2,1,0:T(8,128)(2,1)S(1)} %get-tuple-element.40), channel_id=1, source_target_pairs={{0,1},{1,0},{2,3},{3,2},{4,5},{5,4},{6,7},{7,6},{8,9},{9,8},{10,11... | collective-permute-start | bytes 196616 | tf_op jit(solution)/shard_map/ppermute | solution.py:386
  2.5 5.1 %collective-permute-start.7 = (bf16[8,32,128]{2,1,0:T(8,128)(2,1)S(1)}, bf16[8,32,128]{2,1,0:T(8,128)(2,1)S(1)}, u32[]{:S(2)}, u32[]{:S(2)}) collective-permute-start(bf16[8,32,128]{2,1,0:T(8,128)(2,1)S(1)} %get-tuple-element.41), channel_id=1, source_target_pairs={{0,4},{1,2},{2,1},{3,7},{4,0},{5,6},{6,5},{7,3},{8,12},{9,10},{10,... | collective-permute-start | bytes 196616 | tf_op jit(solution)/shard_map/ppermute | solution.py:385
  7.6 0.7 collective-permute-start.2
  8.3 2.1 %collective-permute-start.1 = (bf16[1,32,128]{2,1,0:T(8,128)(2,1)S(1)}, bf16[1,32,128]{2,1,0:T(8,128)(2,1)S(1)}, u32[]{:S(2)}, u32[]{:S(2)}) collective-permute-start(bf16[1,32,128]{2,1,0:T(8,128)(2,1)S(1)} %get-tuple-element.37.part0), channel_id=1, source_target_pairs={{0,128},{4,132},{8,136},{12,140},{16,144},{20,148},{24,152},{28,15... | collective-permute-start | bytes 24584 | tf_op jit(solution)/shard_map/ppermute | solution.py:366
  10.4 0.0 collective-permute-start
  10.4 0.0 collective-permute-done.2.part3
  10.4 1.3 %collective-permute-done.1.part2 = bf16[1,32,128]{2,1,0:T(8,128)(2,1)S(1)} collective-permute-done((bf16[1,32,128]{2,1,0:T(8,128)(2,1)S(1)}, bf16[1,32,128]{2,1,0:T(8,128)(2,1)S(1)}, u32[]{:S(2)}, u32[]{:S(2)}) %collective-permute-start.1) | collective-permute-done | bytes 8224 | tf_op jit(solution)/shard_map/ppermute | solution.py:366
  11.7 1.2 %collective-permute-done.part1 = bf16[1,32,128]{2,1,0:T(8,128)(2,1)S(1)} collective-permute-done((bf16[1,32,128]{2,1,0:T(8,128)(2,1)S(1)}, bf16[1,32,128]{2,1,0:T(8,128)(2,1)S(1)}, u32[]{:S(2)}, u32[]{:S(2)}) %collective-permute-start) | collective-permute-done | bytes 8224 | tf_op jit(solution)/shard_map/ppermute | solution.py:366
  12.9 2.7 %collective-permute-start.5 = (bf16[4,32,128]{2,1,0:T(8,128)(2,1)S(1)}, bf16[4,32,128]{2,1,0:T(8,128)(2,1)S(1)}, u32[]{:S(2)}, u32[]{:S(2)}) collective-permute-start(bf16[4,32,128]{2,1,0:T(8,128)(2,1)S(1)} %shard_map.93.part0), channel_id=1, source_target_pairs={{0,48},{4,52},{8,56},{12,60},{16,32},{20,36},{24,40},{28,44},{32,1... | collective-permute-start | bytes 98312 | tf_op jit(solution)/shard_map/ppermute | solution.py:366
  15.7 0.3 collective-permute-start.4
  16.0 0.2 collective-permute-start.3
  16.2 0.8 %copy.11 = s32[8,8,3]{2,1,0:T(8,128)S(1)} copy(s32[8,8,3]{1,0,2:T(8,128)} %param.12) | data formatting | bytes 1536 | tf_op args[3]
  17.1 0.1 reshape.15.neighbour_in
  17.2 4.0 %shard_map.91 = (bf16[64,3,128,128]{3,2,1,0:T(8,128)(2,1)S(1)}, bf16[64,128,128]{2,1,0:T(8,128)(2,1)S(1)}, s32[192]{0:T(256)S(4)}) custom-call(s32[192]{0:T(256)S(1)} %reshape.15.neighbour_in, bf16[64,3,128,128]{3,2,1,0:T(8,128)(2,1)} %bitcast.4, bf16[64,128,128]{2,1,0:T(8,128)(2,1)} %bitcast.5), custom_call_target="tpu_custom_call" | custom-call | bytes 8388608 | tf_op jit(solution)/shard_map/pallas_call | solution.py:312
  21.2 0.0 collective-permute-done.6.from_near.near
  21.2 0.0 collective-permute-done.7.from_far.far
  21.3 0.0 collective-permute-done.5.part3
  21.3 0.0 collective-permute-done.4.part2
  21.3 0.0 collective-permute-done.3.part1
  21.3 2.6 %collective-permute-start.10 = (bf16[16,32,128]{2,1,0:T(8,128)(2,1)S(1)}, bf16[16,32,128]{2,1,0:T(8,128)(2,1)S(1)}, u32[]{:S(2)}, u32[]{:S(2)}) collective-permute-start(bf16[16,32,128]{2,1,0:T(8,128)(2,1)S(1)} %shard_map.95.rows0), channel_id=1, source_target_pairs={{0,12},{4,8},{8,4},{12,0},{16,28},{20,24},{24,20},{28,16},{32,44},... | collective-permute-start | bytes 393224 | tf_op jit(solution)/shard_map/ppermute | solution.py:366
  23.9 0.5 collective-permute-start.9
  24.4 0.3 collective-permute-start.8
  24.7 5.3 %collective-permute-start.12 = (bf16[10,32,128]{2,1,0:T(8,128)(2,1)S(1)}, bf16[10,32,128]{2,1,0:T(8,128)(2,1)S(1)}, u32[]{:S(2)}, u32[]{:S(2)}) collective-permute-start(bf16[10,32,128]{2,1,0:T(8,128)(2,1)S(1)} %get-tuple-element.43), channel_id=1, source_target_pairs={{0,1},{1,0},{2,3},{3,2},{4,8},{5,9},{6,10},{7,11},{8,4},{9,5},{10,... | collective-permute-start | bytes 245768 | tf_op jit(solution)/shard_map/ppermute | solution.py:392
  30.0 0.0 collective-permute-start.11
  30.0 3.1 %collective-permute-done.12.other = bf16[10,32,128]{2,1,0:T(8,128)(2,1)S(1)} collective-permute-done((bf16[10,32,128]{2,1,0:T(8,128)(2,1)S(1)}, bf16[10,32,128]{2,1,0:T(8,128)(2,1)S(1)}, u32[]{:S(2)}, u32[]{:S(2)}) %collective-permute-start.12) | collective-permute-done | bytes 81952 | tf_op jit(solution)/shard_map/ppermute | solution.py:392
  33.1 0.5 collective-permute-done.11.mate
  33.5 2.9 %shard_map.96 = (bf16[64,32,128]{2,1,0:T(8,128)(2,1)S(1)}, bf16[100,32,128]{2,1,0:T(8,128)(2,1)S(1)}) custom-call(s32[192]{0:T(256)S(4)} %get-tuple-element.36.neighbour, bf16[64,32,128]{2,1,0:T(8,128)(2,1)S(1)} %get-tuple-element.39.x, bf16[8,32,128]{2,1,0:T(8,128)(2,1)S(1)} %collective-permute-done.6.from_near.near, ...), custom_call_target="tpu_custom_call" | custom-call | flops 268435456 | bytes 9437184 | tf_op jit(solution)/shard_map/pallas_call | solution.py:312
  36.4 0.0 collective-permute-done.10.rows3
  36.4 0.0 collective-permute-done.9.rows2
  36.4 0.0 collective-permute-done.8.rows1
  36.4 1.1 %shard_map.97 = (bf16[64,32,128]{2,1,0:T(8,128)(2,1)S(1)}, f32[64,32,128]{2,1,0:T(8,128)S(1)}, bf16[8,32,128]{2,1,0:T(8,128)(2,1)S(1)}, bf16[8,32,128]{2,1,0:T(8...) custom-call(s32[192]{0:T(256)S(4)} %get-tuple-element.36.neighbour, s32[1,1,4]{2,1,0:T(1,128)} %well.1, ...), custom_call_target="tpu_custom_call" | custom-call | tf_op jit(solution)/shard_map/pallas_call | solution.py:312
  37.6 2.0 %collective-permute-start.13 = (bf16[8,32,128]{2,1,0:T(8,128)(2,1)S(1)}, bf16[8,32,128]{2,1,0:T(8,128)(2,1)S(1)}, u32[]{:S(2)}, u32[]{:S(2)}) collective-permute-start(bf16[8,32,128]{2,1,0:T(8,128)(2,1)S(1)} %get-tuple-element.49), channel_id=1, source_target_pairs={{0,1},{1,0},{2,3},{3,2},{4,5},{5,4},{6,7},{7,6},{8,9},{9,8},{10,11... | collective-permute-start | bytes 196616 | tf_op jit(solution)/shard_map/ppermute | solution.py:348
  39.6 3.0 %collective-permute-start.14 = (bf16[8,32,128]{2,1,0:T(8,128)(2,1)S(1)}, bf16[8,32,128]{2,1,0:T(8,128)(2,1)S(1)}, u32[]{:S(2)}, u32[]{:S(2)}) collective-permute-start(bf16[8,32,128]{2,1,0:T(8,128)(2,1)S(1)} %get-tuple-element.50), channel_id=1, source_target_pairs={{0,4},{1,2},{2,1},{3,7},{4,0},{5,6},{6,5},{7,3},{8,12},{9,10},{10,... | collective-permute-start | bytes 196616 | tf_op jit(solution)/shard_map/ppermute | solution.py:347
  42.6 0.0 collective-permute-start.15
  42.6 3.9 %collective-permute-start.16 = (bf16[8,32,128]{2,1,0:T(8,128)(2,1)S(1)}, bf16[8,32,128]{2,1,0:T(8,128)(2,1)S(1)}, u32[]{:S(2)}, u32[]{:S(2)}) collective-permute-start(bf16[8,32,128]{2,1,0:T(8,128)(2,1)S(1)} %get-tuple-element.52), channel_id=1, source_target_pairs={{0,1},{1,0},{2,3},{3,2},{4,8},{5,9},{6,10},{7,11},{8,4},{9,5},{10,... | collective-permute-start | bytes 196616 | tf_op jit(solution)/shard_map/ppermute | solution.py:350
  46.6 0.0 collective-permute-done.13.refs_0_.from_near
  46.6 0.7 collective-permute-done.14.refs_1_.from_far
  47.2 0.1 collective-permute-start.17
  47.3 2.3 %collective-permute-start.18 = (bf16[2,32,128]{2,1,0:T(8,128)(2,1)S(1)}, bf16[2,32,128]{2,1,0:T(8,128)(2,1)S(1)}, u32[]{:S(2)}, u32[]{:S(2)}) collective-permute-start(bf16[2,32,128]{2,1,0:T(8,128)(2,1)S(1)} %get-tuple-element.57), channel_id=1, source_target_pairs={{0,1},{1,0},{2,3},{3,2},{4,8},{5,9},{6,10},{7,11},{8,4},{9,5},{10,... | collective-permute-start | bytes 49160 | tf_op jit(solution)/shard_map/ppermute | solution.py:355
  49.7 0.0 collective-permute-done.15.refs_2_
  49.7 1.9 %collective-permute-done.16.refs_3_ = bf16[8,32,128]{2,1,0:T(8,128)(2,1)S(1)} collective-permute-done((bf16[8,32,128]{2,1,0:T(8,128)(2,1)S(1)}, bf16[8,32,128]{2,1,0:T(8,128)(2,1)S(1)}, u32[]{:S(2)}, u32[]{:S(2)}) %collective-permute-start.16) | collective-permute-done | bytes 65568 | tf_op jit(solution)/shard_map/ppermute | solution.py:350
  51.6 2.7 %shard_map.98 = (bf16[64,32,128]{2,1,0:T(8,128)(2,1)S(1)}, bf16[100,32,128]{2,1,0:T(8,128)(2,1)S(1)}) custom-call(s32[192]{0:T(256)S(4)} %get-tuple-element.36.neighbour, bf16[64,32,128]{2,1,0:T(8,128)(2,1)S(1)} %get-tuple-element.48.x, bf16[8,32,128]{2,1,0:T(8,128)(2,1)S(1)} %collective-permute-done.13.refs_0_.from_near, ...), custom_call_target="tpu_custom_call" | custom-call | flops 268435456 | bytes 9437184 | tf_op jit(solution)/shard_map/pallas_call | solution.py:312
  54.3 0.0 collective-permute-done.17.mate
  54.3 0.0 collective-permute-done.18.other
  54.3 0.4 shard_map.100
  54.7 0.1 collective-permute-start.19
  54.8 4.1 %collective-permute-start.20 = (bf16[8,32,128]{2,1,0:T(8,128)(2,1)S(1)}, bf16[8,32,128]{2,1,0:T(8,128)(2,1)S(1)}, u32[]{:S(2)}, u32[]{:S(2)}) collective-permute-start(bf16[8,32,128]{2,1,0:T(8,128)(2,1)S(1)} %get-tuple-element.60), channel_id=1, source_target_pairs={{0,4},{1,2},{2,1},{3,7},{4,0},{5,6},{6,5},{7,3},{8,12},{9,10},{10,... | collective-permute-start | bytes 196616 | tf_op jit(solution)/shard_map/ppermute | solution.py:347
  58.9 0.0 collective-permute-start.21
  58.9 3.9 %collective-permute-start.22 = (bf16[8,32,128]{2,1,0:T(8,128)(2,1)S(1)}, bf16[8,32,128]{2,1,0:T(8,128)(2,1)S(1)}, u32[]{:S(2)}, u32[]{:S(2)}) collective-permute-start(bf16[8,32,128]{2,1,0:T(8,128)(2,1)S(1)} %get-tuple-element.62), channel_id=1, source_target_pairs={{0,1},{1,0},{2,3},{3,2},{4,8},{5,9},{6,10},{7,11},{8,4},{9,5},{10,... | collective-permute-start | bytes 196616 | tf_op jit(solution)/shard_map/ppermute | solution.py:350
  62.9 0.0 collective-permute-done.19.near.from_near
  62.9 0.0 collective-permute-done.20.far.from_far
  62.9 0.1 collective-permute-start.23
  63.0 2.0 %collective-permute-start.24 = (bf16[2,32,128]{2,1,0:T(8,128)(2,1)S(1)}, bf16[2,32,128]{2,1,0:T(8,128)(2,1)S(1)}, u32[]{:S(2)}, u32[]{:S(2)}) collective-permute-start(bf16[2,32,128]{2,1,0:T(8,128)(2,1)S(1)} %get-tuple-element.66), channel_id=1, source_target_pairs={{0,1},{1,0},{2,3},{3,2},{4,8},{5,9},{6,10},{7,11},{8,4},{9,5},{10,... | collective-permute-start | bytes 49160 | tf_op jit(solution)/shard_map/ppermute | solution.py:355
  65.0 0.0 collective-permute-done.21.mate
  65.0 2.9 %collective-permute-done.22.other = bf16[8,32,128]{2,1,0:T(8,128)(2,1)S(1)} collective-permute-done((bf16[8,32,128]{2,1,0:T(8,128)(2,1)S(1)}, bf16[8,32,128]{2,1,0:T(8,128)(2,1)S(1)}, u32[]{:S(2)}, u32[]{:S(2)}) %collective-permute-start.22) | collective-permute-done | bytes 65568 | tf_op jit(solution)/shard_map/ppermute | solution.py:350
  67.9 3.9 %shard_map.101 = (f32[32,64,128]{2,1,0:T(8,128)}, bf16[100,32,128]{2,1,0:T(8,128)(2,1)S(1)}) custom-call(s32[192]{0:T(256)S(4)} %get-tuple-element.36.neighbour, bf16[64,32,128]{2,1,0:T(8,128)(2,1)S(1)} %get-tuple-element.54.edges.x, bf16[4,32,128]{2,1,0:T(8,128)(2,1)S(1)} %get-tuple-element.58.corners, ...), custom_call_target="tpu_custom_call" | custom-call | flops 268435456 | bytes 9437184 | tf_op jit(solution)/shard_map/pallas_call | solution.py:312
  71.8 0.0 collective-permute-done.23.mate
  71.9 0.0 collective-permute-done.24.other
  71.9 1.0 %shard_map.103 = f32[32,64,128]{2,1,0:T(8,128)} custom-call(s32[192]{0:T(256)S(4)} %get-tuple-element.36.neighbour, f32[32,64,128]{2,1,0:T(8,128)} %get-tuple-element.63.partial, bf16[100,32,128]{2,1,0:T(8,128)(2,1)S(1)} %get-tuple-element.64.grid, bf16[2,32,128]{2,1,0:T(8,128)(2,1)S(1)} %collective-permute-done.23.mate, ...), custom_call_target="tpu_custom_call", output_to_operand_aliasing={{}: (1, {})} | custom-call | tf_op jit(solution)/shard_map/pallas_call | solution.py:312
  (5 shorter events, 0.1 us)
Async XLA Ops:
  1.7 19.4 %collective-permute-start.6 = (bf16[8,32,128]{2,1,0:T(8,128)(2,1)S(1)}, bf16[8,32,128]{2,1,0:T(8,128)(2,1)S(1)}, u32[]{:S(2)}, u32[]{:S(2)}) collective-permute-start(bf16[8,32,128]{2,1,0:T(8,128)(2,1)S(1)} %get-tuple-element.40), channel_id=1, source_target_pairs={{0,1},{1,0},{2,3},{3,2},{4,5},{5,4},{6,7},{7,6},{8,9},{9,8},{10,11... | collective-permute-start | bytes 196616 | tf_op jit(solution)/shard_map/ppermute | solution.py:386
  2.5 18.7 %collective-permute-start.7 = (bf16[8,32,128]{2,1,0:T(8,128)(2,1)S(1)}, bf16[8,32,128]{2,1,0:T(8,128)(2,1)S(1)}, u32[]{:S(2)}, u32[]{:S(2)}) collective-permute-start(bf16[8,32,128]{2,1,0:T(8,128)(2,1)S(1)} %get-tuple-element.41), channel_id=1, source_target_pairs={{0,4},{1,2},{2,1},{3,7},{4,0},{5,6},{6,5},{7,3},{8,12},{9,10},{10,... | collective-permute-start | bytes 196616 | tf_op jit(solution)/shard_map/ppermute | solution.py:385
  7.6 2.8 %collective-permute-start.2 = (bf16[1,32,128]{2,1,0:T(8,128)(2,1)S(1)}, bf16[1,32,128]{2,1,0:T(8,128)(2,1)S(1)}, u32[]{:S(2)}, u32[]{:S(2)}) collective-permute-start(bf16[1,32,128]{2,1,0:T(8,128)(2,1)S(1)} %get-tuple-element.37.part0), channel_id=1, source_target_pairs={{0,192},{4,196},{8,200},{12,204},{16,208},{20,212},{24,216},{28,22... | collective-permute-start | bytes 24584 | tf_op jit(solution)/shard_map/ppermute | solution.py:366
  8.3 3.4 %collective-permute-start.1 = (bf16[1,32,128]{2,1,0:T(8,128)(2,1)S(1)}, bf16[1,32,128]{2,1,0:T(8,128)(2,1)S(1)}, u32[]{:S(2)}, u32[]{:S(2)}) collective-permute-start(bf16[1,32,128]{2,1,0:T(8,128)(2,1)S(1)} %get-tuple-element.37.part0), channel_id=1, source_target_pairs={{0,128},{4,132},{8,136},{12,140},{16,144},{20,148},{24,152},{28,15... | collective-permute-start | bytes 24584 | tf_op jit(solution)/shard_map/ppermute | solution.py:366
  10.4 2.5 %collective-permute-start = (bf16[1,32,128]{2,1,0:T(8,128)(2,1)S(1)}, bf16[1,32,128]{2,1,0:T(8,128)(2,1)S(1)}, u32[]{:S(2)}, u32[]{:S(2)}) collective-permute-start(bf16[1,32,128]{2,1,0:T(8,128)(2,1)S(1)} %get-tuple-element.37.part0), channel_id=1, source_target_pairs={{0,64},{4,68},{8,72},{12,76},{16,80},{20,84},{24,88},{28,92},{32,9... | collective-permute-start | bytes 24584 | tf_op jit(solution)/shard_map/ppermute | solution.py:366
  12.9 8.3 %collective-permute-start.5 = (bf16[4,32,128]{2,1,0:T(8,128)(2,1)S(1)}, bf16[4,32,128]{2,1,0:T(8,128)(2,1)S(1)}, u32[]{:S(2)}, u32[]{:S(2)}) collective-permute-start(bf16[4,32,128]{2,1,0:T(8,128)(2,1)S(1)} %shard_map.93.part0), channel_id=1, source_target_pairs={{0,48},{4,52},{8,56},{12,60},{16,32},{20,36},{24,40},{28,44},{32,1... | collective-permute-start | bytes 98312 | tf_op jit(solution)/shard_map/ppermute | solution.py:366
  15.7 5.6 %collective-permute-start.4 = (bf16[4,32,128]{2,1,0:T(8,128)(2,1)S(1)}, bf16[4,32,128]{2,1,0:T(8,128)(2,1)S(1)}, u32[]{:S(2)}, u32[]{:S(2)}) collective-permute-start(bf16[4,32,128]{2,1,0:T(8,128)(2,1)S(1)} %shard_map.93.part0), channel_id=1, source_target_pairs={{0,32},{4,36},{8,40},{12,44},{16,48},{20,52},{24,56},{28,60},{32,0... | collective-permute-start | bytes 98312 | tf_op jit(solution)/shard_map/ppermute | solution.py:366
  16.0 5.3 %collective-permute-start.3 = (bf16[4,32,128]{2,1,0:T(8,128)(2,1)S(1)}, bf16[4,32,128]{2,1,0:T(8,128)(2,1)S(1)}, u32[]{:S(2)}, u32[]{:S(2)}) collective-permute-start(bf16[4,32,128]{2,1,0:T(8,128)(2,1)S(1)} %shard_map.93.part0), channel_id=1, source_target_pairs={{0,16},{4,20},{8,24},{12,28},{16,0},{20,4},{24,8},{28,12},{32,48},... | collective-permute-start | bytes 98312 | tf_op jit(solution)/shard_map/ppermute | solution.py:366
  21.3 15.1 %collective-permute-start.10 = (bf16[16,32,128]{2,1,0:T(8,128)(2,1)S(1)}, bf16[16,32,128]{2,1,0:T(8,128)(2,1)S(1)}, u32[]{:S(2)}, u32[]{:S(2)}) collective-permute-start(bf16[16,32,128]{2,1,0:T(8,128)(2,1)S(1)} %shard_map.95.rows0), channel_id=1, source_target_pairs={{0,12},{4,8},{8,4},{12,0},{16,28},{20,24},{24,20},{28,16},{32,44},... | collective-permute-start | bytes 393224 | tf_op jit(solution)/shard_map/ppermute | solution.py:366
  23.9 12.5 %collective-permute-start.9 = (bf16[16,32,128]{2,1,0:T(8,128)(2,1)S(1)}, bf16[16,32,128]{2,1,0:T(8,128)(2,1)S(1)}, u32[]{:S(2)}, u32[]{:S(2)}) collective-permute-start(bf16[16,32,128]{2,1,0:T(8,128)(2,1)S(1)} %shard_map.95.rows0), channel_id=1, source_target_pairs={{0,8},{4,12},{8,0},{12,4},{16,24},{20,28},{24,16},{28,20},{32,40},... | collective-permute-start | bytes 393224 | tf_op jit(solution)/shard_map/ppermute | solution.py:366
  24.4 12.0 %collective-permute-start.8 = (bf16[16,32,128]{2,1,0:T(8,128)(2,1)S(1)}, bf16[16,32,128]{2,1,0:T(8,128)(2,1)S(1)}, u32[]{:S(2)}, u32[]{:S(2)}) collective-permute-start(bf16[16,32,128]{2,1,0:T(8,128)(2,1)S(1)} %shard_map.95.rows0), channel_id=1, source_target_pairs={{0,4},{4,0},{8,12},{12,8},{16,20},{20,16},{24,28},{28,24},{32,36},... | collective-permute-start | bytes 393224 | tf_op jit(solution)/shard_map/ppermute | solution.py:366
  24.7 8.4 %collective-permute-start.12 = (bf16[10,32,128]{2,1,0:T(8,128)(2,1)S(1)}, bf16[10,32,128]{2,1,0:T(8,128)(2,1)S(1)}, u32[]{:S(2)}, u32[]{:S(2)}) collective-permute-start(bf16[10,32,128]{2,1,0:T(8,128)(2,1)S(1)} %get-tuple-element.43), channel_id=1, source_target_pairs={{0,1},{1,0},{2,3},{3,2},{4,8},{5,9},{6,10},{7,11},{8,4},{9,5},{10,... | collective-permute-start | bytes 245768 | tf_op jit(solution)/shard_map/ppermute | solution.py:392
  30.0 3.6 %collective-permute-start.11 = (bf16[10,32,128]{2,1,0:T(8,128)(2,1)S(1)}, bf16[10,32,128]{2,1,0:T(8,128)(2,1)S(1)}, u32[]{:S(2)}, u32[]{:S(2)}) collective-permute-start(bf16[10,32,128]{2,1,0:T(8,128)(2,1)S(1)} %get-tuple-element.42.after_and_whole_1_), channel_id=1, source_target_pairs={{0,4},{1,5},{2,6},{3,7},{4,0},{5,1},{6,2},{7,3},{8,12},{9,13},{10,... | collective-permute-start | bytes 245768 | tf_op jit(solution)/shard_map/ppermute | solution.py:392
  37.6 9.0 %collective-permute-start.13 = (bf16[8,32,128]{2,1,0:T(8,128)(2,1)S(1)}, bf16[8,32,128]{2,1,0:T(8,128)(2,1)S(1)}, u32[]{:S(2)}, u32[]{:S(2)}) collective-permute-start(bf16[8,32,128]{2,1,0:T(8,128)(2,1)S(1)} %get-tuple-element.49), channel_id=1, source_target_pairs={{0,1},{1,0},{2,3},{3,2},{4,5},{5,4},{6,7},{7,6},{8,9},{9,8},{10,11... | collective-permute-start | bytes 196616 | tf_op jit(solution)/shard_map/ppermute | solution.py:348
  39.6 7.6 %collective-permute-start.14 = (bf16[8,32,128]{2,1,0:T(8,128)(2,1)S(1)}, bf16[8,32,128]{2,1,0:T(8,128)(2,1)S(1)}, u32[]{:S(2)}, u32[]{:S(2)}) collective-permute-start(bf16[8,32,128]{2,1,0:T(8,128)(2,1)S(1)} %get-tuple-element.50), channel_id=1, source_target_pairs={{0,4},{1,2},{2,1},{3,7},{4,0},{5,6},{6,5},{7,3},{8,12},{9,10},{10,... | collective-permute-start | bytes 196616 | tf_op jit(solution)/shard_map/ppermute | solution.py:347
  42.6 7.1 %collective-permute-start.15 = (bf16[8,32,128]{2,1,0:T(8,128)(2,1)S(1)}, bf16[8,32,128]{2,1,0:T(8,128)(2,1)S(1)}, u32[]{:S(2)}, u32[]{:S(2)}) collective-permute-start(bf16[8,32,128]{2,1,0:T(8,128)(2,1)S(1)} %get-tuple-element.51), channel_id=1, source_target_pairs={{0,4},{1,5},{2,6},{3,7},{4,0},{5,1},{6,2},{7,3},{8,12},{9,13},{10,... | collective-permute-start | bytes 196616 | tf_op jit(solution)/shard_map/ppermute | solution.py:349
  42.6 9.0 %collective-permute-start.16 = (bf16[8,32,128]{2,1,0:T(8,128)(2,1)S(1)}, bf16[8,32,128]{2,1,0:T(8,128)(2,1)S(1)}, u32[]{:S(2)}, u32[]{:S(2)}) collective-permute-start(bf16[8,32,128]{2,1,0:T(8,128)(2,1)S(1)} %get-tuple-element.52), channel_id=1, source_target_pairs={{0,1},{1,0},{2,3},{3,2},{4,8},{5,9},{6,10},{7,11},{8,4},{9,5},{10,... | collective-permute-start | bytes 196616 | tf_op jit(solution)/shard_map/ppermute | solution.py:350
  47.2 7.1 %collective-permute-start.17 = (bf16[2,32,128]{2,1,0:T(8,128)(2,1)S(1)}, bf16[2,32,128]{2,1,0:T(8,128)(2,1)S(1)}, u32[]{:S(2)}, u32[]{:S(2)}) collective-permute-start(bf16[2,32,128]{2,1,0:T(8,128)(2,1)S(1)} %get-tuple-element.56), channel_id=1, source_target_pairs={{0,4},{1,5},{2,6},{3,7},{4,0},{5,1},{6,2},{7,3},{8,12},{9,13},{10,... | collective-permute-start | bytes 49160 | tf_op jit(solution)/shard_map/ppermute | solution.py:355
  47.3 7.0 %collective-permute-start.18 = (bf16[2,32,128]{2,1,0:T(8,128)(2,1)S(1)}, bf16[2,32,128]{2,1,0:T(8,128)(2,1)S(1)}, u32[]{:S(2)}, u32[]{:S(2)}) collective-permute-start(bf16[2,32,128]{2,1,0:T(8,128)(2,1)S(1)} %get-tuple-element.57), channel_id=1, source_target_pairs={{0,1},{1,0},{2,3},{3,2},{4,8},{5,9},{6,10},{7,11},{8,4},{9,5},{10,... | collective-permute-start | bytes 49160 | tf_op jit(solution)/shard_map/ppermute | solution.py:355
  54.7 8.2 %collective-permute-start.19 = (bf16[8,32,128]{2,1,0:T(8,128)(2,1)S(1)}, bf16[8,32,128]{2,1,0:T(8,128)(2,1)S(1)}, u32[]{:S(2)}, u32[]{:S(2)}) collective-permute-start(bf16[8,32,128]{2,1,0:T(8,128)(2,1)S(1)} %get-tuple-element.59), channel_id=1, source_target_pairs={{0,1},{1,0},{2,3},{3,2},{4,5},{5,4},{6,7},{7,6},{8,9},{9,8},{10,11... | collective-permute-start | bytes 196616 | tf_op jit(solution)/shard_map/ppermute | solution.py:348
  54.8 8.1 %collective-permute-start.20 = (bf16[8,32,128]{2,1,0:T(8,128)(2,1)S(1)}, bf16[8,32,128]{2,1,0:T(8,128)(2,1)S(1)}, u32[]{:S(2)}, u32[]{:S(2)}) collective-permute-start(bf16[8,32,128]{2,1,0:T(8,128)(2,1)S(1)} %get-tuple-element.60), channel_id=1, source_target_pairs={{0,4},{1,2},{2,1},{3,7},{4,0},{5,6},{6,5},{7,3},{8,12},{9,10},{10,... | collective-permute-start | bytes 196616 | tf_op jit(solution)/shard_map/ppermute | solution.py:347
  58.9 6.1 %collective-permute-start.21 = (bf16[8,32,128]{2,1,0:T(8,128)(2,1)S(1)}, bf16[8,32,128]{2,1,0:T(8,128)(2,1)S(1)}, u32[]{:S(2)}, u32[]{:S(2)}) collective-permute-start(bf16[8,32,128]{2,1,0:T(8,128)(2,1)S(1)} %get-tuple-element.61), channel_id=1, source_target_pairs={{0,4},{1,5},{2,6},{3,7},{4,0},{5,1},{6,2},{7,3},{8,12},{9,13},{10,... | collective-permute-start | bytes 196616 | tf_op jit(solution)/shard_map/ppermute | solution.py:349
  58.9 9.0 %collective-permute-start.22 = (bf16[8,32,128]{2,1,0:T(8,128)(2,1)S(1)}, bf16[8,32,128]{2,1,0:T(8,128)(2,1)S(1)}, u32[]{:S(2)}, u32[]{:S(2)}) collective-permute-start(bf16[8,32,128]{2,1,0:T(8,128)(2,1)S(1)} %get-tuple-element.62), channel_id=1, source_target_pairs={{0,1},{1,0},{2,3},{3,2},{4,8},{5,9},{6,10},{7,11},{8,4},{9,5},{10,... | collective-permute-start | bytes 196616 | tf_op jit(solution)/shard_map/ppermute | solution.py:350
  62.9 8.9 %collective-permute-start.23 = (bf16[2,32,128]{2,1,0:T(8,128)(2,1)S(1)}, bf16[2,32,128]{2,1,0:T(8,128)(2,1)S(1)}, u32[]{:S(2)}, u32[]{:S(2)}) collective-permute-start(bf16[2,32,128]{2,1,0:T(8,128)(2,1)S(1)} %get-tuple-element.65), channel_id=1, source_target_pairs={{0,4},{1,5},{2,6},{3,7},{4,0},{5,1},{6,2},{7,3},{8,12},{9,13},{10,... | collective-permute-start | bytes 49160 | tf_op jit(solution)/shard_map/ppermute | solution.py:355
  63.0 8.8 %collective-permute-start.24 = (bf16[2,32,128]{2,1,0:T(8,128)(2,1)S(1)}, bf16[2,32,128]{2,1,0:T(8,128)(2,1)S(1)}, u32[]{:S(2)}, u32[]{:S(2)}) collective-permute-start(bf16[2,32,128]{2,1,0:T(8,128)(2,1)S(1)} %get-tuple-element.66), channel_id=1, source_target_pairs={{0,1},{1,0},{2,3},{3,2},{4,8},{5,9},{6,10},{7,11},{8,4},{9,5},{10,... | collective-permute-start | bytes 49160 | tf_op jit(solution)/shard_map/ppermute | solution.py:355

commit v7 on v6

--- a/solution.py
+++ b/solution.py
@@ -385,11 +385,11 @@
     from_far = lax.ppermute(to_far, both, far_pairs)
     from_near = lax.ppermute(to_near, "slab", on_chip)
     to_mate, to_other = call(rows_to_send, [blocks(WIDE)] * 2, vmem(x, from_near, from_far))
-    (part,) = call(join, [blocks(4)], vmem(*swaps(part, 16)))
-    (part,) = call(join, [blocks(16)], vmem(*swaps(part, 4), weights[1], to_mate))
+    got = from_near, from_far, lax.ppermute(to_mate, both, mates), lax.ppermute(to_other, both, others)
+    (part,) = call(join, [blocks(4)], vmem(*swaps(part, 16), to_mate))
+    (part,) = call(join, [blocks(16)], vmem(*swaps(part, 4), weights[1], *got[2:]))
     rows = swaps(part, 1)
 
-    got = from_near, from_far, lax.ppermute(to_mate, both, mates), lax.ppermute(to_other, both, others)
 
     wells = [(SMEM_FROM_HBM, v) for v in (perf_well, injector_row, perf_block, perf_rate)]
     x, whole_grid = call(

time: 73.9 us -> 78.2 us (1.058)
  starting transfers between devices: 42.3 us -> 46 us
  waiting for transfers between devices: 11.5 us -> 12.9 us
    ppermute x2, starting transfers between devices: 7.9 us -> 1.28 us  [exchange(): from_other = lax.ppermute(to_other, both, others)]
    ppermute x2, starting transfers between devices: 7.14 us -> 12.6 us  [exchange(): from_far = lax.ppermute(to_far, both, far_pairs)]
    ppermute x2, starting transfers between devices: 4.36 us -> 7.68 us  [exchange_corners(): lax.ppermute(to_other, both, others)]
    ppermute x9, waiting for transfers between devices: 2.51 us -> 5.83 us  [swaps(): lax.ppermute(part, 'tile', [(t, t ^ m * step) for t in range(tiles)])]
    ppermute x1, waiting for transfers between devices: 3.11 us -> 0.01 us  [body(): lax.ppermute(to_other, both, others)]
    ppermute x1, waiting for transfers between devices: 0.01 us -> 2.54 us  [body(): from_far = lax.ppermute(to_far, both, far_pairs)]
    ppermute x2, waiting for transfers between devices: 4.77 us -> 3.03 us  [exchange(): from_other = lax.ppermute(to_other, both, others)]
    ppermute x2, starting transfers between devices: 2.12 us -> 0.54 us  [exchange(): from_near = lax.ppermute(to_near, 'slab', on_chip)]
  transfers between devices with their start and end apart: 25 -> 25, of which waited for: 7 -> 9; matrix products, arithmetic and copies ran while one was open for 1% -> 1% of each run, Pallas kernels for 19% -> 17%
where the time goes in v7:
time: 78.2 us; the launch traced here: 78.1 us
  starting transfers between devices  46 us (59%)
  Pallas kernels  17.8 us (23%)
  waiting for transfers between devices  12.9 us (16%)
  local copies, waits for them, and re-layouts  0.95 us (1%)
    pallas_call x13, Pallas kernels, call(): pl.pallas_call(kernel, out_shape=shapes, in_specs=[SMEM if isinstance(whe...  17.8 us
    ppermute x2, starting transfers between devices, exchange(): from_far = lax.ppermute(to_far, both, far_pairs)  12.6 us
    ppermute x9, starting transfers between devices, swaps(): lax.ppermute(part, 'tile', [(t, t ^ m * step) for t in range(tiles)])  10.8 us
    ppermute x2, starting transfers between devices, exchange_corners(): lax.ppermute(to_other, both, others)  7.68 us
    ppermute x9, waiting for transfers between devices, swaps(): lax.ppermute(part, 'tile', [(t, t ^ m * step) for t in range(tiles)])  5.83 us
    ppermute x1, starting transfers between devices, body(): from_far = lax.ppermute(to_far, both, far_pairs)  5.1 us
    ppermute x1, starting transfers between devices, body(): lax.ppermute(to_other, both, others)  4.87 us
    ppermute x2, waiting for transfers between devices, exchange(): from_other = lax.ppermute(to_other, both, others)  3.03 us
  transfers between devices with their start and end apart: 25, of which 9 were waited for; matrix products, arithmetic and copies ran while one was open for 1% of the time, Pallas kernels for 17%

profile of v7, /device:TPU:65, one launch (start us, length us, event | category | flops | bytes accessed | tf_op | source)
XLA Modules:
  0.0 78.1 jit_solution(17304659210273042619)
XLA Ops:
  0.0 1.7 %shard_map.92 = (bf16[64,32,128]{2,1,0:T(8,128)(2,1)S(1)}, f32[64,32,128]{2,1,0:T(8,128)S(1)}, bf16[8,32,128]{2,1,0:T(8,128)(2,1)S(1)}, bf16[8,32,128]{2,1,0:T(8,128)(2,1)S(1)}, bf16[1,32,128]{2,1,0:T(8,128)(2,1)S(1)}) custom-call(f32[32,64,128]{2,1,0:T(8,128)} %bitcast.6, f32[1,32,128]{2,1,0:T(8,128)} %stream.1), custom_call_target="tpu_custom_call" | custom-call | bytes 4194304 | tf_op jit(solution)/shard_map/pallas_call | solution.py:312
  1.7 0.8 collective-permute-start.3
  2.5 5.1 %collective-permute-start.4 = (bf16[8,32,128]{2,1,0:T(8,128)(2,1)S(1)}, bf16[8,32,128]{2,1,0:T(8,128)(2,1)S(1)}, u32[]{:S(2)}, u32[]{:S(2)}) collective-permute-start(bf16[8,32,128]{2,1,0:T(8,128)(2,1)S(1)} %get-tuple-element.40), channel_id=1, source_target_pairs={{0,4},{1,2},{2,1},{3,7},{4,0},{5,6},{6,5},{7,3},{8,12},{9,10},{10,... | collective-permute-start | bytes 196616 | tf_op jit(solution)/shard_map/ppermute | solution.py:385
  7.6 0.0 collective-permute-done.3.from_near.near
  7.6 2.5 %collective-permute-done.4.from_far.far = bf16[8,32,128]{2,1,0:T(8,128)(2,1)S(1)} collective-permute-done((bf16[8,32,128]{2,1,0:T(8,128)(2,1)S(1)}, bf16[8,32,128]{2,1,0:T(8,128)(2,1)S(1)}, u32[]{:S(2)}, u32[]{:S(2)}) %collective-permute-start.4) | collective-permute-done | bytes 65568 | tf_op jit(solution)/shard_map/ppermute | solution.py:385
  10.2 4.9 %collective-permute-start.9 = (bf16[10,32,128]{2,1,0:T(8,128)(2,1)S(1)}, bf16[10,32,128]{2,1,0:T(8,128)(2,1)S(1)}, u32[]{:S(2)}, u32[]{:S(2)}) collective-permute-start(bf16[10,32,128]{2,1,0:T(8,128)(2,1)S(1)} %get-tuple-element.43), channel_id=1, source_target_pairs={{0,1},{1,0},{2,3},{3,2},{4,8},{5,9},{6,10},{7,11},{8,4},{9,5},{10,... | collective-permute-start | bytes 245768 | tf_op jit(solution)/shard_map/ppermute | solution.py:388
  15.1 0.0 collective-permute-start.8
  15.1 0.8 %collective-permute-start.2 = (bf16[1,32,128]{2,1,0:T(8,128)(2,1)S(1)}, bf16[1,32,128]{2,1,0:T(8,128)(2,1)S(1)}, u32[]{:S(2)}, u32[]{:S(2)}) collective-permute-start(bf16[1,32,128]{2,1,0:T(8,128)(2,1)S(1)} %get-tuple-element.37.part0), channel_id=1, source_target_pairs={{0,192},{4,196},{8,200},{12,204},{16,208},{20,212},{24,216},{28,22... | collective-permute-start | bytes 24584 | tf_op jit(solution)/shard_map/ppermute | solution.py:366
  15.9 3.3 %collective-permute-start.1 = (bf16[1,32,128]{2,1,0:T(8,128)(2,1)S(1)}, bf16[1,32,128]{2,1,0:T(8,128)(2,1)S(1)}, u32[]{:S(2)}, u32[]{:S(2)}) collective-permute-start(bf16[1,32,128]{2,1,0:T(8,128)(2,1)S(1)} %get-tuple-element.37.part0), channel_id=1, source_target_pairs={{0,128},{4,132},{8,136},{12,140},{16,144},{20,148},{24,152},{28,15... | collective-permute-start | bytes 24584 | tf_op jit(solution)/shard_map/ppermute | solution.py:366
  19.2 0.0 collective-permute-start
  19.2 0.0 collective-permute-done.2.part3
  19.2 1.1 %collective-permute-done.1.part2 = bf16[1,32,128]{2,1,0:T(8,128)(2,1)S(1)} collective-permute-done((bf16[1,32,128]{2,1,0:T(8,128)(2,1)S(1)}, bf16[1,32,128]{2,1,0:T(8,128)(2,1)S(1)}, u32[]{:S(2)}, u32[]{:S(2)}) %collective-permute-start.1) | collective-permute-done | bytes 8224 | tf_op jit(solution)/shard_map/ppermute | solution.py:366
  20.4 1.4 %collective-permute-done.part1 = bf16[1,32,128]{2,1,0:T(8,128)(2,1)S(1)} collective-permute-done((bf16[1,32,128]{2,1,0:T(8,128)(2,1)S(1)}, bf16[1,32,128]{2,1,0:T(8,128)(2,1)S(1)}, u32[]{:S(2)}, u32[]{:S(2)}) %collective-permute-start) | collective-permute-done | bytes 8224 | tf_op jit(solution)/shard_map/ppermute | solution.py:366
  21.7 0.1 collective-permute-start.7
  21.9 0.1 collective-permute-start.6
  22.0 3.0 %collective-permute-start.5 = (bf16[4,32,128]{2,1,0:T(8,128)(2,1)S(1)}, bf16[4,32,128]{2,1,0:T(8,128)(2,1)S(1)}, u32[]{:S(2)}, u32[]{:S(2)}) collective-permute-start(bf16[4,32,128]{2,1,0:T(8,128)(2,1)S(1)} %shard_map.94.part0), channel_id=1, source_target_pairs={{0,16},{4,20},{8,24},{12,28},{16,0},{20,4},{24,8},{28,12},{32,48},... | collective-permute-start | bytes 98312 | tf_op jit(solution)/shard_map/ppermute | solution.py:366
  25.0 0.8 %copy.11 = s32[8,8,3]{2,1,0:T(8,128)S(1)} copy(s32[8,8,3]{1,0,2:T(8,128)} %param.12) | data formatting | bytes 1536 | tf_op args[3]
  25.8 0.1 reshape.15.neighbour_in
  26.0 4.0 %shard_map.91 = (bf16[64,3,128,128]{3,2,1,0:T(8,128)(2,1)S(1)}, bf16[64,128,128]{2,1,0:T(8,128)(2,1)S(1)}, s32[192]{0:T(256)S(4)}) custom-call(s32[192]{0:T(256)S(1)} %reshape.15.neighbour_in, bf16[64,3,128,128]{3,2,1,0:T(8,128)(2,1)} %bitcast.4, bf16[64,128,128]{2,1,0:T(8,128)(2,1)} %bitcast.5), custom_call_target="tpu_custom_call" | custom-call | bytes 8388608 | tf_op jit(solution)/shard_map/pallas_call | solution.py:312
  29.9 0.0 collective-permute-done.7.part3
  30.0 0.0 collective-permute-done.6.part2
  30.0 0.0 collective-permute-done.5.part1
  30.0 0.0 collective-permute-done.9.after_and_whole_2_.other
  30.0 0.0 collective-permute-done.8.after_and_whole_1_.mate
  30.0 0.1 collective-permute-start.12
  30.1 3.2 %collective-permute-start.11 = (bf16[16,32,128]{2,1,0:T(8,128)(2,1)S(1)}, bf16[16,32,128]{2,1,0:T(8,128)(2,1)S(1)}, u32[]{:S(2)}, u32[]{:S(2)}) collective-permute-start(bf16[16,32,128]{2,1,0:T(8,128)(2,1)S(1)} %shard_map.95.rows0), channel_id=1, source_target_pairs={{0,8},{4,12},{8,0},{12,4},{16,24},{20,28},{24,16},{28,20},{32,40},... | collective-permute-start | bytes 393224 | tf_op jit(solution)/shard_map/ppermute | solution.py:366
  33.4 0.0 collective-permute-start.10
  33.4 2.9 %shard_map.96 = (bf16[64,32,128]{2,1,0:T(8,128)(2,1)S(1)}, bf16[100,32,128]{2,1,0:T(8,128)(2,1)S(1)}) custom-call(s32[192]{0:T(256)S(4)} %get-tuple-element.36.neighbour, bf16[64,32,128]{2,1,0:T(8,128)(2,1)S(1)} %get-tuple-element.38.x, bf16[8,32,128]{2,1,0:T(8,128)(2,1)S(1)} %collective-permute-done.3.from_near.near, ...), custom_call_target="tpu_custom_call" | custom-call | flops 268435456 | bytes 9437184 | tf_op jit(solution)/shard_map/pallas_call | solution.py:312
  36.2 2.4 %collective-permute-done.12.rows3 = bf16[16,32,128]{2,1,0:T(8,128)(2,1)S(1)} collective-permute-done((bf16[16,32,128]{2,1,0:T(8,128)(2,1)S(1)}, bf16[16,32,128]{2,1,0:T(8,128)(2,1)S(1)}, u32[]{:S(2)}, u32[]{:S(2)}) %collective-permute-start.12) | collective-permute-done | bytes 131104 | tf_op jit(solution)/shard_map/ppermute | solution.py:366
  38.7 0.0 collective-permute-done.11.rows2
  38.7 0.9 %collective-permute-done.10.rows1 = bf16[16,32,128]{2,1,0:T(8,128)(2,1)S(1)} collective-permute-done((bf16[16,32,128]{2,1,0:T(8,128)(2,1)S(1)}, bf16[16,32,128]{2,1,0:T(8,128)(2,1)S(1)}, u32[]{:S(2)}, u32[]{:S(2)}) %collective-permute-start.10) | collective-permute-done | bytes 131104 | tf_op jit(solution)/shard_map/ppermute | solution.py:366
  39.6 1.1 %shard_map.97 = (bf16[64,32,128]{2,1,0:T(8,128)(2,1)S(1)}, f32[64,32,128]{2,1,0:T(8,128)S(1)}, bf16[8,32,128]{2,1,0:T(8,128)(2,1)S(1)}, bf16[8,32,128]{2,1,0:T(8...) custom-call(s32[192]{0:T(256)S(4)} %get-tuple-element.36.neighbour, s32[1,1,4]{2,1,0:T(1,128)} %well.1, ...), custom_call_target="tpu_custom_call" | custom-call | tf_op jit(solution)/shard_map/pallas_call | solution.py:312
  40.7 0.4 collective-permute-start.13
  41.1 6.6 %collective-permute-start.14 = (bf16[8,32,128]{2,1,0:T(8,128)(2,1)S(1)}, bf16[8,32,128]{2,1,0:T(8,128)(2,1)S(1)}, u32[]{:S(2)}, u32[]{:S(2)}) collective-permute-start(bf16[8,32,128]{2,1,0:T(8,128)(2,1)S(1)} %get-tuple-element.50), channel_id=1, source_target_pairs={{0,4},{1,2},{2,1},{3,7},{4,0},{5,6},{6,5},{7,3},{8,12},{9,10},{10,... | collective-permute-start | bytes 196616 | tf_op jit(solution)/shard_map/ppermute | solution.py:347
  47.8 1.1 %collective-permute-start.15 = (bf16[8,32,128]{2,1,0:T(8,128)(2,1)S(1)}, bf16[8,32,128]{2,1,0:T(8,128)(2,1)S(1)}, u32[]{:S(2)}, u32[]{:S(2)}) collective-permute-start(bf16[8,32,128]{2,1,0:T(8,128)(2,1)S(1)} %get-tuple-element.51), channel_id=1, source_target_pairs={{0,4},{1,5},{2,6},{3,7},{4,0},{5,1},{6,2},{7,3},{8,12},{9,13},{10,... | collective-permute-start | bytes 196616 | tf_op jit(solution)/shard_map/ppermute | solution.py:349
  48.9 0.5 collective-permute-start.16
  49.4 0.0 collective-permute-done.13.refs_0_.from_near
  49.4 0.3 collective-permute-done.14.refs_1_.from_far
  49.7 1.2 %collective-permute-start.17 = (bf16[2,32,128]{2,1,0:T(8,128)(2,1)S(1)}, bf16[2,32,128]{2,1,0:T(8,128)(2,1)S(1)}, u32[]{:S(2)}, u32[]{:S(2)}) collective-permute-start(bf16[2,32,128]{2,1,0:T(8,128)(2,1)S(1)} %get-tuple-element.56), channel_id=1, source_target_pairs={{0,4},{1,5},{2,6},{3,7},{4,0},{5,1},{6,2},{7,3},{8,12},{9,13},{10,... | collective-permute-start | bytes 49160 | tf_op jit(solution)/shard_map/ppermute | solution.py:355
  51.0 3.8 %collective-permute-start.18 = (bf16[2,32,128]{2,1,0:T(8,128)(2,1)S(1)}, bf16[2,32,128]{2,1,0:T(8,128)(2,1)S(1)}, u32[]{:S(2)}, u32[]{:S(2)}) collective-permute-start(bf16[2,32,128]{2,1,0:T(8,128)(2,1)S(1)} %get-tuple-element.57), channel_id=1, source_target_pairs={{0,1},{1,0},{2,3},{3,2},{4,8},{5,9},{6,10},{7,11},{8,4},{9,5},{10,... | collective-permute-start | bytes 49160 | tf_op jit(solution)/shard_map/ppermute | solution.py:355
  54.8 0.0 collective-permute-done.15.refs_2_
  54.8 1.4 %collective-permute-done.16.refs_3_ = bf16[8,32,128]{2,1,0:T(8,128)(2,1)S(1)} collective-permute-done((bf16[8,32,128]{2,1,0:T(8,128)(2,1)S(1)}, bf16[8,32,128]{2,1,0:T(8,128)(2,1)S(1)}, u32[]{:S(2)}, u32[]{:S(2)}) %collective-permute-start.16) | collective-permute-done | bytes 65568 | tf_op jit(solution)/shard_map/ppermute | solution.py:350
  56.2 2.7 %shard_map.98 = (bf16[64,32,128]{2,1,0:T(8,128)(2,1)S(1)}, bf16[100,32,128]{2,1,0:T(8,128)(2,1)S(1)}) custom-call(s32[192]{0:T(256)S(4)} %get-tuple-element.36.neighbour, bf16[64,32,128]{2,1,0:T(8,128)(2,1)S(1)} %get-tuple-element.48.x, bf16[8,32,128]{2,1,0:T(8,128)(2,1)S(1)} %collective-permute-done.13.refs_0_.from_near, ...), custom_call_target="tpu_custom_call" | custom-call | flops 268435456 | bytes 9437184 | tf_op jit(solution)/shard_map/pallas_call | solution.py:312
  58.9 0.0 collective-permute-done.17.mate
  58.9 0.0 collective-permute-done.18.other
  58.9 0.4 shard_map.100
  59.3 0.1 collective-permute-start.19
  59.4 6.0 %collective-permute-start.20 = (bf16[8,32,128]{2,1,0:T(8,128)(2,1)S(1)}, bf16[8,32,128]{2,1,0:T(8,128)(2,1)S(1)}, u32[]{:S(2)}, u32[]{:S(2)}) collective-permute-start(bf16[8,32,128]{2,1,0:T(8,128)(2,1)S(1)} %get-tuple-element.60), channel_id=1, source_target_pairs={{0,4},{1,2},{2,1},{3,7},{4,0},{5,6},{6,5},{7,3},{8,12},{9,10},{10,... | collective-permute-start | bytes 196616 | tf_op jit(solution)/shard_map/ppermute | solution.py:347
  65.4 0.0 collective-permute-start.21
  65.4 0.7 collective-permute-start.22
  66.1 0.0 collective-permute-done.19.near.from_near
  66.1 1.2 %collective-permute-done.20.far.from_far = bf16[8,32,128]{2,1,0:T(8,128)(2,1)S(1)} collective-permute-done((bf16[8,32,128]{2,1,0:T(8,128)(2,1)S(1)}, bf16[8,32,128]{2,1,0:T(8,128)(2,1)S(1)}, u32[]{:S(2)}, u32[]{:S(2)}) %collective-permute-start.20) | collective-permute-done | bytes 65568 | tf_op jit(solution)/shard_map/ppermute | solution.py:347
  67.4 0.1 collective-permute-start.23
  67.5 3.8 %collective-permute-start.24 = (bf16[2,32,128]{2,1,0:T(8,128)(2,1)S(1)}, bf16[2,32,128]{2,1,0:T(8,128)(2,1)S(1)}, u32[]{:S(2)}, u32[]{:S(2)}) collective-permute-start(bf16[2,32,128]{2,1,0:T(8,128)(2,1)S(1)} %get-tuple-element.66), channel_id=1, source_target_pairs={{0,1},{1,0},{2,3},{3,2},{4,8},{5,9},{6,10},{7,11},{8,4},{9,5},{10,... | collective-permute-start | bytes 49160 | tf_op jit(solution)/shard_map/ppermute | solution.py:355
  71.3 0.0 collective-permute-done.21.mate
  71.3 1.6 %collective-permute-done.22.other = bf16[8,32,128]{2,1,0:T(8,128)(2,1)S(1)} collective-permute-done((bf16[8,32,128]{2,1,0:T(8,128)(2,1)S(1)}, bf16[8,32,128]{2,1,0:T(8,128)(2,1)S(1)}, u32[]{:S(2)}, u32[]{:S(2)}) %collective-permute-start.22) | collective-permute-done | bytes 65568 | tf_op jit(solution)/shard_map/ppermute | solution.py:350
  72.9 3.9 %shard_map.101 = (f32[32,64,128]{2,1,0:T(8,128)}, bf16[100,32,128]{2,1,0:T(8,128)(2,1)S(1)}) custom-call(s32[192]{0:T(256)S(4)} %get-tuple-element.36.neighbour, bf16[64,32,128]{2,1,0:T(8,128)(2,1)S(1)} %get-tuple-element.54.edges.x, bf16[4,32,128]{2,1,0:T(8,128)(2,1)S(1)} %get-tuple-element.58.corners, ...), custom_call_target="tpu_custom_call" | custom-call | flops 268435456 | bytes 9437184 | tf_op jit(solution)/shard_map/pallas_call | solution.py:312
  76.9 0.0 collective-permute-done.23.mate
  76.9 0.0 collective-permute-done.24.other
  76.9 1.0 %shard_map.103 = f32[32,64,128]{2,1,0:T(8,128)} custom-call(s32[192]{0:T(256)S(4)} %get-tuple-element.36.neighbour, f32[32,64,128]{2,1,0:T(8,128)} %get-tuple-element.63.partial, bf16[100,32,128]{2,1,0:T(8,128)(2,1)S(1)} %get-tuple-element.64.grid, bf16[2,32,128]{2,1,0:T(8,128)(2,1)S(1)} %collective-permute-done.23.mate, ...), custom_call_target="tpu_custom_call", output_to_operand_aliasing={{}: (1, {})} | custom-call | tf_op jit(solution)/shard_map/pallas_call | solution.py:312
  (5 shorter events, 0.1 us)
Async XLA Ops:
  1.7 5.9 %collective-permute-start.3 = (bf16[8,32,128]{2,1,0:T(8,128)(2,1)S(1)}, bf16[8,32,128]{2,1,0:T(8,128)(2,1)S(1)}, u32[]{:S(2)}, u32[]{:S(2)}) collective-permute-start(bf16[8,32,128]{2,1,0:T(8,128)(2,1)S(1)} %get-tuple-element.39), channel_id=1, source_target_pairs={{0,1},{1,0},{2,3},{3,2},{4,5},{5,4},{6,7},{7,6},{8,9},{9,8},{10,11... | collective-permute-start | bytes 196616 | tf_op jit(solution)/shard_map/ppermute | solution.py:386
  2.5 7.6 %collective-permute-start.4 = (bf16[8,32,128]{2,1,0:T(8,128)(2,1)S(1)}, bf16[8,32,128]{2,1,0:T(8,128)(2,1)S(1)}, u32[]{:S(2)}, u32[]{:S(2)}) collective-permute-start(bf16[8,32,128]{2,1,0:T(8,128)(2,1)S(1)} %get-tuple-element.40), channel_id=1, source_target_pairs={{0,4},{1,2},{2,1},{3,7},{4,0},{5,6},{6,5},{7,3},{8,12},{9,10},{10,... | collective-permute-start | bytes 196616 | tf_op jit(solution)/shard_map/ppermute | solution.py:385
  10.2 19.8 %collective-permute-start.9 = (bf16[10,32,128]{2,1,0:T(8,128)(2,1)S(1)}, bf16[10,32,128]{2,1,0:T(8,128)(2,1)S(1)}, u32[]{:S(2)}, u32[]{:S(2)}) collective-permute-start(bf16[10,32,128]{2,1,0:T(8,128)(2,1)S(1)} %get-tuple-element.43), channel_id=1, source_target_pairs={{0,1},{1,0},{2,3},{3,2},{4,8},{5,9},{6,10},{7,11},{8,4},{9,5},{10,... | collective-permute-start | bytes 245768 | tf_op jit(solution)/shard_map/ppermute | solution.py:388
  15.1 14.9 %collective-permute-start.8 = (bf16[10,32,128]{2,1,0:T(8,128)(2,1)S(1)}, bf16[10,32,128]{2,1,0:T(8,128)(2,1)S(1)}, u32[]{:S(2)}, u32[]{:S(2)}) collective-permute-start(bf16[10,32,128]{2,1,0:T(8,128)(2,1)S(1)} %get-tuple-element.41.after_and_whole_0_), channel_id=1, source_target_pairs={{0,4},{1,5},{2,6},{3,7},{4,0},{5,1},{6,2},{7,3},{8,12},{9,13},{10,... | collective-permute-start | bytes 245768 | tf_op jit(solution)/shard_map/ppermute | solution.py:388
  15.1 4.2 %collective-permute-start.2 = (bf16[1,32,128]{2,1,0:T(8,128)(2,1)S(1)}, bf16[1,32,128]{2,1,0:T(8,128)(2,1)S(1)}, u32[]{:S(2)}, u32[]{:S(2)}) collective-permute-start(bf16[1,32,128]{2,1,0:T(8,128)(2,1)S(1)} %get-tuple-element.37.part0), channel_id=1, source_target_pairs={{0,192},{4,196},{8,200},{12,204},{16,208},{20,212},{24,216},{28,22... | collective-permute-start | bytes 24584 | tf_op jit(solution)/shard_map/ppermute | solution.py:366
  15.9 4.5 %collective-permute-start.1 = (bf16[1,32,128]{2,1,0:T(8,128)(2,1)S(1)}, bf16[1,32,128]{2,1,0:T(8,128)(2,1)S(1)}, u32[]{:S(2)}, u32[]{:S(2)}) collective-permute-start(bf16[1,32,128]{2,1,0:T(8,128)(2,1)S(1)} %get-tuple-element.37.part0), channel_id=1, source_target_pairs={{0,128},{4,132},{8,136},{12,140},{16,144},{20,148},{24,152},{28,15... | collective-permute-start | bytes 24584 | tf_op jit(solution)/shard_map/ppermute | solution.py:366
  19.2 2.5 %collective-permute-start = (bf16[1,32,128]{2,1,0:T(8,128)(2,1)S(1)}, bf16[1,32,128]{2,1,0:T(8,128)(2,1)S(1)}, u32[]{:S(2)}, u32[]{:S(2)}) collective-permute-start(bf16[1,32,128]{2,1,0:T(8,128)(2,1)S(1)} %get-tuple-element.37.part0), channel_id=1, source_target_pairs={{0,64},{4,68},{8,72},{12,76},{16,80},{20,84},{24,88},{28,92},{32,9... | collective-permute-start | bytes 24584 | tf_op jit(solution)/shard_map/ppermute | solution.py:366
  21.7 8.2 %collective-permute-start.7 = (bf16[4,32,128]{2,1,0:T(8,128)(2,1)S(1)}, bf16[4,32,128]{2,1,0:T(8,128)(2,1)S(1)}, u32[]{:S(2)}, u32[]{:S(2)}) collective-permute-start(bf16[4,32,128]{2,1,0:T(8,128)(2,1)S(1)} %shard_map.94.part0), channel_id=1, source_target_pairs={{0,48},{4,52},{8,56},{12,60},{16,32},{20,36},{24,40},{28,44},{32,1... | collective-permute-start | bytes 98312 | tf_op jit(solution)/shard_map/ppermute | solution.py:366
  21.9 8.1 %collective-permute-start.6 = (bf16[4,32,128]{2,1,0:T(8,128)(2,1)S(1)}, bf16[4,32,128]{2,1,0:T(8,128)(2,1)S(1)}, u32[]{:S(2)}, u32[]{:S(2)}) collective-permute-start(bf16[4,32,128]{2,1,0:T(8,128)(2,1)S(1)} %shard_map.94.part0), channel_id=1, source_target_pairs={{0,32},{4,36},{8,40},{12,44},{16,48},{20,52},{24,56},{28,60},{32,0... | collective-permute-start | bytes 98312 | tf_op jit(solution)/shard_map/ppermute | solution.py:366
  22.0 8.0 %collective-permute-start.5 = (bf16[4,32,128]{2,1,0:T(8,128)(2,1)S(1)}, bf16[4,32,128]{2,1,0:T(8,128)(2,1)S(1)}, u32[]{:S(2)}, u32[]{:S(2)}) collective-permute-start(bf16[4,32,128]{2,1,0:T(8,128)(2,1)S(1)} %shard_map.94.part0), channel_id=1, source_target_pairs={{0,16},{4,20},{8,24},{12,28},{16,0},{20,4},{24,8},{28,12},{32,48},... | collective-permute-start | bytes 98312 | tf_op jit(solution)/shard_map/ppermute | solution.py:366
  30.0 8.6 %collective-permute-start.12 = (bf16[16,32,128]{2,1,0:T(8,128)(2,1)S(1)}, bf16[16,32,128]{2,1,0:T(8,128)(2,1)S(1)}, u32[]{:S(2)}, u32[]{:S(2)}) collective-permute-start(bf16[16,32,128]{2,1,0:T(8,128)(2,1)S(1)} %shard_map.95.rows0), channel_id=1, source_target_pairs={{0,12},{4,8},{8,4},{12,0},{16,28},{20,24},{24,20},{28,16},{32,44},... | collective-permute-start | bytes 393224 | tf_op jit(solution)/shard_map/ppermute | solution.py:366
  30.1 8.5 %collective-permute-start.11 = (bf16[16,32,128]{2,1,0:T(8,128)(2,1)S(1)}, bf16[16,32,128]{2,1,0:T(8,128)(2,1)S(1)}, u32[]{:S(2)}, u32[]{:S(2)}) collective-permute-start(bf16[16,32,128]{2,1,0:T(8,128)(2,1)S(1)} %shard_map.95.rows0), channel_id=1, source_target_pairs={{0,8},{4,12},{8,0},{12,4},{16,24},{20,28},{24,16},{28,20},{32,40},... | collective-permute-start | bytes 393224 | tf_op jit(solution)/shard_map/ppermute | solution.py:366
  33.4 6.2 %collective-permute-start.10 = (bf16[16,32,128]{2,1,0:T(8,128)(2,1)S(1)}, bf16[16,32,128]{2,1,0:T(8,128)(2,1)S(1)}, u32[]{:S(2)}, u32[]{:S(2)}) collective-permute-start(bf16[16,32,128]{2,1,0:T(8,128)(2,1)S(1)} %shard_map.95.rows0), channel_id=1, source_target_pairs={{0,4},{4,0},{8,12},{12,8},{16,20},{20,16},{24,28},{28,24},{32,36},... | collective-permute-start | bytes 393224 | tf_op jit(solution)/shard_map/ppermute | solution.py:366
  40.7 8.8 %collective-permute-start.13 = (bf16[8,32,128]{2,1,0:T(8,128)(2,1)S(1)}, bf16[8,32,128]{2,1,0:T(8,128)(2,1)S(1)}, u32[]{:S(2)}, u32[]{:S(2)}) collective-permute-start(bf16[8,32,128]{2,1,0:T(8,128)(2,1)S(1)} %get-tuple-element.49), channel_id=1, source_target_pairs={{0,1},{1,0},{2,3},{3,2},{4,5},{5,4},{6,7},{7,6},{8,9},{9,8},{10,11... | collective-permute-start | bytes 196616 | tf_op jit(solution)/shard_map/ppermute | solution.py:348
  41.1 8.6 %collective-permute-start.14 = (bf16[8,32,128]{2,1,0:T(8,128)(2,1)S(1)}, bf16[8,32,128]{2,1,0:T(8,128)(2,1)S(1)}, u32[]{:S(2)}, u32[]{:S(2)}) collective-permute-start(bf16[8,32,128]{2,1,0:T(8,128)(2,1)S(1)} %get-tuple-element.50), channel_id=1, source_target_pairs={{0,4},{1,2},{2,1},{3,7},{4,0},{5,6},{6,5},{7,3},{8,12},{9,10},{10,... | collective-permute-start | bytes 196616 | tf_op jit(solution)/shard_map/ppermute | solution.py:347
  47.8 7.0 %collective-permute-start.15 = (bf16[8,32,128]{2,1,0:T(8,128)(2,1)S(1)}, bf16[8,32,128]{2,1,0:T(8,128)(2,1)S(1)}, u32[]{:S(2)}, u32[]{:S(2)}) collective-permute-start(bf16[8,32,128]{2,1,0:T(8,128)(2,1)S(1)} %get-tuple-element.51), channel_id=1, source_target_pairs={{0,4},{1,5},{2,6},{3,7},{4,0},{5,1},{6,2},{7,3},{8,12},{9,13},{10,... | collective-permute-start | bytes 196616 | tf_op jit(solution)/shard_map/ppermute | solution.py:349
  48.9 7.3 %collective-permute-start.16 = (bf16[8,32,128]{2,1,0:T(8,128)(2,1)S(1)}, bf16[8,32,128]{2,1,0:T(8,128)(2,1)S(1)}, u32[]{:S(2)}, u32[]{:S(2)}) collective-permute-start(bf16[8,32,128]{2,1,0:T(8,128)(2,1)S(1)} %get-tuple-element.52), channel_id=1, source_target_pairs={{0,1},{1,0},{2,3},{3,2},{4,8},{5,9},{6,10},{7,11},{8,4},{9,5},{10,... | collective-permute-start | bytes 196616 | tf_op jit(solution)/shard_map/ppermute | solution.py:350
  49.7 9.2 %collective-permute-start.17 = (bf16[2,32,128]{2,1,0:T(8,128)(2,1)S(1)}, bf16[2,32,128]{2,1,0:T(8,128)(2,1)S(1)}, u32[]{:S(2)}, u32[]{:S(2)}) collective-permute-start(bf16[2,32,128]{2,1,0:T(8,128)(2,1)S(1)} %get-tuple-element.56), channel_id=1, source_target_pairs={{0,4},{1,5},{2,6},{3,7},{4,0},{5,1},{6,2},{7,3},{8,12},{9,13},{10,... | collective-permute-start | bytes 49160 | tf_op jit(solution)/shard_map/ppermute | solution.py:355
  51.0 8.0 %collective-permute-start.18 = (bf16[2,32,128]{2,1,0:T(8,128)(2,1)S(1)}, bf16[2,32,128]{2,1,0:T(8,128)(2,1)S(1)}, u32[]{:S(2)}, u32[]{:S(2)}) collective-permute-start(bf16[2,32,128]{2,1,0:T(8,128)(2,1)S(1)} %get-tuple-element.57), channel_id=1, source_target_pairs={{0,1},{1,0},{2,3},{3,2},{4,8},{5,9},{6,10},{7,11},{8,4},{9,5},{10,... | collective-permute-start | bytes 49160 | tf_op jit(solution)/shard_map/ppermute | solution.py:355
  59.3 6.8 %collective-permute-start.19 = (bf16[8,32,128]{2,1,0:T(8,128)(2,1)S(1)}, bf16[8,32,128]{2,1,0:T(8,128)(2,1)S(1)}, u32[]{:S(2)}, u32[]{:S(2)}) collective-permute-start(bf16[8,32,128]{2,1,0:T(8,128)(2,1)S(1)} %get-tuple-element.59), channel_id=1, source_target_pairs={{0,1},{1,0},{2,3},{3,2},{4,5},{5,4},{6,7},{7,6},{8,9},{9,8},{10,11... | collective-permute-start | bytes 196616 | tf_op jit(solution)/shard_map/ppermute | solution.py:348
  59.4 7.9 %collective-permute-start.20 = (bf16[8,32,128]{2,1,0:T(8,128)(2,1)S(1)}, bf16[8,32,128]{2,1,0:T(8,128)(2,1)S(1)}, u32[]{:S(2)}, u32[]{:S(2)}) collective-permute-start(bf16[8,32,128]{2,1,0:T(8,128)(2,1)S(1)} %get-tuple-element.60), channel_id=1, source_target_pairs={{0,4},{1,2},{2,1},{3,7},{4,0},{5,6},{6,5},{7,3},{8,12},{9,10},{10,... | collective-permute-start | bytes 196616 | tf_op jit(solution)/shard_map/ppermute | solution.py:347
  65.4 5.9 %collective-permute-start.21 = (bf16[8,32,128]{2,1,0:T(8,128)(2,1)S(1)}, bf16[8,32,128]{2,1,0:T(8,128)(2,1)S(1)}, u32[]{:S(2)}, u32[]{:S(2)}) collective-permute-start(bf16[8,32,128]{2,1,0:T(8,128)(2,1)S(1)} %get-tuple-element.61), channel_id=1, source_target_pairs={{0,4},{1,5},{2,6},{3,7},{4,0},{5,1},{6,2},{7,3},{8,12},{9,13},{10,... | collective-permute-start | bytes 196616 | tf_op jit(solution)/shard_map/ppermute | solution.py:349
  65.4 7.5 %collective-permute-start.22 = (bf16[8,32,128]{2,1,0:T(8,128)(2,1)S(1)}, bf16[8,32,128]{2,1,0:T(8,128)(2,1)S(1)}, u32[]{:S(2)}, u32[]{:S(2)}) collective-permute-start(bf16[8,32,128]{2,1,0:T(8,128)(2,1)S(1)} %get-tuple-element.62), channel_id=1, source_target_pairs={{0,1},{1,0},{2,3},{3,2},{4,8},{5,9},{6,10},{7,11},{8,4},{9,5},{10,... | collective-permute-start | bytes 196616 | tf_op jit(solution)/shard_map/ppermute | solution.py:350
  67.4 9.5 %collective-permute-start.23 = (bf16[2,32,128]{2,1,0:T(8,128)(2,1)S(1)}, bf16[2,32,128]{2,1,0:T(8,128)(2,1)S(1)}, u32[]{:S(2)}, u32[]{:S(2)}) collective-permute-start(bf16[2,32,128]{2,1,0:T(8,128)(2,1)S(1)} %get-tuple-element.65), channel_id=1, source_target_pairs={{0,4},{1,5},{2,6},{3,7},{4,0},{5,1},{6,2},{7,3},{8,12},{9,13},{10,... | collective-permute-start | bytes 49160 | tf_op jit(solution)/shard_map/ppermute | solution.py:355
  67.5 9.4 %collective-permute-start.24 = (bf16[2,32,128]{2,1,0:T(8,128)(2,1)S(1)}, bf16[2,32,128]{2,1,0:T(8,128)(2,1)S(1)}, u32[]{:S(2)}, u32[]{:S(2)}) collective-permute-start(bf16[2,32,128]{2,1,0:T(8,128)(2,1)S(1)} %get-tuple-element.66), channel_id=1, source_target_pairs={{0,1},{1,0},{2,3},{3,2},{4,8},{5,9},{6,10},{7,11},{8,4},{9,5},{10,... | collective-permute-start | bytes 49160 | tf_op jit(solution)/shard_map/ppermute | solution.py:355

commit v8 on v7

--- a/solution.py
+++ b/solution.py
@@ -91,7 +91,8 @@
     row[...] = held_row[...].astype(BF16)
 
 
-def rows_to_send(x, from_near, from_far, to_mate, to_other):
+def rows_to_send(x, from_near, from_far, after, to_mate, to_other):
+    del after
     right, even = parity() == 0, even_tile()
     real = far_is_real()
     rows = []
@@ -165,7 +166,8 @@
     return row.astype(F32)
 
 
-def load(neighbour_in, upwind_far, diag_far, upwind, diag, neighbour, sems):
+def load(neighbour_in, after, upwind_far, diag_far, upwind, diag, neighbour, sems):
+    del after
     copies = [
         pltpu.make_async_copy(upwind_far, upwind, sems.at[0]),
         pltpu.make_async_copy(diag_far, diag, sems.at[1]),
@@ -374,21 +376,21 @@
     )
     upwind_shape = jax.ShapeDtypeStruct((64, 3, 128, 128), BF16)
     diag_shape = jax.ShapeDtypeStruct((64, 128, 128), BF16)
+    from_far = lax.ppermute(to_far, both, far_pairs)
+    from_near = lax.ppermute(to_near, "slab", on_chip)
+    (part,) = call(join, [blocks(4)], vmem(*swaps(part, 16)))
+    to_mate, to_other = call(rows_to_send, [blocks(WIDE)] * 2, vmem(x, from_near, from_far, part))
+    got = from_near, from_far, lax.ppermute(to_mate, both, mates), lax.ppermute(to_other, both, others)
+    (part,) = call(join, [blocks(16)], vmem(*swaps(part, 4), *got[2:]))
+    rows = swaps(part, 1)
     *weights, neighbour_here = call(
         load,
         [(VMEM, upwind_shape), (VMEM, diag_shape), (SMEM, jax.ShapeDtypeStruct((192,), jnp.int32))],
-        [neighbour, (HBM, upwind.reshape(upwind_shape.shape)), (HBM, diag_inverse.reshape(diag_shape.shape))],
+        [neighbour, (VMEM, part), (HBM, upwind.reshape(upwind_shape.shape)), (HBM, diag_inverse.reshape(diag_shape.shape))],
         [dma((2,))],
         moved=8 * 2**20,
     )
     neighbour = (SMEM_KEPT, neighbour_here)
-    from_far = lax.ppermute(to_far, both, far_pairs)
-    from_near = lax.ppermute(to_near, "slab", on_chip)
-    to_mate, to_other = call(rows_to_send, [blocks(WIDE)] * 2, vmem(x, from_near, from_far))
-    got = from_near, from_far, lax.ppermute(to_mate, both, mates), lax.ppermute(to_other, both, others)
-    (part,) = call(join, [blocks(4)], vmem(*swaps(part, 16), to_mate))
-    (part,) = call(join, [blocks(16)], vmem(*swaps(part, 4), weights[1], *got[2:]))
-    rows = swaps(part, 1)
 
 
     wells = [(SMEM_FROM_HBM, v) for v in (perf_well, injector_row, perf_block, perf_rate)]

time: 78.2 us -> 72.2 us (0.923)
  waiting for transfers between devices: 12.9 us -> 6.92 us
    ppermute x2, starting transfers between devices: 1.28 us -> 5.58 us  [exchange(): from_other = lax.ppermute(to_other, both, others)]
    ppermute x1, waiting for transfers between devices: 2.54 us -> 0.01 us  [body(): from_far = lax.ppermute(to_far, both, far_pairs)]
    ppermute x2, starting transfers between devices: 12.6 us -> 10.5 us  [exchange(): from_far = lax.ppermute(to_far, both, far_pairs)]
    ppermute x9, waiting for transfers between devices: 5.83 us -> 4.19 us  [swaps(): lax.ppermute(part, 'tile', [(t, t ^ m * step) for t in range(tiles)])]
    ppermute x9, starting transfers between devices: 10.8 us -> 9.41 us  [swaps(): lax.ppermute(part, 'tile', [(t, t ^ m * step) for t in range(tiles)])]
    ppermute x2, waiting for transfers between devices: 1.5 us -> 0.19 us  [exchange(): from_far = lax.ppermute(to_far, both, far_pairs)]
    ppermute x1, starting transfers between devices: 0.01 us -> 1.3 us  [body(): lax.ppermute(to_mate, both, mates)]
    ppermute x2, starting transfers between devices: 1.3 us -> 0.19 us  [exchange_corners(): lax.ppermute(to_mate, both, mates)]
  transfers between devices with their start and end apart: 25 -> 25, of which waited for: 9 -> 9; matrix products, arithmetic and copies ran while one was open for 1% -> 1% of each run, Pallas kernels for 17% -> 19%
where the time goes in v8:
time: 72.2 us; the launch traced here: 72 us
  starting transfers between devices  46 us (64%)
  Pallas kernels  17.8 us (25%)
  waiting for transfers between devices  6.92 us (10%)
  local copies, waits for them, and re-layouts  0.95 us (1%)
    pallas_call x13, Pallas kernels, call(): pl.pallas_call(kernel, out_shape=shapes, in_specs=[SMEM if isinstance(whe...  17.8 us
    ppermute x2, starting transfers between devices, exchange(): from_far = lax.ppermute(to_far, both, far_pairs)  10.5 us
    ppermute x9, starting transfers between devices, swaps(): lax.ppermute(part, 'tile', [(t, t ^ m * step) for t in range(tiles)])  9.41 us
    ppermute x2, starting transfers between devices, exchange_corners(): lax.ppermute(to_other, both, others)  6.82 us
    ppermute x2, starting transfers between devices, exchange(): from_other = lax.ppermute(to_other, both, others)  5.58 us
    ppermute x1, starting transfers between devices, body(): from_far = lax.ppermute(to_far, both, far_pairs)  5.1 us
    ppermute x1, starting transfers between devices, body(): lax.ppermute(to_other, both, others)  4.7 us
    ppermute x9, waiting for transfers between devices, swaps(): lax.ppermute(part, 'tile', [(t, t ^ m * step) for t in range(tiles)])  4.19 us
  transfers between devices with their start and end apart: 25, of which 9 were waited for; matrix products, arithmetic and copies ran while one was open for 1% of the time, Pallas kernels for 19%

profile of v8, /device:TPU:65, one launch (start us, length us, event | category | flops | bytes accessed | tf_op | source)
XLA Modules:
  0.0 72.0 jit_solution(7430926833753507703)
XLA Ops:
  0.0 1.7 %shard_map.91 = (bf16[64,32,128]{2,1,0:T(8,128)(2,1)S(1)}, f32[64,32,128]{2,1,0:T(8,128)S(1)}, bf16[8,32,128]{2,1,0:T(8,128)(2,1)S(1)}, bf16[8,32,128]{2,1,0:T(8,128)(2,1)S(1)}, bf16[1,32,128]{2,1,0:T(8,128)(2,1)S(1)}) custom-call(f32[32,64,128]{2,1,0:T(8,128)} %bitcast.6, f32[1,32,128]{2,1,0:T(8,128)} %stream.1), custom_call_target="tpu_custom_call" | custom-call | bytes 4194304 | tf_op jit(solution)/shard_map/pallas_call | solution.py:314
  1.7 0.8 %collective-permute-start.6 = (bf16[8,32,128]{2,1,0:T(8,128)(2,1)S(1)}, bf16[8,32,128]{2,1,0:T(8,128)(2,1)S(1)}, u32[]{:S(2)}, u32[]{:S(2)}) collective-permute-start(bf16[8,32,128]{2,1,0:T(8,128)(2,1)S(1)} %get-tuple-element.38), channel_id=1, source_target_pairs={{0,1},{1,0},{2,3},{3,2},{4,5},{5,4},{6,7},{7,6},{8,9},{9,8},{10,11... | collective-permute-start | bytes 196616 | tf_op jit(solution)/shard_map/ppermute | solution.py:380
  2.5 5.1 %collective-permute-start.7 = (bf16[8,32,128]{2,1,0:T(8,128)(2,1)S(1)}, bf16[8,32,128]{2,1,0:T(8,128)(2,1)S(1)}, u32[]{:S(2)}, u32[]{:S(2)}) collective-permute-start(bf16[8,32,128]{2,1,0:T(8,128)(2,1)S(1)} %get-tuple-element.39), channel_id=1, source_target_pairs={{0,4},{1,2},{2,1},{3,7},{4,0},{5,6},{6,5},{7,3},{8,12},{9,10},{10,... | collective-permute-start | bytes 196616 | tf_op jit(solution)/shard_map/ppermute | solution.py:379
  7.6 0.7 %collective-permute-start.2 = (bf16[1,32,128]{2,1,0:T(8,128)(2,1)S(1)}, bf16[1,32,128]{2,1,0:T(8,128)(2,1)S(1)}, u32[]{:S(2)}, u32[]{:S(2)}) collective-permute-start(bf16[1,32,128]{2,1,0:T(8,128)(2,1)S(1)} %get-tuple-element.36.part0), channel_id=1, source_target_pairs={{0,192},{4,196},{8,200},{12,204},{16,208},{20,212},{24,216},{28,22... | collective-permute-start | bytes 24584 | tf_op jit(solution)/shard_map/ppermute | solution.py:368
  8.3 2.1 %collective-permute-start.1 = (bf16[1,32,128]{2,1,0:T(8,128)(2,1)S(1)}, bf16[1,32,128]{2,1,0:T(8,128)(2,1)S(1)}, u32[]{:S(2)}, u32[]{:S(2)}) collective-permute-start(bf16[1,32,128]{2,1,0:T(8,128)(2,1)S(1)} %get-tuple-element.36.part0), channel_id=1, source_target_pairs={{0,128},{4,132},{8,136},{12,140},{16,144},{20,148},{24,152},{28,15... | collective-permute-start | bytes 24584 | tf_op jit(solution)/shard_map/ppermute | solution.py:368
  10.4 0.0 collective-permute-start
  10.4 0.0 collective-permute-done.2.part3
  10.4 1.3 %collective-permute-done.1.part2 = bf16[1,32,128]{2,1,0:T(8,128)(2,1)S(1)} collective-permute-done((bf16[1,32,128]{2,1,0:T(8,128)(2,1)S(1)}, bf16[1,32,128]{2,1,0:T(8,128)(2,1)S(1)}, u32[]{:S(2)}, u32[]{:S(2)}) %collective-permute-start.1) | collective-permute-done | bytes 8224 | tf_op jit(solution)/shard_map/ppermute | solution.py:368
  11.7 1.2 %collective-permute-done.part1 = bf16[1,32,128]{2,1,0:T(8,128)(2,1)S(1)} collective-permute-done((bf16[1,32,128]{2,1,0:T(8,128)(2,1)S(1)}, bf16[1,32,128]{2,1,0:T(8,128)(2,1)S(1)}, u32[]{:S(2)}, u32[]{:S(2)}) %collective-permute-start) | collective-permute-done | bytes 8224 | tf_op jit(solution)/shard_map/ppermute | solution.py:368
  12.9 0.0 collective-permute-done.6.from_near.near
  12.9 0.0 collective-permute-done.7.from_far.far
  13.0 1.3 %collective-permute-start.8 = (bf16[10,32,128]{2,1,0:T(8,128)(2,1)S(1)}, bf16[10,32,128]{2,1,0:T(8,128)(2,1)S(1)}, u32[]{:S(2)}, u32[]{:S(2)}) collective-permute-start(bf16[10,32,128]{2,1,0:T(8,128)(2,1)S(1)} %get-tuple-element.40), channel_id=1, source_target_pairs={{0,4},{1,5},{2,6},{3,7},{4,0},{5,1},{6,2},{7,3},{8,12},{9,13},{10,... | collective-permute-start | bytes 245768 | tf_op jit(solution)/shard_map/ppermute | solution.py:383
  14.3 4.7 %collective-permute-start.9 = (bf16[10,32,128]{2,1,0:T(8,128)(2,1)S(1)}, bf16[10,32,128]{2,1,0:T(8,128)(2,1)S(1)}, u32[]{:S(2)}, u32[]{:S(2)}) collective-permute-start(bf16[10,32,128]{2,1,0:T(8,128)(2,1)S(1)} %get-tuple-element.41), channel_id=1, source_target_pairs={{0,1},{1,0},{2,3},{3,2},{4,8},{5,9},{6,10},{7,11},{8,4},{9,5},{10,... | collective-permute-start | bytes 245768 | tf_op jit(solution)/shard_map/ppermute | solution.py:383
  19.0 0.0 collective-permute-start.5
  19.0 0.1 collective-permute-start.4
  19.1 3.2 %collective-permute-start.3 = (bf16[4,32,128]{2,1,0:T(8,128)(2,1)S(1)}, bf16[4,32,128]{2,1,0:T(8,128)(2,1)S(1)}, u32[]{:S(2)}, u32[]{:S(2)}) collective-permute-start(bf16[4,32,128]{2,1,0:T(8,128)(2,1)S(1)} %shard_map.92.after.part0), channel_id=1, source_target_pairs={{0,16},{4,20},{8,24},{12,28},{16,0},{20,4},{24,8},{28,12},{32,48},... | collective-permute-start | bytes 98312 | tf_op jit(solution)/shard_map/ppermute | solution.py:368
  22.2 0.7 %collective-permute-done.5.part3 = bf16[4,32,128]{2,1,0:T(8,128)(2,1)S(1)} collective-permute-done((bf16[4,32,128]{2,1,0:T(8,128)(2,1)S(1)}, bf16[4,32,128]{2,1,0:T(8,128)(2,1)S(1)}, u32[]{:S(2)}, u32[]{:S(2)}) %collective-permute-start.5) | collective-permute-done | bytes 32800 | tf_op jit(solution)/shard_map/ppermute | solution.py:368
  23.0 0.8 %collective-permute-done.4.part2 = bf16[4,32,128]{2,1,0:T(8,128)(2,1)S(1)} collective-permute-done((bf16[4,32,128]{2,1,0:T(8,128)(2,1)S(1)}, bf16[4,32,128]{2,1,0:T(8,128)(2,1)S(1)}, u32[]{:S(2)}, u32[]{:S(2)}) %collective-permute-start.4) | collective-permute-done | bytes 32800 | tf_op jit(solution)/shard_map/ppermute | solution.py:368
  23.8 0.1 collective-permute-done.3.part1
  23.9 0.0 collective-permute-done.8.after_and_whole_0_.mate
  23.9 0.0 collective-permute-done.9.after_and_whole_1_.other
  24.0 0.1 collective-permute-start.12
  24.1 1.4 %collective-permute-start.11 = (bf16[16,32,128]{2,1,0:T(8,128)(2,1)S(1)}, bf16[16,32,128]{2,1,0:T(8,128)(2,1)S(1)}, u32[]{:S(2)}, u32[]{:S(2)}) collective-permute-start(bf16[16,32,128]{2,1,0:T(8,128)(2,1)S(1)} %shard_map.94.after.rows0), channel_id=1, source_target_pairs={{0,8},{4,12},{8,0},{12,4},{16,24},{20,28},{24,16},{28,20},{32,40},... | collective-permute-start | bytes 393224 | tf_op jit(solution)/shard_map/ppermute | solution.py:368
  25.5 1.8 %collective-permute-start.10 = (bf16[16,32,128]{2,1,0:T(8,128)(2,1)S(1)}, bf16[16,32,128]{2,1,0:T(8,128)(2,1)S(1)}, u32[]{:S(2)}, u32[]{:S(2)}) collective-permute-start(bf16[16,32,128]{2,1,0:T(8,128)(2,1)S(1)} %shard_map.94.after.rows0), channel_id=1, source_target_pairs={{0,4},{4,0},{8,12},{12,8},{16,20},{20,16},{24,28},{28,24},{32,36},... | collective-permute-start | bytes 393224 | tf_op jit(solution)/shard_map/ppermute | solution.py:368
  27.3 0.8 %copy.11 = s32[8,8,3]{2,1,0:T(8,128)S(1)} copy(s32[8,8,3]{1,0,2:T(8,128)} %param.12) | data formatting | bytes 1536 | tf_op args[3]
  28.1 0.1 reshape.15.neighbour_in
  28.3 4.0 %shard_map.95 = (bf16[64,3,128,128]{3,2,1,0:T(8,128)(2,1)S(1)}, bf16[64,128,128]{2,1,0:T(8,128)(2,1)S(1)}, s32[192]{0:T(256)S(4)}) custom-call(s32[192]{0:T(256)S(1)} %reshape.15.neighbour_in, bf16[16,32,128]{2,1,0:T(8,128)(2,1)S(1)} %shard_map.94.after.rows0, bf16[64,3,128,128]{3,2,1,0:T(8,128)(2,1)} %bitcast.4, bf16[64,128,128]{2,1,0:T(8,128)(2,1)} %bitcast.5), custom_call_target="tpu_custom_call" | custom-call | bytes 8388608 | tf_op jit(solution)/shard_map/pallas_call | solution.py:314
  32.2 2.9 %shard_map.96 = (bf16[64,32,128]{2,1,0:T(8,128)(2,1)S(1)}, bf16[100,32,128]{2,1,0:T(8,128)(2,1)S(1)}) custom-call(s32[192]{0:T(256)S(4)} %get-tuple-element.42.neighbour, bf16[64,32,128]{2,1,0:T(8,128)(2,1)S(1)} %get-tuple-element.37.x, bf16[8,32,128]{2,1,0:T(8,128)(2,1)S(1)} %collective-permute-done.6.from_near.near, ...), custom_call_target="tpu_custom_call" | custom-call | flops 268435456 | bytes 9437184 | tf_op jit(solution)/shard_map/pallas_call | solution.py:314
  35.1 0.0 collective-permute-done.12.rows3
  35.1 0.0 collective-permute-done.11.rows2
  35.1 0.0 collective-permute-done.10.rows1
  35.2 1.1 %shard_map.97 = (bf16[64,32,128]{2,1,0:T(8,128)(2,1)S(1)}, f32[64,32,128]{2,1,0:T(8,128)S(1)}, bf16[8,32,128]{2,1,0:T(8,128)(2,1)S(1)}, bf16[8,32,128]{2,1,0:T(8...) custom-call(s32[192]{0:T(256)S(4)} %get-tuple-element.42.neighbour, s32[1,1,4]{2,1,0:T(1,128)} %well.1, ...), custom_call_target="tpu_custom_call" | custom-call | tf_op jit(solution)/shard_map/pallas_call | solution.py:314
  36.3 1.4 %collective-permute-start.13 = (bf16[8,32,128]{2,1,0:T(8,128)(2,1)S(1)}, bf16[8,32,128]{2,1,0:T(8,128)(2,1)S(1)}, u32[]{:S(2)}, u32[]{:S(2)}) collective-permute-start(bf16[8,32,128]{2,1,0:T(8,128)(2,1)S(1)} %get-tuple-element.49), channel_id=1, source_target_pairs={{0,1},{1,0},{2,3},{3,2},{4,5},{5,4},{6,7},{7,6},{8,9},{9,8},{10,11... | collective-permute-start | bytes 196616 | tf_op jit(solution)/shard_map/ppermute | solution.py:350
  37.7 4.2 %collective-permute-start.14 = (bf16[8,32,128]{2,1,0:T(8,128)(2,1)S(1)}, bf16[8,32,128]{2,1,0:T(8,128)(2,1)S(1)}, u32[]{:S(2)}, u32[]{:S(2)}) collective-permute-start(bf16[8,32,128]{2,1,0:T(8,128)(2,1)S(1)} %get-tuple-element.50), channel_id=1, source_target_pairs={{0,4},{1,2},{2,1},{3,7},{4,0},{5,6},{6,5},{7,3},{8,12},{9,10},{10,... | collective-permute-start | bytes 196616 | tf_op jit(solution)/shard_map/ppermute | solution.py:349
  41.8 0.1 collective-permute-start.15
  42.0 3.1 %collective-permute-start.16 = (bf16[8,32,128]{2,1,0:T(8,128)(2,1)S(1)}, bf16[8,32,128]{2,1,0:T(8,128)(2,1)S(1)}, u32[]{:S(2)}, u32[]{:S(2)}) collective-permute-start(bf16[8,32,128]{2,1,0:T(8,128)(2,1)S(1)} %get-tuple-element.52), channel_id=1, source_target_pairs={{0,1},{1,0},{2,3},{3,2},{4,8},{5,9},{6,10},{7,11},{8,4},{9,5},{10,... | collective-permute-start | bytes 196616 | tf_op jit(solution)/shard_map/ppermute | solution.py:352
  45.1 0.0 collective-permute-done.13.refs_0_.from_near
  45.1 0.2 collective-permute-done.14.refs_1_.from_far
  45.3 0.1 collective-permute-start.17
  45.4 3.5 %collective-permute-start.18 = (bf16[2,32,128]{2,1,0:T(8,128)(2,1)S(1)}, bf16[2,32,128]{2,1,0:T(8,128)(2,1)S(1)}, u32[]{:S(2)}, u32[]{:S(2)}) collective-permute-start(bf16[2,32,128]{2,1,0:T(8,128)(2,1)S(1)} %get-tuple-element.57), channel_id=1, source_target_pairs={{0,1},{1,0},{2,3},{3,2},{4,8},{5,9},{6,10},{7,11},{8,4},{9,5},{10,... | collective-permute-start | bytes 49160 | tf_op jit(solution)/shard_map/ppermute | solution.py:357
  48.9 0.0 collective-permute-done.15.refs_2_
  48.9 0.4 collective-permute-done.16.refs_3_
  49.3 2.7 %shard_map.98 = (bf16[64,32,128]{2,1,0:T(8,128)(2,1)S(1)}, bf16[100,32,128]{2,1,0:T(8,128)(2,1)S(1)}) custom-call(s32[192]{0:T(256)S(4)} %get-tuple-element.42.neighbour, bf16[64,32,128]{2,1,0:T(8,128)(2,1)S(1)} %get-tuple-element.48.x, bf16[8,32,128]{2,1,0:T(8,128)(2,1)S(1)} %collective-permute-done.13.refs_0_.from_near, ...), custom_call_target="tpu_custom_call" | custom-call | flops 268435456 | bytes 9437184 | tf_op jit(solution)/shard_map/pallas_call | solution.py:314
  52.0 0.0 collective-permute-done.17.mate
  52.0 0.3 collective-permute-done.18.other
  52.3 0.4 shard_map.100
  52.6 0.1 collective-permute-start.19
  52.7 6.3 %collective-permute-start.20 = (bf16[8,32,128]{2,1,0:T(8,128)(2,1)S(1)}, bf16[8,32,128]{2,1,0:T(8,128)(2,1)S(1)}, u32[]{:S(2)}, u32[]{:S(2)}) collective-permute-start(bf16[8,32,128]{2,1,0:T(8,128)(2,1)S(1)} %get-tuple-element.60), channel_id=1, source_target_pairs={{0,4},{1,2},{2,1},{3,7},{4,0},{5,6},{6,5},{7,3},{8,12},{9,10},{10,... | collective-permute-start | bytes 196616 | tf_op jit(solution)/shard_map/ppermute | solution.py:349
  59.1 0.0 collective-permute-start.21
  59.1 2.5 %collective-permute-start.22 = (bf16[8,32,128]{2,1,0:T(8,128)(2,1)S(1)}, bf16[8,32,128]{2,1,0:T(8,128)(2,1)S(1)}, u32[]{:S(2)}, u32[]{:S(2)}) collective-permute-start(bf16[8,32,128]{2,1,0:T(8,128)(2,1)S(1)} %get-tuple-element.62), channel_id=1, source_target_pairs={{0,1},{1,0},{2,3},{3,2},{4,8},{5,9},{6,10},{7,11},{8,4},{9,5},{10,... | collective-permute-start | bytes 196616 | tf_op jit(solution)/shard_map/ppermute | solution.py:352
  61.6 0.0 collective-permute-done.19.near.from_near
  61.6 0.0 collective-permute-done.20.far.from_far
  61.6 0.1 collective-permute-start.23
  61.7 3.3 %collective-permute-start.24 = (bf16[2,32,128]{2,1,0:T(8,128)(2,1)S(1)}, bf16[2,32,128]{2,1,0:T(8,128)(2,1)S(1)}, u32[]{:S(2)}, u32[]{:S(2)}) collective-permute-start(bf16[2,32,128]{2,1,0:T(8,128)(2,1)S(1)} %get-tuple-element.66), channel_id=1, source_target_pairs={{0,1},{1,0},{2,3},{3,2},{4,8},{5,9},{6,10},{7,11},{8,4},{9,5},{10,... | collective-permute-start | bytes 49160 | tf_op jit(solution)/shard_map/ppermute | solution.py:357
  65.0 0.0 collective-permute-done.21.mate
  65.0 1.9 %collective-permute-done.22.other = bf16[8,32,128]{2,1,0:T(8,128)(2,1)S(1)} collective-permute-done((bf16[8,32,128]{2,1,0:T(8,128)(2,1)S(1)}, bf16[8,32,128]{2,1,0:T(8,128)(2,1)S(1)}, u32[]{:S(2)}, u32[]{:S(2)}) %collective-permute-start.22) | collective-permute-done | bytes 65568 | tf_op jit(solution)/shard_map/ppermute | solution.py:352
  66.8 3.9 %shard_map.101 = (f32[32,64,128]{2,1,0:T(8,128)}, bf16[100,32,128]{2,1,0:T(8,128)(2,1)S(1)}) custom-call(s32[192]{0:T(256)S(4)} %get-tuple-element.42.neighbour, bf16[64,32,128]{2,1,0:T(8,128)(2,1)S(1)} %get-tuple-element.54.edges.x, bf16[4,32,128]{2,1,0:T(8,128)(2,1)S(1)} %get-tuple-element.58.corners, ...), custom_call_target="tpu_custom_call" | custom-call | flops 268435456 | bytes 9437184 | tf_op jit(solution)/shard_map/pallas_call | solution.py:314
  70.8 0.0 collective-permute-done.23.mate
  70.8 0.0 collective-permute-done.24.other
  70.8 1.0 %shard_map.103 = f32[32,64,128]{2,1,0:T(8,128)} custom-call(s32[192]{0:T(256)S(4)} %get-tuple-element.42.neighbour, f32[32,64,128]{2,1,0:T(8,128)} %get-tuple-element.63.partial, bf16[100,32,128]{2,1,0:T(8,128)(2,1)S(1)} %get-tuple-element.64.grid, bf16[2,32,128]{2,1,0:T(8,128)(2,1)S(1)} %collective-permute-done.23.mate, ...), custom_call_target="tpu_custom_call", output_to_operand_aliasing={{}: (1, {})} | custom-call | tf_op jit(solution)/shard_map/pallas_call | solution.py:314
  (5 shorter events, 0.1 us)
Async XLA Ops:
  1.7 11.2 %collective-permute-start.6 = (bf16[8,32,128]{2,1,0:T(8,128)(2,1)S(1)}, bf16[8,32,128]{2,1,0:T(8,128)(2,1)S(1)}, u32[]{:S(2)}, u32[]{:S(2)}) collective-permute-start(bf16[8,32,128]{2,1,0:T(8,128)(2,1)S(1)} %get-tuple-element.38), channel_id=1, source_target_pairs={{0,1},{1,0},{2,3},{3,2},{4,5},{5,4},{6,7},{7,6},{8,9},{9,8},{10,11... | collective-permute-start | bytes 196616 | tf_op jit(solution)/shard_map/ppermute | solution.py:380
  2.5 10.4 %collective-permute-start.7 = (bf16[8,32,128]{2,1,0:T(8,128)(2,1)S(1)}, bf16[8,32,128]{2,1,0:T(8,128)(2,1)S(1)}, u32[]{:S(2)}, u32[]{:S(2)}) collective-permute-start(bf16[8,32,128]{2,1,0:T(8,128)(2,1)S(1)} %get-tuple-element.39), channel_id=1, source_target_pairs={{0,4},{1,2},{2,1},{3,7},{4,0},{5,6},{6,5},{7,3},{8,12},{9,10},{10,... | collective-permute-start | bytes 196616 | tf_op jit(solution)/shard_map/ppermute | solution.py:379
  7.6 2.8 %collective-permute-start.2 = (bf16[1,32,128]{2,1,0:T(8,128)(2,1)S(1)}, bf16[1,32,128]{2,1,0:T(8,128)(2,1)S(1)}, u32[]{:S(2)}, u32[]{:S(2)}) collective-permute-start(bf16[1,32,128]{2,1,0:T(8,128)(2,1)S(1)} %get-tuple-element.36.part0), channel_id=1, source_target_pairs={{0,192},{4,196},{8,200},{12,204},{16,208},{20,212},{24,216},{28,22... | collective-permute-start | bytes 24584 | tf_op jit(solution)/shard_map/ppermute | solution.py:368
  8.3 3.4 %collective-permute-start.1 = (bf16[1,32,128]{2,1,0:T(8,128)(2,1)S(1)}, bf16[1,32,128]{2,1,0:T(8,128)(2,1)S(1)}, u32[]{:S(2)}, u32[]{:S(2)}) collective-permute-start(bf16[1,32,128]{2,1,0:T(8,128)(2,1)S(1)} %get-tuple-element.36.part0), channel_id=1, source_target_pairs={{0,128},{4,132},{8,136},{12,140},{16,144},{20,148},{24,152},{28,15... | collective-permute-start | bytes 24584 | tf_op jit(solution)/shard_map/ppermute | solution.py:368
  10.4 2.5 %collective-permute-start = (bf16[1,32,128]{2,1,0:T(8,128)(2,1)S(1)}, bf16[1,32,128]{2,1,0:T(8,128)(2,1)S(1)}, u32[]{:S(2)}, u32[]{:S(2)}) collective-permute-start(bf16[1,32,128]{2,1,0:T(8,128)(2,1)S(1)} %get-tuple-element.36.part0), channel_id=1, source_target_pairs={{0,64},{4,68},{8,72},{12,76},{16,80},{20,84},{24,88},{28,92},{32,9... | collective-permute-start | bytes 24584 | tf_op jit(solution)/shard_map/ppermute | solution.py:368
  13.0 10.9 %collective-permute-start.8 = (bf16[10,32,128]{2,1,0:T(8,128)(2,1)S(1)}, bf16[10,32,128]{2,1,0:T(8,128)(2,1)S(1)}, u32[]{:S(2)}, u32[]{:S(2)}) collective-permute-start(bf16[10,32,128]{2,1,0:T(8,128)(2,1)S(1)} %get-tuple-element.40), channel_id=1, source_target_pairs={{0,4},{1,5},{2,6},{3,7},{4,0},{5,1},{6,2},{7,3},{8,12},{9,13},{10,... | collective-permute-start | bytes 245768 | tf_op jit(solution)/shard_map/ppermute | solution.py:383
  14.3 9.7 %collective-permute-start.9 = (bf16[10,32,128]{2,1,0:T(8,128)(2,1)S(1)}, bf16[10,32,128]{2,1,0:T(8,128)(2,1)S(1)}, u32[]{:S(2)}, u32[]{:S(2)}) collective-permute-start(bf16[10,32,128]{2,1,0:T(8,128)(2,1)S(1)} %get-tuple-element.41), channel_id=1, source_target_pairs={{0,1},{1,0},{2,3},{3,2},{4,8},{5,9},{6,10},{7,11},{8,4},{9,5},{10,... | collective-permute-start | bytes 245768 | tf_op jit(solution)/shard_map/ppermute | solution.py:383
  19.0 4.0 %collective-permute-start.5 = (bf16[4,32,128]{2,1,0:T(8,128)(2,1)S(1)}, bf16[4,32,128]{2,1,0:T(8,128)(2,1)S(1)}, u32[]{:S(2)}, u32[]{:S(2)}) collective-permute-start(bf16[4,32,128]{2,1,0:T(8,128)(2,1)S(1)} %shard_map.92.after.part0), channel_id=1, source_target_pairs={{0,48},{4,52},{8,56},{12,60},{16,32},{20,36},{24,40},{28,44},{32,1... | collective-permute-start | bytes 98312 | tf_op jit(solution)/shard_map/ppermute | solution.py:368
  19.0 4.8 %collective-permute-start.4 = (bf16[4,32,128]{2,1,0:T(8,128)(2,1)S(1)}, bf16[4,32,128]{2,1,0:T(8,128)(2,1)S(1)}, u32[]{:S(2)}, u32[]{:S(2)}) collective-permute-start(bf16[4,32,128]{2,1,0:T(8,128)(2,1)S(1)} %shard_map.92.after.part0), channel_id=1, source_target_pairs={{0,32},{4,36},{8,40},{12,44},{16,48},{20,52},{24,56},{28,60},{32,0... | collective-permute-start | bytes 98312 | tf_op jit(solution)/shard_map/ppermute | solution.py:368
  19.1 4.9 %collective-permute-start.3 = (bf16[4,32,128]{2,1,0:T(8,128)(2,1)S(1)}, bf16[4,32,128]{2,1,0:T(8,128)(2,1)S(1)}, u32[]{:S(2)}, u32[]{:S(2)}) collective-permute-start(bf16[4,32,128]{2,1,0:T(8,128)(2,1)S(1)} %shard_map.92.after.part0), channel_id=1, source_target_pairs={{0,16},{4,20},{8,24},{12,28},{16,0},{20,4},{24,8},{28,12},{32,48},... | collective-permute-start | bytes 98312 | tf_op jit(solution)/shard_map/ppermute | solution.py:368
  24.0 11.2 %collective-permute-start.12 = (bf16[16,32,128]{2,1,0:T(8,128)(2,1)S(1)}, bf16[16,32,128]{2,1,0:T(8,128)(2,1)S(1)}, u32[]{:S(2)}, u32[]{:S(2)}) collective-permute-start(bf16[16,32,128]{2,1,0:T(8,128)(2,1)S(1)} %shard_map.94.after.rows0), channel_id=1, source_target_pairs={{0,12},{4,8},{8,4},{12,0},{16,28},{20,24},{24,20},{28,16},{32,44},... | collective-permute-start | bytes 393224 | tf_op jit(solution)/shard_map/ppermute | solution.py:368
  24.1 11.1 %collective-permute-start.11 = (bf16[16,32,128]{2,1,0:T(8,128)(2,1)S(1)}, bf16[16,32,128]{2,1,0:T(8,128)(2,1)S(1)}, u32[]{:S(2)}, u32[]{:S(2)}) collective-permute-start(bf16[16,32,128]{2,1,0:T(8,128)(2,1)S(1)} %shard_map.94.after.rows0), channel_id=1, source_target_pairs={{0,8},{4,12},{8,0},{12,4},{16,24},{20,28},{24,16},{28,20},{32,40},... | collective-permute-start | bytes 393224 | tf_op jit(solution)/shard_map/ppermute | solution.py:368
  25.5 9.7 %collective-permute-start.10 = (bf16[16,32,128]{2,1,0:T(8,128)(2,1)S(1)}, bf16[16,32,128]{2,1,0:T(8,128)(2,1)S(1)}, u32[]{:S(2)}, u32[]{:S(2)}) collective-permute-start(bf16[16,32,128]{2,1,0:T(8,128)(2,1)S(1)} %shard_map.94.after.rows0), channel_id=1, source_target_pairs={{0,4},{4,0},{8,12},{12,8},{16,20},{20,16},{24,28},{28,24},{32,36},... | collective-permute-start | bytes 393224 | tf_op jit(solution)/shard_map/ppermute | solution.py:368
  36.3 8.8 %collective-permute-start.13 = (bf16[8,32,128]{2,1,0:T(8,128)(2,1)S(1)}, bf16[8,32,128]{2,1,0:T(8,128)(2,1)S(1)}, u32[]{:S(2)}, u32[]{:S(2)}) collective-permute-start(bf16[8,32,128]{2,1,0:T(8,128)(2,1)S(1)} %get-tuple-element.49), channel_id=1, source_target_pairs={{0,1},{1,0},{2,3},{3,2},{4,5},{5,4},{6,7},{7,6},{8,9},{9,8},{10,11... | collective-permute-start | bytes 196616 | tf_op jit(solution)/shard_map/ppermute | solution.py:350
  37.7 7.6 %collective-permute-start.14 = (bf16[8,32,128]{2,1,0:T(8,128)(2,1)S(1)}, bf16[8,32,128]{2,1,0:T(8,128)(2,1)S(1)}, u32[]{:S(2)}, u32[]{:S(2)}) collective-permute-start(bf16[8,32,128]{2,1,0:T(8,128)(2,1)S(1)} %get-tuple-element.50), channel_id=1, source_target_pairs={{0,4},{1,2},{2,1},{3,7},{4,0},{5,6},{6,5},{7,3},{8,12},{9,10},{10,... | collective-permute-start | bytes 196616 | tf_op jit(solution)/shard_map/ppermute | solution.py:349
  41.8 7.1 %collective-permute-start.15 = (bf16[8,32,128]{2,1,0:T(8,128)(2,1)S(1)}, bf16[8,32,128]{2,1,0:T(8,128)(2,1)S(1)}, u32[]{:S(2)}, u32[]{:S(2)}) collective-permute-start(bf16[8,32,128]{2,1,0:T(8,128)(2,1)S(1)} %get-tuple-element.51), channel_id=1, source_target_pairs={{0,4},{1,5},{2,6},{3,7},{4,0},{5,1},{6,2},{7,3},{8,12},{9,13},{10,... | collective-permute-start | bytes 196616 | tf_op jit(solution)/shard_map/ppermute | solution.py:351
  42.0 7.3 %collective-permute-start.16 = (bf16[8,32,128]{2,1,0:T(8,128)(2,1)S(1)}, bf16[8,32,128]{2,1,0:T(8,128)(2,1)S(1)}, u32[]{:S(2)}, u32[]{:S(2)}) collective-permute-start(bf16[8,32,128]{2,1,0:T(8,128)(2,1)S(1)} %get-tuple-element.52), channel_id=1, source_target_pairs={{0,1},{1,0},{2,3},{3,2},{4,8},{5,9},{6,10},{7,11},{8,4},{9,5},{10,... | collective-permute-start | bytes 196616 | tf_op jit(solution)/shard_map/ppermute | solution.py:352
  45.3 6.7 %collective-permute-start.17 = (bf16[2,32,128]{2,1,0:T(8,128)(2,1)S(1)}, bf16[2,32,128]{2,1,0:T(8,128)(2,1)S(1)}, u32[]{:S(2)}, u32[]{:S(2)}) collective-permute-start(bf16[2,32,128]{2,1,0:T(8,128)(2,1)S(1)} %get-tuple-element.56), channel_id=1, source_target_pairs={{0,4},{1,5},{2,6},{3,7},{4,0},{5,1},{6,2},{7,3},{8,12},{9,13},{10,... | collective-permute-start | bytes 49160 | tf_op jit(solution)/shard_map/ppermute | solution.py:357
  45.4 6.9 %collective-permute-start.18 = (bf16[2,32,128]{2,1,0:T(8,128)(2,1)S(1)}, bf16[2,32,128]{2,1,0:T(8,128)(2,1)S(1)}, u32[]{:S(2)}, u32[]{:S(2)}) collective-permute-start(bf16[2,32,128]{2,1,0:T(8,128)(2,1)S(1)} %get-tuple-element.57), channel_id=1, source_target_pairs={{0,1},{1,0},{2,3},{3,2},{4,8},{5,9},{6,10},{7,11},{8,4},{9,5},{10,... | collective-permute-start | bytes 49160 | tf_op jit(solution)/shard_map/ppermute | solution.py:357
  52.6 8.9 %collective-permute-start.19 = (bf16[8,32,128]{2,1,0:T(8,128)(2,1)S(1)}, bf16[8,32,128]{2,1,0:T(8,128)(2,1)S(1)}, u32[]{:S(2)}, u32[]{:S(2)}) collective-permute-start(bf16[8,32,128]{2,1,0:T(8,128)(2,1)S(1)} %get-tuple-element.59), channel_id=1, source_target_pairs={{0,1},{1,0},{2,3},{3,2},{4,5},{5,4},{6,7},{7,6},{8,9},{9,8},{10,11... | collective-permute-start | bytes 196616 | tf_op jit(solution)/shard_map/ppermute | solution.py:350
  52.7 8.8 %collective-permute-start.20 = (bf16[8,32,128]{2,1,0:T(8,128)(2,1)S(1)}, bf16[8,32,128]{2,1,0:T(8,128)(2,1)S(1)}, u32[]{:S(2)}, u32[]{:S(2)}) collective-permute-start(bf16[8,32,128]{2,1,0:T(8,128)(2,1)S(1)} %get-tuple-element.60), channel_id=1, source_target_pairs={{0,4},{1,2},{2,1},{3,7},{4,0},{5,6},{6,5},{7,3},{8,12},{9,10},{10,... | collective-permute-start | bytes 196616 | tf_op jit(solution)/shard_map/ppermute | solution.py:349
  59.1 5.9 %collective-permute-start.21 = (bf16[8,32,128]{2,1,0:T(8,128)(2,1)S(1)}, bf16[8,32,128]{2,1,0:T(8,128)(2,1)S(1)}, u32[]{:S(2)}, u32[]{:S(2)}) collective-permute-start(bf16[8,32,128]{2,1,0:T(8,128)(2,1)S(1)} %get-tuple-element.61), channel_id=1, source_target_pairs={{0,4},{1,5},{2,6},{3,7},{4,0},{5,1},{6,2},{7,3},{8,12},{9,13},{10,... | collective-permute-start | bytes 196616 | tf_op jit(solution)/shard_map/ppermute | solution.py:351
  59.1 7.8 %collective-permute-start.22 = (bf16[8,32,128]{2,1,0:T(8,128)(2,1)S(1)}, bf16[8,32,128]{2,1,0:T(8,128)(2,1)S(1)}, u32[]{:S(2)}, u32[]{:S(2)}) collective-permute-start(bf16[8,32,128]{2,1,0:T(8,128)(2,1)S(1)} %get-tuple-element.62), channel_id=1, source_target_pairs={{0,1},{1,0},{2,3},{3,2},{4,8},{5,9},{6,10},{7,11},{8,4},{9,5},{10,... | collective-permute-start | bytes 196616 | tf_op jit(solution)/shard_map/ppermute | solution.py:352
  61.6 9.2 %collective-permute-start.23 = (bf16[2,32,128]{2,1,0:T(8,128)(2,1)S(1)}, bf16[2,32,128]{2,1,0:T(8,128)(2,1)S(1)}, u32[]{:S(2)}, u32[]{:S(2)}) collective-permute-start(bf16[2,32,128]{2,1,0:T(8,128)(2,1)S(1)} %get-tuple-element.65), channel_id=1, source_target_pairs={{0,4},{1,5},{2,6},{3,7},{4,0},{5,1},{6,2},{7,3},{8,12},{9,13},{10,... | collective-permute-start | bytes 49160 | tf_op jit(solution)/shard_map/ppermute | solution.py:357
  61.7 9.1 %collective-permute-start.24 = (bf16[2,32,128]{2,1,0:T(8,128)(2,1)S(1)}, bf16[2,32,128]{2,1,0:T(8,128)(2,1)S(1)}, u32[]{:S(2)}, u32[]{:S(2)}) collective-permute-start(bf16[2,32,128]{2,1,0:T(8,128)(2,1)S(1)} %get-tuple-element.66), channel_id=1, source_target_pairs={{0,1},{1,0},{2,3},{3,2},{4,8},{5,9},{6,10},{7,11},{8,4},{9,5},{10,... | collective-permute-start | bytes 49160 | tf_op jit(solution)/shard_map/ppermute | solution.py:357
